TPU v7x, 32 devices: a whole 2x2x4 slice. The times are simulated.
32 devices in a mesh: gx: 4 (over z), gy: 2 (over x), gz: 4 (over y, core).
Axes of the slice: x: 2, y: 2, z: 4, core: 2. Of those that a mesh axis runs over, the one named last changes fastest.
Arguments:
- velocity: float32 [3, 64, 64, 256], P(None, 'gz', 'gx', 'gy'), may hold values from -20 to 20
- owner: int32 [32768, 1], P(('gx', 'gy', 'gz')), may hold values from 0 to 7; in each aligned block of 1024 rows (0 to 1023, 1024 to 2047, ...) at most 512 rows name the same one
- cell_x: int32 [32768], P(('gx', 'gy', 'gz')), may hold values from 0 to 14
- cell_y: int32 [32768], P(('gx', 'gy', 'gz')), may hold values from 0 to 126
- cell_z: int32 [32768], P(('gx', 'gy', 'gz')), may hold values from 0 to 14
- query_weights: float32 [3, 32768], P(None, ('gx', 'gy', 'gz')), may hold values from 0 to 1
Outputs:
- query_stress: float32 [6, 32768], P(None, ('gx', 'gy', 'gz'))
Inputs may be any that keep to these rules, and one draw needn't show every extreme that they name: Among the queries held by one device, at most 512 name the same owner, and in every draw some owner is named by exactly 512 of them. `cell_x`: the corner cell plus one stays in the same brick.
All inputs are finite; a program needn't handle non-finite values.
Results may differ from a plain program's by a relative error of at most 0.0003.
Values sent between devices are 32-bit elements; how exact they have to be, the bound alone decides.
No kernel may reach another device: no remote copies, remote signals or barrier semaphores. Data moves between devices by JAX's collectives and lax.ppermute only.
A program may use at most 64 MiB of HBM per device.

v0:
```python
import jax
import jax.numpy as jnp
from jax import lax
from jax.sharding import PartitionSpec as P

FW = 32


PAIRS = ((0, 0), (0, 1), (0, 2), (1, 1), (1, 2), (2, 2))


def padded(x, sides, width):
    for axis, dim in sides:
        devices, length = (lax.axis_size(axis), x.shape[dim])
        up = [(i, (i + 1) % devices) for i in range(devices)]
        down = [(j, i) for i, j in up]
        last = lax.slice_in_dim(x, length - width, length, axis=dim)
        initial = lax.slice_in_dim(x, 0, width, axis=dim)
        before = lax.ppermute(last, axis, up)
        after = lax.ppermute(initial, axis, down)
        x = jnp.concatenate([before, x, after], axis=dim)
    return x


def taps(radius, width):
    offsets = jnp.arange(2 * radius + 1).astype(jnp.float32) - radius
    values = jnp.exp(-6.0 * offsets * offsets / (width * width))
    return values / jnp.sum(values)


def band(length, radius, width):
    weights = taps(radius, width)
    rows = jnp.arange(length + 2 * radius)[:, None]
    cols = jnp.arange(length)[None, :]
    offset = rows - cols
    inside = (offset >= 0) & (offset <= 2 * radius)
    picked = weights[jnp.clip(offset, 0, 2 * radius)]
    return jnp.where(inside, picked, jnp.zeros_like(picked))


def filter_x(fields, matrix):
    return jnp.einsum("czpy,pq->czqy", fields, matrix, precision=lax.Precision.HIGHEST)


def filter_y(fields, matrix):
    return jnp.einsum("czxp,pq->czxq", fields, matrix, precision=lax.Precision.HIGHEST)


def interpolate(flat_stress, index, weight, size_x, size_y):
    shape = index.shape[1:]
    base = index[0].reshape(-1)
    offsets = weight.reshape(3, -1)
    wx = offsets[0]
    wy = offsets[1]
    wz = offsets[2]
    total = jnp.zeros((6, base.shape[0]), jnp.float32)
    for dz in (0, 1):
        for dx in (0, 1):
            for dy in (0, 1):
                corner = base + dz * size_x * size_y + dx * size_y + dy
                values = jnp.take(flat_stress, corner, axis=1)
                term = (
                    (wz if dz else 1.0 - wz) * (wx if dx else 1.0 - wx) * (wy if dy else 1.0 - wy)
                )
                total = total + term[None, :] * values
    return total.reshape((6,) + shape)


def on_device(velocity, owner, cell_x, cell_y, cell_z, query_weights):
    radius = FW // 2
    size_z = velocity.shape[1]
    size_x = velocity.shape[2]
    size_y = velocity.shape[3]
    layered = padded(velocity, (("gz", 1),), radius)
    band_z = band(size_z, radius, FW)
    band_x = band(size_x, radius, FW)
    band_y = band(size_y, radius, FW)
    fields = []
    for comp in range(3):
        fields.append(
            jnp.einsum("pxy,pz->zxy", layered[comp], band_z, precision=lax.Precision.HIGHEST)
        )
    for first, second in PAIRS:
        product = layered[first] * layered[second]
        fields.append(jnp.einsum("pxy,pz->zxy", product, band_z, precision=lax.Precision.HIGHEST))
    stacked = jnp.stack(fields)
    margin_x = padded(stacked, (("gx", 2),), radius)
    along_x = filter_x(margin_x, band_x)
    margin_y = padded(along_x, (("gy", 3),), radius)
    filtered = filter_y(margin_y, band_y)
    stress = jnp.stack(
        [
            filtered[3 + k] - filtered[first] * filtered[second]
            for k, (first, second) in enumerate(PAIRS)
        ]
    )
    flat_stress = stress.reshape(6, -1)
    bricks_x = lax.axis_size("gx")
    bricks_y = lax.axis_size("gy")
    owners = bricks_x * bricks_y
    count = owner.shape[0]
    capacity = 4 * count // owners
    target = owner[:, 0]
    order = jnp.argsort(target, stable=True)
    sorted_target = target[order]
    tally = jnp.sum(
        (target[:, None] == jnp.arange(owners, dtype=jnp.int32)[None, :]).astype(jnp.int32), axis=0
    )
    starts = jnp.cumsum(tally) - tally
    sorted_rank = jnp.arange(count, dtype=jnp.int32) - starts[sorted_target]
    rank = jnp.zeros((count,), jnp.int32).at[order].set(sorted_rank)
    slot = target * capacity + rank
    local_cell = (cell_z * size_x + cell_x) * size_y + cell_y
    send_index = jnp.zeros((owners * capacity,), jnp.int32).at[slot].set(local_cell)
    send_weight = jnp.zeros((3, owners * capacity), jnp.float32).at[:, slot].set(query_weights)
    values = interpolate(
        flat_stress,
        lax.all_to_all(
            send_index.reshape(1, owners, capacity),
            ("gx", "gy"),
            split_axis=1,
            concat_axis=1,
            tiled=True,
        ),
        lax.all_to_all(
            send_weight.reshape(3, owners, capacity),
            ("gx", "gy"),
            split_axis=1,
            concat_axis=1,
            tiled=True,
        ),
        size_x,
        size_y,
    )
    returned = lax.all_to_all(values, ("gx", "gy"), split_axis=1, concat_axis=1, tiled=True)
    flat_back = returned.reshape(6, owners * capacity)
    return jnp.take(flat_back, slot, axis=1)


def solution(mesh):
    placed = (
        P(None, "gz", "gx", "gy"),
        P(("gx", "gy", "gz"), None),
        P(("gx", "gy", "gz")),
        P(("gx", "gy", "gz")),
        P(("gx", "gy", "gz")),
        P(None, ("gx", "gy", "gz")),
    )
    return jax.shard_map(
        on_device,
        mesh=mesh,
        in_specs=placed,
        out_specs=P(None, ("gx", "gy", "gz")),
        check_vma=False,
    )
```

profile of v0, /device:TPU:0, one launch (start us, length us, event | category | flops | bytes accessed | tf_op | source)
XLA Modules:
  0.0 409.9 jit_solution(11611495036117247126)
XLA Ops:
  4.5 5.1 %sort.17 = (s32[1024]{0:T(1024)}, s32[1024]{0:T(1024)S(1)}) sort(s32[1024]{0:T(1024)} %bitcast.196, s32[1024]{0:T(1024)S(1)} %iota.50), dimensions={0}, to_apply=%region_0.0 | sort | flops 10240 | bytes 16384 | tf_op jit(solution)/shard_map/jit(argsort)/sort | solution.py:104
  10.5 4.5 %gather_fusion = s32[1024]{0:T(1024)S(1)} fusion(s32[1024]{0:T(1024)S(1)} %bitcast.197, s32[1024]{0:T(1024)S(1)} %get-tuple-element.45), kind=kCustom, calls=%fused_computation.8 | custom fusion | bytes 12288 | tf_op jit(solution)/shard_map/gather | solution.py:105
  15.1 4.3 %compare_select_fusion.11 = s32[1024,1]{0,1:T(1,128)S(1)} fusion(s32[]{:T(128)} %bitcast.5, s32[]{:T(128)} %bitcast.6, s32[]{:T(128)} %bitcast.7, s32[]{:T(128)} %bitcast.8, s32[]{:T(128)} %bitcast.9, s32[]{:T(128)} %bitcast.11, s32[]{:T(128)} %bitcast.10, s32[1024,1]{0,1:T(1,128)S(1)} %bitcast.213), kind=kLoop, calls=%fused_computation.127 | loop fusion | flops 15360 | bytes 8220 | tf_op jit(solution)/shard_map/gather | solution.py:110
  21.4 4.8 %gather_fusion.1 = f32[768]{0:T(1024)S(1)} fusion(f32[33]{0:T(128)S(1)} %broadcast_divide_fusion, s32[1024]{0:T(1024)S(1)} %get-tuple-element.55), kind=kCustom, calls=%fused_computation.9 | custom fusion | bytes 9216 | tf_op jit(solution)/shard_map/gather | solution.py:37
  26.3 4.3 %scatter_custom_fusion = s32[1024]{0:T(1024)S(1)} fusion(s32[1024]{0:T(1024)S(1)} %get-tuple-element.46, s32[1024]{0:T(1024)S(1)} %select_subtract_fusion, s32[]{:T(128)} %constant.31.clone.1), kind=kCustom, calls=%fused_computation.162 | custom fusion | bytes 4100 | tf_op jit(solution)/shard_map/scatter | solution.py:111
  38.5 4.9 %scatter_custom_fusion.2 = s32[4096]{0:T(1024)} fusion(s32[1024]{0:T(1024)S(1)} %get-tuple-element.9, s32[1024]{0:T(1024)S(1)} %multiply_add_fusion, s32[]{:T(128)} %constant.31.clone.1), kind=kCustom, calls=%fused_computation.150 | custom fusion | bytes 16388 | tf_op jit(solution)/shard_map/scatter | solution.py:114
  43.4 4.2 %all-to-all-start.1 = ((s32[1,8,512]{2,0,1:T(1,128)}), s32[1,8,512]{2,0,1:T(1,128)S(1)}, u32[]{:S(2)}, u32[]{:S(2)}) async-start(s32[1,8,512]{2,0,1:T(1,128)} %bitcast.18), calls=%async_computation.1 | async-start | bytes 32768 | tf_op jit(solution)/shard_map/all_to_all | solution.py:118
  47.6 121.4 %gather_fusion.2 = f32[20480]{0:T(1024)S(1)} fusion(f32[33]{0:T(128)S(1)} %broadcast_divide_fusion, s32[20480]{0:T(1024)S(1)} %fusion.36), kind=kCustom, calls=%fused_computation.10 | custom fusion | bytes 245760 | tf_op jit(solution)/shard_map/gather | solution.py:37
  170.0 4.0 scatter_custom_fusion.1
  175.3 6.0 %all-to-all-start = ((f32[3,8,512]{2,0,1:T(4,128)}), f32[3,8,512]{2,0,1:T(4,128)S(1)}, u32[]{:S(2)}, u32[]{:S(2)}) async-start(f32[3,8,512]{2,0,1:T(4,128)} %copy.97), calls=%async_computation | async-start | bytes 131072 | tf_op jit(solution)/shard_map/all_to_all | solution.py:125
  181.4 6.8 %all-to-all-done = f32[3,8,512]{2,0,1:T(4,128)S(1)} async-done(((f32[3,8,512]{2,0,1:T(4,128)}), f32[3,8,512]{2,0,1:T(4,128)S(1)}, u32[]{:S(2)}, u32[]{:S(2)}) %all-to-all-start) | async-done | bytes 49184 | tf_op jit(solution)/shard_map/all_to_all | solution.py:125
  195.4 26.9 %collective-permute-done.4 = f32[9,16,16,16]{3,2,1,0:T(8,128)S(1)} collective-permute-done((f32[9,16,16,16]{3,2,1,0:T(8,128)S(1)}, f32[9,16,16,16]{3,2,1,0:T(8,128)S(1)}, u32[]{:S(2)}, u32[]{:S(2)}) %collective-permute-start.4) | collective-permute-done | bytes 147488 | tf_op jit(solution)/shard_map/ppermute | solution.py:19
  222.3 21.6 %collective-permute-done.5 = f32[9,16,16,16]{3,2,1,0:T(8,128)S(1)} collective-permute-done((f32[9,16,16,16]{3,2,1,0:T(8,128)S(1)}, f32[9,16,16,16]{3,2,1,0:T(8,128)S(1)}, u32[]{:S(2)}, u32[]{:S(2)}) %collective-permute-start.5) | collective-permute-done | bytes 147488 | tf_op jit(solution)/shard_map/ppermute | solution.py:20
  247.6 9.0 %copy.112 = f32[6,32768]{0,1:T(8,128)} copy(f32[6,32768]{1,0:T(8,128)S(1)} %stack.67) | data formatting | bytes 1572864 | tf_op jit(solution)/shard_map/stack | solution.py:91
  256.6 16.5 %gather_fusion.4 = f32[4096,6]{1,0:T(8,128)S(1)} fusion(f32[6,32768]{0,1:T(8,128)} %copy.112, s32[4096]{0:T(1024)S(1)} %get-tuple-element.37), kind=kCustom, calls=%fused_computation.clone | custom fusion | bytes 212992 | tf_op jit(solution)/shard_map/jit(_take)/gather | solution.py:61
  273.8 16.5 %gather_fusion.5 = f32[4096,6]{1,0:T(8,128)S(1)} fusion(f32[6,32768]{0,1:T(8,128)} %copy.112, s32[4096]{0:T(1024)S(1)} %get-tuple-element.42), kind=kCustom, calls=%fused_computation.1.clone | custom fusion | bytes 212992 | tf_op jit(solution)/shard_map/jit(_take)/gather | solution.py:61
  290.9 16.5 %gather_fusion.6 = f32[4096,6]{1,0:T(8,128)S(1)} fusion(f32[6,32768]{0,1:T(8,128)} %copy.112, s32[4096]{0:T(1024)S(1)} %get-tuple-element.41), kind=kCustom, calls=%fused_computation.2.clone | custom fusion | bytes 212992 | tf_op jit(solution)/shard_map/jit(_take)/gather | solution.py:61
  308.1 16.5 %gather_fusion.7 = f32[4096,6]{1,0:T(8,128)S(1)} fusion(f32[6,32768]{0,1:T(8,128)} %copy.112, s32[4096]{0:T(1024)S(1)} %get-tuple-element.40), kind=kCustom, calls=%fused_computation.3.clone | custom fusion | bytes 212992 | tf_op jit(solution)/shard_map/jit(_take)/gather | solution.py:61
  325.2 16.5 %gather_fusion.8 = f32[4096,6]{1,0:T(8,128)S(1)} fusion(f32[6,32768]{0,1:T(8,128)} %copy.112, s32[4096]{0:T(1024)S(1)} %get-tuple-element.39), kind=kCustom, calls=%fused_computation.4.clone | custom fusion | bytes 212992 | tf_op jit(solution)/shard_map/jit(_take)/gather | solution.py:61
  342.4 16.5 %gather_fusion.9 = f32[4096,6]{1,0:T(8,128)S(1)} fusion(f32[6,32768]{0,1:T(8,128)} %copy.112, s32[4096]{0:T(1024)S(1)} %get-tuple-element.38), kind=kCustom, calls=%fused_computation.5.clone | custom fusion | bytes 212992 | tf_op jit(solution)/shard_map/jit(_take)/gather | solution.py:61
  359.6 16.5 %gather_fusion.10 = f32[4096,6]{1,0:T(8,128)S(1)} fusion(f32[6,32768]{0,1:T(8,128)} %copy.112, s32[4096]{0:T(1024)S(1)} %get-tuple-element.43), kind=kCustom, calls=%fused_computation.6.clone | custom fusion | bytes 212992 | tf_op jit(solution)/shard_map/jit(_take)/gather | solution.py:61
  376.7 16.5 %gather_fusion.11 = f32[4096,6]{1,0:T(8,128)S(1)} fusion(f32[6,32768]{0,1:T(8,128)} %copy.112, s32[4096]{0:T(1024)S(1)} %get-tuple-element.44), kind=kCustom, calls=%fused_computation.7.clone | custom fusion | bytes 212992 | tf_op jit(solution)/shard_map/jit(_take)/gather | solution.py:61
  394.7 3.4 all-to-all-start.2
  398.1 7.3 %all-to-all-done.2 = f32[6,8,512]{2,0,1:T(8,128)S(1)} async-done(((f32[6,8,512]{2,0,1:T(8,128)}), f32[6,8,512]{2,0,1:T(8,128)S(1)}, u32[]{:S(2)}, u32[]{:S(2)}) %all-to-all-start.2) | async-done | bytes 98336 | tf_op jit(solution)/shard_map/all_to_all | solution.py:135
  (78 shorter events, 38.8 us)
Async XLA Ops:
  0.0 10.5 %copy-start = (s32[1024,1]{0,1:T(1,128)S(1)}, s32[1024,1]{0,1:T(1,128)}, u32[]{:S(2)}) copy-start(s32[1024,1]{0,1:T(1,128)} %param.9) | copy-start | bytes 12292
  1.1 29.4 %collective-permute-start = (f32[3,16,16,128]{3,1,2,0:T(8,128)S(1)}, f32[3,16,16,128]{3,1,2,0:T(8,128)S(1)}, u32[]{:S(2)}, u32[]{:S(2)}) collective-permute-start(f32[3,16,16,128]{3,1,2,0:T(8,128)S(1)} %copy.98), channel_id=1, source_target_pairs={{0,1},{1,2},{2,3},{3,0},{4,5},{5,6},{6,7},{7,4},{8,9},{9,10},{10,1... | collective-permute-start | bytes 1179656 | tf_op jit(solution)/shard_map/ppermute | solution.py:19
  1.6 29.1 %collective-permute-start.1 = (f32[3,16,16,128]{3,1,2,0:T(8,128)S(1)}, f32[3,16,16,128]{3,1,2,0:T(8,128)S(1)}, u32[]{:S(2)}, u32[]{:S(2)}) collective-permute-start(f32[3,16,16,128]{3,1,2,0:T(8,128)S(1)} %copy.98), channel_id=1, source_target_pairs={{1,0},{2,1},{3,2},{0,3},{5,4},{6,5},{7,6},{4,7},{9,8},{10,9},{11,1... | collective-permute-start | bytes 1179656 | tf_op jit(solution)/shard_map/ppermute | solution.py:20
  10.5 10.2 %copy-start.3 = (s32[1024]{0:T(1024)S(1)}, s32[1024]{0:T(1024)}, u32[]{:S(2)}) copy-start(s32[1024]{0:T(1024)} %param.11) | copy-start | bytes 12292
  10.5 10.2 %copy-start.4 = (s32[1024]{0:T(1024)S(1)}, s32[1024]{0:T(1024)}, u32[]{:S(2)}) copy-start(s32[1024]{0:T(1024)} %param.10) | copy-start | bytes 12292
  10.5 10.2 %copy-start.5 = (s32[1024]{0:T(1024)S(1)}, s32[1024]{0:T(1024)}, u32[]{:S(2)}) copy-start(s32[1024]{0:T(1024)} %param.12) | copy-start | bytes 12292
  21.4 9.2 %copy-start.1 = (f32[3,16,16,128]{3,2,1,0:T(8,128)S(1)}, f32[3,16,16,128]{3,2,1,0:T(8,128)}, u32[]{:S(2)}) copy-start(f32[3,16,16,128]{3,2,1,0:T(8,128)} %param.8) | copy-start | bytes 1179652
  34.0 154.2 %collective-permute-start.2 = (f32[9,16,16,128]{3,1,2,0:T(8,128)S(1)}, f32[9,16,16,128]{3,1,2,0:T(8,128)}, u32[]{:S(2)}, u32[]{:S(2)}) collective-permute-start(f32[9,16,16,128]{3,1,2,0:T(8,128)S(1)} %fusion.11), channel_id=1, source_target_pairs={{0,8},{8,16},{16,24},{24,0},{1,9},{9,17},{17,25},{25,1},{2,10},{10... | collective-permute-start | bytes 3538952 | tf_op jit(solution)/shard_map/ppermute | solution.py:19
  36.4 151.8 %collective-permute-start.3 = (f32[9,16,16,128]{3,1,2,0:T(8,128)S(1)}, f32[9,16,16,128]{3,1,2,0:T(8,128)}, u32[]{:S(2)}, u32[]{:S(2)}) collective-permute-start(f32[9,16,16,128]{3,1,2,0:T(8,128)S(1)} %fusion.11), channel_id=1, source_target_pairs={{8,0},{16,8},{24,16},{0,24},{9,1},{17,9},{25,17},{1,25},{10,2},{18... | collective-permute-start | bytes 3538952 | tf_op jit(solution)/shard_map/ppermute | solution.py:20
  43.4 131.9 %all-to-all-start.1 = ((s32[1,8,512]{2,0,1:T(1,128)}), s32[1,8,512]{2,0,1:T(1,128)S(1)}, u32[]{:S(2)}, u32[]{:S(2)}) async-start(s32[1,8,512]{2,0,1:T(1,128)} %bitcast.18), calls=%async_computation.1 | async-start | bytes 32768 | tf_op jit(solution)/shard_map/all_to_all | solution.py:118
  47.6 121.4 %copy-start.2 = (f32[3,1024]{1,0:T(4,128)S(1)}, f32[3,1024]{1,0:T(4,128)}, u32[]{:S(2)}) copy-start(f32[3,1024]{1,0:T(4,128)} %param.13) | copy-start | bytes 36868
  175.3 12.9 %all-to-all-start = ((f32[3,8,512]{2,0,1:T(4,128)}), f32[3,8,512]{2,0,1:T(4,128)S(1)}, u32[]{:S(2)}, u32[]{:S(2)}) async-start(f32[3,8,512]{2,0,1:T(4,128)} %copy.97), calls=%async_computation | async-start | bytes 131072 | tf_op jit(solution)/shard_map/all_to_all | solution.py:125
  193.3 29.0 %collective-permute-start.4 = (f32[9,16,16,16]{3,2,1,0:T(8,128)S(1)}, f32[9,16,16,16]{3,2,1,0:T(8,128)S(1)}, u32[]{:S(2)}, u32[]{:S(2)}) collective-permute-start(f32[9,16,16,16]{3,2,1,0:T(8,128)S(1)} %get-tuple-element.16), channel_id=1, source_target_pairs={{0,4},{4,0},{1,5},{5,1},{2,6},{6,2},{3,7},{7,3},{8,12},{12,8},{9,1... | collective-permute-start | bytes 442376 | tf_op jit(solution)/shard_map/ppermute | solution.py:19
  193.7 50.1 %collective-permute-start.5 = (f32[9,16,16,16]{3,2,1,0:T(8,128)S(1)}, f32[9,16,16,16]{3,2,1,0:T(8,128)S(1)}, u32[]{:S(2)}, u32[]{:S(2)}) collective-permute-start(f32[9,16,16,16]{3,2,1,0:T(8,128)S(1)} %get-tuple-element.17), channel_id=1, source_target_pairs={{4,0},{0,4},{5,1},{1,5},{6,2},{2,6},{7,3},{3,7},{12,8},{8,12},{13,... | collective-permute-start | bytes 442376 | tf_op jit(solution)/shard_map/ppermute | solution.py:20
  394.7 10.7 %all-to-all-start.2 = ((f32[6,8,512]{2,0,1:T(8,128)}), f32[6,8,512]{2,0,1:T(8,128)S(1)}, u32[]{:S(2)}, u32[]{:S(2)}) async-start(f32[6,8,512]{2,0,1:T(8,128)} %bitcast.61), calls=%async_computation.2 | async-start | bytes 262144 | tf_op jit(solution)/shard_map/all_to_all | solution.py:135
where the time goes:
time: 411 us; the launch traced here: 410 us
  local copies, waits for them, and re-layouts  301 us (73%)
  waiting for transfers between devices  62.5 us (15%)
  starting transfers between devices  22.6 us (5%)
  other arithmetic  15.5 us (4%)
  matrix products  8.24 us (2%)
    gather x16, local copies, waits for them, and re-layouts, interpolate(): values = jnp.take(flat_stress, corner, axis=1)  137 us
    gather x3, local copies, waits for them, and re-layouts, band(): picked = weights[jnp.clip(offset, 0, 2 * radius)]  126 us
    ppermute x3, waiting for transfers between devices, padded(): before = lax.ppermute(last, axis, up)  26.9 us
    ppermute x3, waiting for transfers between devices, padded(): after = lax.ppermute(initial, axis, down)  21.6 us
    another operation x2, local copies, waits for them, and re-layouts, on_device(): jnp.stack([filtered[3 + k] - filtered[first] * filtered[second] for k, (f...  10.3 us
  transfers between devices with their start and end apart: 9, of which 4 were waited for; matrix products, arithmetic and copies ran while one was open for 39% of the time, Pallas kernels for 0%

commit v1 on v0

--- a/solution.py
+++ b/solution.py
@@ -106,7 +106,8 @@
     tally = jnp.sum(
         (target[:, None] == jnp.arange(owners, dtype=jnp.int32)[None, :]).astype(jnp.int32), axis=0
     )
-    starts = jnp.cumsum(tally) - tally
+    earlier = jnp.arange(owners)[None, :] < jnp.arange(owners)[:, None]
+    starts = jnp.sum(jnp.where(earlier, tally[None, :], 0), axis=1)
     sorted_rank = jnp.arange(count, dtype=jnp.int32) - starts[sorted_target]
     rank = jnp.zeros((count,), jnp.int32).at[order].set(sorted_rank)
     slot = target * capacity + rank

time: 411 us -> 411 us (level)
  no operation moved by 1% of the time
where the time goes in v1:
time: 411 us; the launch traced here: 410 us
  local copies, waits for them, and re-layouts  301 us (73%)
  waiting for transfers between devices  62.5 us (15%)
  starting transfers between devices  22.6 us (5%)
  other arithmetic  15.5 us (4%)
  matrix products  8.23 us (2%)
    gather x16, local copies, waits for them, and re-layouts, interpolate(): values = jnp.take(flat_stress, corner, axis=1)  137 us
    gather x3, local copies, waits for them, and re-layouts, band(): picked = weights[jnp.clip(offset, 0, 2 * radius)]  126 us
    ppermute x3, waiting for transfers between devices, padded(): before = lax.ppermute(last, axis, up)  26.9 us
    ppermute x3, waiting for transfers between devices, padded(): after = lax.ppermute(initial, axis, down)  21.6 us
    another operation x2, local copies, waits for them, and re-layouts, on_device(): jnp.stack([filtered[3 + k] - filtered[first] * filtered[second] for k, (f...  10.3 us
  transfers between devices with their start and end apart: 9, of which 4 were waited for; matrix products, arithmetic and copies ran while one was open for 39% of the time, Pallas kernels for 0%

profile of v1, /device:TPU:0, one launch (start us, length us, event | category | flops | bytes accessed | tf_op | source)
XLA Modules:
  0.0 409.8 jit_solution(8461817480949750806)
XLA Ops:
  4.5 5.1 %sort.17 = (s32[1024]{0:T(1024)}, s32[1024]{0:T(1024)S(1)}) sort(s32[1024]{0:T(1024)} %bitcast.193, s32[1024]{0:T(1024)S(1)} %iota.56), dimensions={0}, to_apply=%region_0.0 | sort | flops 10240 | bytes 16384 | tf_op jit(solution)/shard_map/jit(argsort)/sort | solution.py:104
  10.5 4.5 %gather_fusion = s32[1024]{0:T(1024)S(1)} fusion(s32[1024]{0:T(1024)S(1)} %bitcast.194, s32[1024]{0:T(1024)S(1)} %get-tuple-element.45), kind=kCustom, calls=%fused_computation.8 | custom fusion | bytes 12288 | tf_op jit(solution)/shard_map/gather | solution.py:105
  15.0 4.3 %compare_select_fusion.11 = s32[1024,1]{0,1:T(1,128)S(1)} fusion(s32[]{:T(128)} %bitcast.3, s32[]{:T(128)} %bitcast.4, s32[]{:T(128)} %bitcast.5, s32[]{:T(128)} %bitcast.6, s32[]{:T(128)} %bitcast.7, s32[]{:T(128)} %bitcast.9, s32[]{:T(128)} %bitcast.8, s32[1024,1]{0,1:T(1,128)S(1)} %bitcast.210), kind=kLoop, calls=%fused_computation.127 | loop fusion | flops 15360 | bytes 8220 | tf_op jit(solution)/shard_map/gather | solution.py:111
  21.3 4.8 %gather_fusion.1 = f32[768]{0:T(1024)S(1)} fusion(f32[33]{0:T(128)S(1)} %broadcast_divide_fusion, s32[1024]{0:T(1024)S(1)} %get-tuple-element.55), kind=kCustom, calls=%fused_computation.9 | custom fusion | bytes 9216 | tf_op jit(solution)/shard_map/gather | solution.py:37
  26.2 4.3 %scatter_custom_fusion = s32[1024]{0:T(1024)S(1)} fusion(s32[1024]{0:T(1024)S(1)} %get-tuple-element.46, s32[1024]{0:T(1024)S(1)} %select_subtract_fusion, s32[]{:T(128)} %constant.31.clone.1), kind=kCustom, calls=%fused_computation.164 | custom fusion | bytes 4100 | tf_op jit(solution)/shard_map/scatter | solution.py:112
  38.4 4.9 %scatter_custom_fusion.2 = s32[4096]{0:T(1024)} fusion(s32[1024]{0:T(1024)S(1)} %get-tuple-element.9, s32[1024]{0:T(1024)S(1)} %multiply_add_fusion, s32[]{:T(128)} %constant.31.clone.1), kind=kCustom, calls=%fused_computation.150 | custom fusion | bytes 16388 | tf_op jit(solution)/shard_map/scatter | solution.py:115
  43.3 4.2 %all-to-all-start.1 = ((s32[1,8,512]{2,0,1:T(1,128)}), s32[1,8,512]{2,0,1:T(1,128)S(1)}, u32[]{:S(2)}, u32[]{:S(2)}) async-start(s32[1,8,512]{2,0,1:T(1,128)} %bitcast.16), calls=%async_computation.1 | async-start | bytes 32768 | tf_op jit(solution)/shard_map/all_to_all | solution.py:119
  47.5 121.4 %gather_fusion.2 = f32[20480]{0:T(1024)S(1)} fusion(f32[33]{0:T(128)S(1)} %broadcast_divide_fusion, s32[20480]{0:T(1024)S(1)} %fusion.36), kind=kCustom, calls=%fused_computation.10 | custom fusion | bytes 245760 | tf_op jit(solution)/shard_map/gather | solution.py:37
  170.0 4.0 scatter_custom_fusion.1
  175.2 6.0 %all-to-all-start = ((f32[3,8,512]{2,0,1:T(4,128)}), f32[3,8,512]{2,0,1:T(4,128)S(1)}, u32[]{:S(2)}, u32[]{:S(2)}) async-start(f32[3,8,512]{2,0,1:T(4,128)} %copy.97), calls=%async_computation | async-start | bytes 131072 | tf_op jit(solution)/shard_map/all_to_all | solution.py:126
  181.3 6.8 %all-to-all-done = f32[3,8,512]{2,0,1:T(4,128)S(1)} async-done(((f32[3,8,512]{2,0,1:T(4,128)}), f32[3,8,512]{2,0,1:T(4,128)S(1)}, u32[]{:S(2)}, u32[]{:S(2)}) %all-to-all-start) | async-done | bytes 49184 | tf_op jit(solution)/shard_map/all_to_all | solution.py:126
  195.3 26.9 %collective-permute-done.4 = f32[9,16,16,16]{3,2,1,0:T(8,128)S(1)} collective-permute-done((f32[9,16,16,16]{3,2,1,0:T(8,128)S(1)}, f32[9,16,16,16]{3,2,1,0:T(8,128)S(1)}, u32[]{:S(2)}, u32[]{:S(2)}) %collective-permute-start.4) | collective-permute-done | bytes 147488 | tf_op jit(solution)/shard_map/ppermute | solution.py:19
  222.2 21.6 %collective-permute-done.5 = f32[9,16,16,16]{3,2,1,0:T(8,128)S(1)} collective-permute-done((f32[9,16,16,16]{3,2,1,0:T(8,128)S(1)}, f32[9,16,16,16]{3,2,1,0:T(8,128)S(1)}, u32[]{:S(2)}, u32[]{:S(2)}) %collective-permute-start.5) | collective-permute-done | bytes 147488 | tf_op jit(solution)/shard_map/ppermute | solution.py:20
  247.5 9.0 %copy.112 = f32[6,32768]{0,1:T(8,128)} copy(f32[6,32768]{1,0:T(8,128)S(1)} %stack.67) | data formatting | bytes 1572864 | tf_op jit(solution)/shard_map/stack | solution.py:91
  256.5 16.5 %gather_fusion.4 = f32[4096,6]{1,0:T(8,128)S(1)} fusion(f32[6,32768]{0,1:T(8,128)} %copy.112, s32[4096]{0:T(1024)S(1)} %get-tuple-element.37), kind=kCustom, calls=%fused_computation.clone | custom fusion | bytes 212992 | tf_op jit(solution)/shard_map/jit(_take)/gather | solution.py:61
  273.7 16.5 %gather_fusion.5 = f32[4096,6]{1,0:T(8,128)S(1)} fusion(f32[6,32768]{0,1:T(8,128)} %copy.112, s32[4096]{0:T(1024)S(1)} %get-tuple-element.42), kind=kCustom, calls=%fused_computation.1.clone | custom fusion | bytes 212992 | tf_op jit(solution)/shard_map/jit(_take)/gather | solution.py:61
  290.8 16.5 %gather_fusion.6 = f32[4096,6]{1,0:T(8,128)S(1)} fusion(f32[6,32768]{0,1:T(8,128)} %copy.112, s32[4096]{0:T(1024)S(1)} %get-tuple-element.41), kind=kCustom, calls=%fused_computation.2.clone | custom fusion | bytes 212992 | tf_op jit(solution)/shard_map/jit(_take)/gather | solution.py:61
  308.0 16.5 %gather_fusion.7 = f32[4096,6]{1,0:T(8,128)S(1)} fusion(f32[6,32768]{0,1:T(8,128)} %copy.112, s32[4096]{0:T(1024)S(1)} %get-tuple-element.40), kind=kCustom, calls=%fused_computation.3.clone | custom fusion | bytes 212992 | tf_op jit(solution)/shard_map/jit(_take)/gather | solution.py:61
  325.2 16.5 %gather_fusion.8 = f32[4096,6]{1,0:T(8,128)S(1)} fusion(f32[6,32768]{0,1:T(8,128)} %copy.112, s32[4096]{0:T(1024)S(1)} %get-tuple-element.39), kind=kCustom, calls=%fused_computation.4.clone | custom fusion | bytes 212992 | tf_op jit(solution)/shard_map/jit(_take)/gather | solution.py:61
  342.3 16.5 %gather_fusion.9 = f32[4096,6]{1,0:T(8,128)S(1)} fusion(f32[6,32768]{0,1:T(8,128)} %copy.112, s32[4096]{0:T(1024)S(1)} %get-tuple-element.38), kind=kCustom, calls=%fused_computation.5.clone | custom fusion | bytes 212992 | tf_op jit(solution)/shard_map/jit(_take)/gather | solution.py:61
  359.5 16.5 %gather_fusion.10 = f32[4096,6]{1,0:T(8,128)S(1)} fusion(f32[6,32768]{0,1:T(8,128)} %copy.112, s32[4096]{0:T(1024)S(1)} %get-tuple-element.43), kind=kCustom, calls=%fused_computation.6.clone | custom fusion | bytes 212992 | tf_op jit(solution)/shard_map/jit(_take)/gather | solution.py:61
  376.7 16.5 %gather_fusion.11 = f32[4096,6]{1,0:T(8,128)S(1)} fusion(f32[6,32768]{0,1:T(8,128)} %copy.112, s32[4096]{0:T(1024)S(1)} %get-tuple-element.44), kind=kCustom, calls=%fused_computation.7.clone | custom fusion | bytes 212992 | tf_op jit(solution)/shard_map/jit(_take)/gather | solution.py:61
  394.7 3.4 all-to-all-start.2
  398.1 7.3 %all-to-all-done.2 = f32[6,8,512]{2,0,1:T(8,128)S(1)} async-done(((f32[6,8,512]{2,0,1:T(8,128)}), f32[6,8,512]{2,0,1:T(8,128)S(1)}, u32[]{:S(2)}, u32[]{:S(2)}) %all-to-all-start.2) | async-done | bytes 98336 | tf_op jit(solution)/shard_map/all_to_all | solution.py:136
  (77 shorter events, 38.7 us)
Async XLA Ops:
  0.0 10.4 %copy-start = (s32[1024,1]{0,1:T(1,128)S(1)}, s32[1024,1]{0,1:T(1,128)}, u32[]{:S(2)}) copy-start(s32[1024,1]{0,1:T(1,128)} %param.9) | copy-start | bytes 12292
  1.1 29.4 %collective-permute-start = (f32[3,16,16,128]{3,1,2,0:T(8,128)S(1)}, f32[3,16,16,128]{3,1,2,0:T(8,128)S(1)}, u32[]{:S(2)}, u32[]{:S(2)}) collective-permute-start(f32[3,16,16,128]{3,1,2,0:T(8,128)S(1)} %copy.98), channel_id=1, source_target_pairs={{0,1},{1,2},{2,3},{3,0},{4,5},{5,6},{6,7},{7,4},{8,9},{9,10},{10,1... | collective-permute-start | bytes 1179656 | tf_op jit(solution)/shard_map/ppermute | solution.py:19
  1.6 29.1 %collective-permute-start.1 = (f32[3,16,16,128]{3,1,2,0:T(8,128)S(1)}, f32[3,16,16,128]{3,1,2,0:T(8,128)S(1)}, u32[]{:S(2)}, u32[]{:S(2)}) collective-permute-start(f32[3,16,16,128]{3,1,2,0:T(8,128)S(1)} %copy.98), channel_id=1, source_target_pairs={{1,0},{2,1},{3,2},{0,3},{5,4},{6,5},{7,6},{4,7},{9,8},{10,9},{11,1... | collective-permute-start | bytes 1179656 | tf_op jit(solution)/shard_map/ppermute | solution.py:20
  10.4 10.2 %copy-start.3 = (s32[1024]{0:T(1024)S(1)}, s32[1024]{0:T(1024)}, u32[]{:S(2)}) copy-start(s32[1024]{0:T(1024)} %param.11) | copy-start | bytes 12292
  10.5 10.2 %copy-start.4 = (s32[1024]{0:T(1024)S(1)}, s32[1024]{0:T(1024)}, u32[]{:S(2)}) copy-start(s32[1024]{0:T(1024)} %param.10) | copy-start | bytes 12292
  10.5 10.2 %copy-start.5 = (s32[1024]{0:T(1024)S(1)}, s32[1024]{0:T(1024)}, u32[]{:S(2)}) copy-start(s32[1024]{0:T(1024)} %param.12) | copy-start | bytes 12292
  21.3 9.2 %copy-start.1 = (f32[3,16,16,128]{3,2,1,0:T(8,128)S(1)}, f32[3,16,16,128]{3,2,1,0:T(8,128)}, u32[]{:S(2)}) copy-start(f32[3,16,16,128]{3,2,1,0:T(8,128)} %param.8) | copy-start | bytes 1179652
  34.0 154.2 %collective-permute-start.2 = (f32[9,16,16,128]{3,1,2,0:T(8,128)S(1)}, f32[9,16,16,128]{3,1,2,0:T(8,128)}, u32[]{:S(2)}, u32[]{:S(2)}) collective-permute-start(f32[9,16,16,128]{3,1,2,0:T(8,128)S(1)} %fusion.11), channel_id=1, source_target_pairs={{0,8},{8,16},{16,24},{24,0},{1,9},{9,17},{17,25},{25,1},{2,10},{10... | collective-permute-start | bytes 3538952 | tf_op jit(solution)/shard_map/ppermute | solution.py:19
  36.3 151.8 %collective-permute-start.3 = (f32[9,16,16,128]{3,1,2,0:T(8,128)S(1)}, f32[9,16,16,128]{3,1,2,0:T(8,128)}, u32[]{:S(2)}, u32[]{:S(2)}) collective-permute-start(f32[9,16,16,128]{3,1,2,0:T(8,128)S(1)} %fusion.11), channel_id=1, source_target_pairs={{8,0},{16,8},{24,16},{0,24},{9,1},{17,9},{25,17},{1,25},{10,2},{18... | collective-permute-start | bytes 3538952 | tf_op jit(solution)/shard_map/ppermute | solution.py:20
  43.3 131.9 %all-to-all-start.1 = ((s32[1,8,512]{2,0,1:T(1,128)}), s32[1,8,512]{2,0,1:T(1,128)S(1)}, u32[]{:S(2)}, u32[]{:S(2)}) async-start(s32[1,8,512]{2,0,1:T(1,128)} %bitcast.16), calls=%async_computation.1 | async-start | bytes 32768 | tf_op jit(solution)/shard_map/all_to_all | solution.py:119
  47.5 121.4 %copy-start.2 = (f32[3,1024]{1,0:T(4,128)S(1)}, f32[3,1024]{1,0:T(4,128)}, u32[]{:S(2)}) copy-start(f32[3,1024]{1,0:T(4,128)} %param.13) | copy-start | bytes 36868
  175.2 12.9 %all-to-all-start = ((f32[3,8,512]{2,0,1:T(4,128)}), f32[3,8,512]{2,0,1:T(4,128)S(1)}, u32[]{:S(2)}, u32[]{:S(2)}) async-start(f32[3,8,512]{2,0,1:T(4,128)} %copy.97), calls=%async_computation | async-start | bytes 131072 | tf_op jit(solution)/shard_map/all_to_all | solution.py:126
  193.2 29.0 %collective-permute-start.4 = (f32[9,16,16,16]{3,2,1,0:T(8,128)S(1)}, f32[9,16,16,16]{3,2,1,0:T(8,128)S(1)}, u32[]{:S(2)}, u32[]{:S(2)}) collective-permute-start(f32[9,16,16,16]{3,2,1,0:T(8,128)S(1)} %get-tuple-element.16), channel_id=1, source_target_pairs={{0,4},{4,0},{1,5},{5,1},{2,6},{6,2},{3,7},{7,3},{8,12},{12,8},{9,1... | collective-permute-start | bytes 442376 | tf_op jit(solution)/shard_map/ppermute | solution.py:19
  193.7 50.1 %collective-permute-start.5 = (f32[9,16,16,16]{3,2,1,0:T(8,128)S(1)}, f32[9,16,16,16]{3,2,1,0:T(8,128)S(1)}, u32[]{:S(2)}, u32[]{:S(2)}) collective-permute-start(f32[9,16,16,16]{3,2,1,0:T(8,128)S(1)} %get-tuple-element.17), channel_id=1, source_target_pairs={{4,0},{0,4},{5,1},{1,5},{6,2},{2,6},{7,3},{3,7},{12,8},{8,12},{13,... | collective-permute-start | bytes 442376 | tf_op jit(solution)/shard_map/ppermute | solution.py:20
  394.7 10.7 %all-to-all-start.2 = ((f32[6,8,512]{2,0,1:T(8,128)}), f32[6,8,512]{2,0,1:T(8,128)S(1)}, u32[]{:S(2)}, u32[]{:S(2)}) async-start(f32[6,8,512]{2,0,1:T(8,128)} %bitcast.59), calls=%async_computation.2 | async-start | bytes 262144 | tf_op jit(solution)/shard_map/all_to_all | solution.py:136

commit v2 on v0

v2 whole, which is shorter than its diff:
```python
import math

import jax
import jax.numpy as jnp
import numpy as np
from jax import lax
from jax.experimental import pallas as pl
from jax.experimental.pallas import tpu as pltpu
from jax.sharding import PartitionSpec as P

FW = 32
PAIRS = ((0, 0), (0, 1), (0, 2), (1, 1), (1, 2), (2, 2))
ROWS = 8
F32 = jnp.float32
BF16 = jnp.bfloat16
WHOLE = pl.BlockSpec(memory_space=pltpu.VMEM)
PARAMS = pltpu.CompilerParams(vmem_limit_bytes=48 * 1024 * 1024)


def taps():
    radius = FW // 2
    values = [math.exp(-6.0 * (m - radius) ** 2 / FW**2) for m in range(2 * radius + 1)]
    return [v / sum(values) for v in values]


def neighbours(x, axis):
    devices = lax.axis_size(axis)
    up = [(i, (i + 1) % devices) for i in range(devices)]
    down = [(j, i) for i, j in up]
    return lax.ppermute(x, axis, up), lax.ppermute(x, axis, down)


def symmetric(values, centre):
    radius = FW // 2
    g = taps()
    total = g[radius] * values[centre]
    for m in range(1, radius + 1):
        total = total + g[radius + m] * (values[centre - m] + values[centre + m])
    return total


def split2(x):
    high = x.astype(BF16)
    return high, (x - high.astype(F32)).astype(BF16)


def split3(x):
    high, rest = x.astype(BF16), None
    rest = x - high.astype(F32)
    middle = rest.astype(BF16)
    return high, middle, (rest - middle.astype(F32)).astype(BF16)


def z_kernel(before, own, after, out, wide):
    layers, size_x = own.shape[1], own.shape[2]
    radius = FW // 2

    for part, (ref, skip) in enumerate(((before, layers - radius), (own, 0), (after, 0))):
        place = (0, radius, radius + layers)[part]

        def products(z, carry, ref=ref, skip=skip, place=place):
            u = [ref[k, z + skip] for k in range(3)]
            for k in range(3):
                wide[k, z + place] = u[k]
            for k, (a, b) in enumerate(PAIRS):
                wide[3 + k, z + place] = u[a] * u[b]
            return carry

        lax.fori_loop(0, layers if part == 1 else radius, products, 0)

    def filtered(f, carry):
        for x in range(0, size_x, 8):
            values = [wide[f, z, x : x + 8] for z in range(layers + 2 * radius)]
            for z in range(layers):
                out[f, z, x : x + 8] = symmetric(values, z + radius)
        return carry

    lax.fori_loop(0, 9, filtered, 0)


def along_z(before, own, after):
    _, z, x, y = own.shape
    return pl.pallas_call(
        z_kernel,
        out_shape=jax.ShapeDtypeStruct((9, z, x, y), F32),
        in_specs=[WHOLE] * 3,
        out_specs=WHOLE,
        scratch_shapes=[pltpu.VMEM((9, z + FW, x, y), F32)],
        compiler_params=PARAMS,
        cost_estimate=pl.CostEstimate(flops=9 * z * x * y * 66, bytes_accessed=21 * z * x * y * 4, transcendentals=0),
    )(before, own, after)


def x_kernel(before, own, after, out, strips, wide):
    layers, size_x, size_y = own.shape[1:]
    radius = FW // 2

    def filtered(n, carry):
        f, z = n // layers, n % layers
        wide[0:radius] = before[f, z, size_x - radius :]
        wide[radius : radius + size_x] = own[f, z]
        wide[radius + size_x :] = after[f, z, :radius]
        values = [wide[i : i + 8] for i in range(size_x + FW - 7)]
        for x in range(0, size_x, 8):
            total = symmetric(values, x + radius)
            row = pl.ds(pl.multiple_of(z * size_x, 8) + x, 8)
            out[f, row] = total
            strips[f, row, :radius] = total[:, :radius]
            strips[f, row, radius:] = total[:, size_y - radius :]
        return carry

    lax.fori_loop(0, 9 * layers, filtered, 0)


def along_x(before, own, after):
    _, z, x, y = own.shape
    return pl.pallas_call(
        x_kernel,
        out_shape=(
            jax.ShapeDtypeStruct((9, z * x, y), F32),
            jax.ShapeDtypeStruct((9, z * x, FW), F32),
        ),
        in_specs=[WHOLE] * 3,
        out_specs=(WHOLE, WHOLE),
        scratch_shapes=[pltpu.VMEM((x + FW, y), F32)],
        compiler_params=PARAMS,
        cost_estimate=pl.CostEstimate(flops=9 * z * x * y * 66, bytes_accessed=40 * z * x * y * 4, transcendentals=0),
    )(before, own, after)


def sample_kernel(own, strips, band, w_high, w_low, w_y, out, field_high, field_low):
    cells, size_y = own.shape[1:]

    def smooth(f):
        a = lax.dot_general(
            band[:, :size_y], own[f], (((1,), (1,)), ((), ())),
            precision=lax.Precision.HIGHEST, preferred_element_type=F32,
        )
        b = lax.dot_general(
            band[:, size_y:], strips[f], (((1,), (1,)), ((), ())),
            precision=lax.Precision.HIGHEST, preferred_element_type=F32,
        )
        return a + b

    mean = [smooth(k) for k in range(3)]
    for k, (a, b) in enumerate(PAIRS):
        high, low = split2(smooth(3 + k) - mean[a] * mean[b])
        field_high[k * size_y : (k + 1) * size_y] = high
        field_low[k * size_y : (k + 1) * size_y] = low

    count = w_y.shape[1]
    block = min(count, 256)

    def sample(n, carry):
        here = pl.ds(pl.multiple_of(n * block, block), block)
        wide = jnp.dot(field_high[...], w_high[:, here], preferred_element_type=F32)
        wide = wide + jnp.dot(field_low[...], w_high[:, here], preferred_element_type=F32)
        wide = wide + jnp.dot(field_high[...], w_low[:, here], preferred_element_type=F32)
        weight = w_y[:, here]
        for k in range(6):
            out[k : k + 1, here] = jnp.sum(wide[k * size_y : (k + 1) * size_y] * weight, axis=0, keepdims=True)
        out[6:8, here] = jnp.zeros((2, block), F32)
        return carry

    lax.fori_loop(0, count // block, sample, 0)


def samples(own, strips, band, w_high, w_low, w_y):
    cells, size_y = own.shape[1:]
    count = w_y.shape[1]
    return pl.pallas_call(
        sample_kernel,
        out_shape=jax.ShapeDtypeStruct((ROWS, count), F32),
        in_specs=[WHOLE] * 6,
        out_specs=WHOLE,
        scratch_shapes=[pltpu.VMEM((6 * size_y, cells), BF16), pltpu.VMEM((6 * size_y, cells), BF16)],
        compiler_params=PARAMS,
        cost_estimate=pl.CostEstimate(flops=6 * size_y * cells * count * 6, bytes_accessed=8 * 1024 * 1024, transcendentals=0),
    )(own, strips, band, w_high, w_low, w_y)


def route_kernel(owners, capacity, owner, cells, weights, out, rank_out):
    count = owner.shape[1]
    target = owner[...]
    named = lax.broadcasted_iota(jnp.int32, (owners, count), 0) == target
    earlier = lax.broadcasted_iota(jnp.int32, (count, count), 0) < lax.broadcasted_iota(jnp.int32, (count, count), 1)
    before = jnp.dot(
        jnp.where(named, 1.0, 0.0).astype(BF16), jnp.where(earlier, 1.0, 0.0).astype(BF16),
        preferred_element_type=F32,
    )
    rank = jnp.sum(jnp.where(named, before, 0.0), axis=0, keepdims=True).astype(jnp.int32)
    rank_out[...] = rank
    slot = lax.broadcasted_iota(jnp.int32, (capacity, count), 0) == rank
    slot = jnp.where(slot, 1.0, 0.0).astype(BF16)
    record = jnp.concatenate(
        [cells[...].astype(F32), weights[...], jnp.zeros((ROWS - 6, count), F32)], axis=0
    )
    total = jnp.zeros((owners * ROWS, capacity), F32)
    for part in split3(record):
        part = part.astype(F32)
        spread = jnp.concatenate(
            [jnp.where(target == o, part, 0.0) for o in range(owners)], axis=0
        ).astype(BF16)
        total = total + lax.dot_general(spread, slot, (((1,), (1,)), ((), ())), preferred_element_type=F32)
    out[...] = total


def route(owner, cells, weights, owners, capacity):
    count = owner.shape[1]

    def kernel(*refs):
        route_kernel(owners, capacity, *refs)

    return pl.pallas_call(
        kernel,
        out_shape=(
            jax.ShapeDtypeStruct((owners * ROWS, capacity), F32),
            jax.ShapeDtypeStruct((1, count), jnp.int32),
        ),
        in_specs=[WHOLE] * 3,
        out_specs=(WHOLE, WHOLE),
        compiler_params=PARAMS,
        cost_estimate=pl.CostEstimate(flops=10 * count * count * owners, bytes_accessed=count * 4 * 40, transcendentals=0),
    )(owner, cells, weights)


def hat_kernel(size_x, size_z, size_y, asked, w_high, w_low, w_y):
    def hat(size, row, offset):
        distance = lax.broadcasted_iota(jnp.int32, (size, asked.shape[1]), 0) - row.astype(jnp.int32)
        return jnp.where(distance == 0, 1.0 - offset, jnp.where(distance == 1, offset, 0.0))

    in_z = hat(size_z, asked[0:1], asked[5:6])
    in_x = hat(size_x, asked[1:2], asked[3:4])
    w_y[...] = hat(size_y, asked[2:3], asked[4:5])
    for z in range(size_z):
        high, low = split2(in_z[z : z + 1] * in_x)
        w_high[z * size_x : (z + 1) * size_x] = high
        w_low[z * size_x : (z + 1) * size_x] = low


def hats(asked, size_z, size_x, size_y):
    count = asked.shape[1]
    block = 512

    def kernel(*refs):
        hat_kernel(size_x, size_z, size_y, *refs)

    def columns(rows):
        return pl.BlockSpec((rows, block), lambda n: (0, n))

    return pl.pallas_call(
        kernel,
        grid=(count // block,),
        out_shape=(
            jax.ShapeDtypeStruct((size_z * size_x, count), BF16),
            jax.ShapeDtypeStruct((size_z * size_x, count), BF16),
            jax.ShapeDtypeStruct((size_y, count), F32),
        ),
        in_specs=[columns(ROWS)],
        out_specs=(columns(size_z * size_x), columns(size_z * size_x), columns(size_y)),
        compiler_params=PARAMS,
        cost_estimate=pl.CostEstimate(flops=count * 2000, bytes_accessed=count * 1600, transcendentals=0),
    )(asked)


def return_kernel(owners, back, owner, rank, out):
    capacity = back.shape[1]
    count = owner.shape[1]
    slot = lax.broadcasted_iota(jnp.int32, (capacity, count), 0) == rank[...]
    slot = jnp.where(slot, 1.0, 0.0).astype(BF16)
    picked = jnp.zeros((owners * ROWS, count), F32)
    for part in split3(back[...]):
        picked = picked + jnp.dot(part, slot, preferred_element_type=F32)
    target = owner[...]
    total = jnp.zeros((ROWS, count), F32)
    for o in range(owners):
        total = total + jnp.where(target == o, picked[o * ROWS : (o + 1) * ROWS], 0.0)
    out[...] = total[:6]


def returned(back, owner, rank, owners):
    count = owner.shape[1]

    def kernel(*refs):
        return_kernel(owners, *refs)

    return pl.pallas_call(
        kernel,
        out_shape=jax.ShapeDtypeStruct((6, count), F32),
        in_specs=[WHOLE] * 3,
        out_specs=WHOLE,
        compiler_params=PARAMS,
        cost_estimate=pl.CostEstimate(flops=6 * owners * ROWS * back.shape[1] * count, bytes_accessed=count * 100, transcendentals=0),
    )(back, owner, rank)


def y_band(size_y):
    radius = FW // 2
    place = np.concatenate([np.arange(size_y + radius), np.arange(-radius, 0)])
    offset = place[None, :] - np.arange(size_y)[:, None] + radius
    g = np.array(taps())
    return np.where((offset >= 0) & (offset <= FW), g[np.clip(offset, 0, FW)], 0.0).astype(np.float32)


def y_strips(edges):
    radius = FW // 2
    devices = lax.axis_size("gy")
    if devices == 2:
        return lax.ppermute(edges, "gy", [(0, 1), (1, 0)])
    up = [(i, (i + 1) % devices) for i in range(devices)]
    down = [(j, i) for i, j in up]
    after = lax.ppermute(edges[..., :radius], "gy", down)
    before = lax.ppermute(edges[..., radius:], "gy", up)
    return jnp.concatenate([after, before], axis=-1)


def on_device(velocity, owner, cell_x, cell_y, cell_z, query_weights):
    _, size_z, size_x, size_y = velocity.shape
    owners = lax.axis_size("gx") * lax.axis_size("gy")
    count = owner.shape[0]
    capacity = 4 * count // owners

    left, right = neighbours(velocity, "gx")
    own_halo = neighbours(velocity, "gz")

    target = owner.reshape(1, count)
    cells = jnp.stack([cell_z, cell_x, cell_y])
    sent, rank = route(target, cells, query_weights, owners, capacity)
    asked = lax.all_to_all(sent.reshape(owners, ROWS, capacity), ("gx", "gy"), split_axis=0, concat_axis=0, tiled=True)
    asked = asked.transpose(1, 0, 2).reshape(ROWS, owners * capacity)
    w_high, w_low, w_y = hats(asked, size_z, size_x, size_y)

    left_halo = neighbours(left, "gz")
    right_halo = neighbours(right, "gz")
    own_z = along_z(own_halo[0], velocity, own_halo[1])
    left_z = along_z(left_halo[0], left, left_halo[1])
    right_z = along_z(right_halo[0], right, right_halo[1])
    fields, edges = along_x(left_z, own_z, right_z)
    values = samples(fields, y_strips(edges), jnp.asarray(y_band(size_y)), w_high, w_low, w_y)
    values = values.reshape(ROWS, owners, capacity).transpose(1, 0, 2)
    back = lax.all_to_all(values, ("gx", "gy"), split_axis=0, concat_axis=0, tiled=True)
    return returned(back.reshape(owners * ROWS, capacity), target, rank, owners)


def solution(mesh):
    placed = (
        P(None, "gz", "gx", "gy"),
        P(("gx", "gy", "gz"), None),
        P(("gx", "gy", "gz")),
        P(("gx", "gy", "gz")),
        P(("gx", "gy", "gz")),
        P(None, ("gx", "gy", "gz")),
    )
    return jax.shard_map(
        on_device,
        mesh=mesh,
        in_specs=placed,
        out_specs=P(None, ("gx", "gy", "gz")),
        check_vma=False,
    )
```

time: 411 us -> 105 us (0.26)
  local copies, waits for them, and re-layouts: 301 us -> 7.02 us
  waiting for transfers between devices: 62.5 us -> 22.7 us
  Pallas kernels: 0 us -> 39.6 us
  blocking collectives: 0 us -> 27.2 us
  other arithmetic: 15.5 us -> 0.02 us
  starting transfers between devices: 22.6 us -> 8.48 us
  matrix products: 8.24 us -> 0 us
    gather x22 -> x0, local copies, waits for them, and re-layouts: 271 us -> none  [the longest x16 137 us: interpolate(): values = jnp.take(flat_stress, corner, axis=1)]
    pallas_call x0 -> x8, Pallas kernels: none -> 39.6 us  [the longest x1 14.2 us: along_x(): pl.pallas_call(x_kernel, out_shape=(jax.ShapeDtypeStruct((9, z * x, y), F...]
    all_to_all x0 -> x2, blocking collectives: none -> 27.2 us  [the longest x1 17.5 us: on_device(): lax.all_to_all(sent.reshape(owners, ROWS, capacity), ('gx', 'gy'), split_...]
    ppermute x6 -> x9, waiting for transfers between devices: 48.5 us -> 22.7 us  [the longest x8 22.7 us: neighbours(): return (lax.ppermute(x, axis, up), lax.ppermute(x, axis, down))]
    all_to_all x3 -> x0, waiting for transfers between devices: 14.1 us -> none  [the longest x1 7.27 us: on_device(): lax.all_to_all(values, ('gx', 'gy'), split_axis=1, concat_axis=1, tiled=T...]
    all_to_all x3 -> x0, starting transfers between devices: 13.5 us -> none  [the longest x1 6 us: on_device(): lax.all_to_all(send_weight.reshape(3, owners, capacity), ('gx', 'gy'), sp...]
    scatter x3 -> x0, local copies, waits for them, and re-layouts: 13.2 us -> none  [the longest x1 4.89 us: on_device(): jnp.zeros((owners * capacity,), jnp.int32).at[slot].set(local_cell)]
    another operation x2 -> x0, local copies, waits for them, and re-layouts: 10.3 us -> none  [on_device(): jnp.stack([filtered[3 + k] - filtered[first] * filtered[second] for k, (f...]
  transfers between devices with their start and end apart: 9 -> 9, of which waited for: 4 -> 5; matrix products, arithmetic and copies ran while one was open for 39% -> 0% of each run, Pallas kernels for 0% -> 9%
where the time goes in v2:
time: 105 us
  Pallas kernels  39.6 us (38%)
  blocking collectives  27.2 us (26%)
  waiting for transfers between devices  22.7 us (22%)
  starting transfers between devices  8.48 us (8%)
  local copies, waits for them, and re-layouts  7.02 us (7%)
    ppermute x8, waiting for transfers between devices, neighbours(): return (lax.ppermute(x, axis, up), lax.ppermute(x, axis, down))  22.7 us
    all_to_all x1, blocking collectives, on_device(): lax.all_to_all(sent.reshape(owners, ROWS, capacity), ('gx', 'gy'), split_...  17.5 us
    pallas_call x1, Pallas kernels, along_x(): pl.pallas_call(x_kernel, out_shape=(jax.ShapeDtypeStruct((9, z * x, y), F...  14.2 us
    pallas_call x1, Pallas kernels, samples(): pl.pallas_call(sample_kernel, out_shape=jax.ShapeDtypeStruct((ROWS, count...  12.1 us
    all_to_all x1, blocking collectives, on_device(): lax.all_to_all(values, ('gx', 'gy'), split_axis=0, concat_axis=0, tiled=T...  9.74 us
    pallas_call x3, Pallas kernels, along_z(): pl.pallas_call(z_kernel, out_shape=jax.ShapeDtypeStruct((9, z, x, y), F32...  6.84 us
    ppermute x8, starting transfers between devices, neighbours(): return (lax.ppermute(x, axis, up), lax.ppermute(x, axis, down))  6.77 us
    unnamed x20, local copies, waits for them, and re-layouts  4.63 us
  transfers between devices with their start and end apart: 9, of which 5 were waited for; matrix products, arithmetic and copies ran while one was open for 0% of the time, Pallas kernels for 9%

profile of v2, /device:TPU:0, one launch (start us, length us, event | category | flops | bytes accessed | tf_op | source)
XLA Modules:
  0.0 105.1 jit_solution(9021259610228226231)
XLA Ops:
  0.0 3.0 %collective-permute-start = (f32[3,16,16,128]{3,2,1,0:T(8,128)}, f32[3,16,16,128]{3,2,1,0:T(8,128)S(1)}, u32[]{:S(2)}, u32[]{:S(2)}) collective-permute-start(f32[3,16,16,128]{3,2,1,0:T(8,128)} %own.1), channel_id=1, source_target_pairs={{0,8},{8,16},{16,24},{24,0},{1,9},{9,17},{17,25},{25,1},{2,10},{10... | collective-permute-start | bytes 1179656 | tf_op jit(solution)/shard_map/ppermute | solution.py:30
  3.0 2.0 %collective-permute-start.5 = (f32[3,16,16,128]{3,2,1,0:T(8,128)}, f32[3,16,16,128]{3,2,1,0:T(8,128)S(1)}, u32[]{:S(2)}, u32[]{:S(2)}) collective-permute-start(f32[3,16,16,128]{3,2,1,0:T(8,128)} %own.1), channel_id=1, source_target_pairs={{8,0},{16,8},{24,16},{0,24},{9,1},{17,9},{25,17},{1,25},{10,2},{18... | collective-permute-start | bytes 1179656 | tf_op jit(solution)/shard_map/ppermute | solution.py:30
  5.1 0.7 collective-permute-start.4
  5.7 9.5 %collective-permute-done.own = f32[3,16,16,128]{3,2,1,0:T(8,128)S(1)} collective-permute-done((f32[3,16,16,128]{3,2,1,0:T(8,128)}, f32[3,16,16,128]{3,2,1,0:T(8,128)S(1)}, u32[]{:S(2)}, u32[]{:S(2)}) %collective-permute-start) | collective-permute-done | bytes 393248 | tf_op jit(solution)/shard_map/ppermute | solution.py:30
  15.8 6.5 %collective-permute-done.5.own = f32[3,16,16,128]{3,2,1,0:T(8,128)S(1)} collective-permute-done((f32[3,16,16,128]{3,2,1,0:T(8,128)}, f32[3,16,16,128]{3,2,1,0:T(8,128)S(1)}, u32[]{:S(2)}, u32[]{:S(2)}) %collective-permute-start.5) | collective-permute-done | bytes 393248 | tf_op jit(solution)/shard_map/ppermute | solution.py:30
  22.8 1.0 copy-done
  23.8 2.3 %shard_map.74.own = f32[9,16,16,128]{3,2,1,0:T(8,128)S(1)} custom-call(f32[3,16,16,128]{3,2,1,0:T(8,128)S(1)} %collective-permute-done.3.before, f32[3,16,16,128]{3,2,1,0:T(8,128)S(1)} %copy-done, f32[3,16,16,128]{3,2,1,0:T(8,128)S(1)} %collective-permute-done.4.after), custom_call_target="tpu_custom_call" | custom-call | flops 19464192 | bytes 2752512 | tf_op jit(solution)/shard_map/pallas_call | solution.py:83
  26.6 2.3 %shard_map.73.before = f32[9,16,16,128]{3,2,1,0:T(8,128)S(1)} custom-call(f32[3,16,16,128]{3,2,1,0:T(8,128)S(1)} %collective-permute-done.1.before, f32[3,16,16,128]{3,2,1,0:T(8,128)S(1)} %collective-permute-done.own, f32[3,16,16,128]{3,2,1,0:T(8,128)S(1)} %collective-permute-done.2.after), custom_call_target="tpu_custom_call" | custom-call | flops 19464192 | bytes 2752512 | tf_op jit(solution)/shard_map/pallas_call | solution.py:83
  28.9 3.4 %collective-permute-done.7.after = f32[3,16,16,128]{3,2,1,0:T(8,128)S(1)} collective-permute-done((f32[3,16,16,128]{3,2,1,0:T(8,128)S(1)}, f32[3,16,16,128]{3,2,1,0:T(8,128)S(1)}, u32[]{:S(2)}, u32[]{:S(2)}) %collective-permute-start.7) | collective-permute-done | bytes 393248 | tf_op jit(solution)/shard_map/ppermute | solution.py:30
  32.3 2.7 %collective-permute-done.6.before = f32[3,16,16,128]{3,2,1,0:T(8,128)S(1)} collective-permute-done((f32[3,16,16,128]{3,2,1,0:T(8,128)S(1)}, f32[3,16,16,128]{3,2,1,0:T(8,128)S(1)}, u32[]{:S(2)}, u32[]{:S(2)}) %collective-permute-start.6) | collective-permute-done | bytes 393248 | tf_op jit(solution)/shard_map/ppermute | solution.py:30
  35.0 2.3 %shard_map.75.after = f32[9,16,16,128]{3,2,1,0:T(8,128)S(1)} custom-call(f32[3,16,16,128]{3,2,1,0:T(8,128)S(1)} %collective-permute-done.6.before, f32[3,16,16,128]{3,2,1,0:T(8,128)S(1)} %collective-permute-done.5.own, f32[3,16,16,128]{3,2,1,0:T(8,128)S(1)} %collective-permute-done.7.after), custom_call_target="tpu_custom_call" | custom-call | flops 19464192 | bytes 2752512 | tf_op jit(solution)/shard_map/pallas_call | solution.py:83
  37.3 14.2 %shard_map.76 = (f32[9,256,128]{2,1,0:T(8,128)S(1)}, f32[9,256,32]{2,1,0:T(8,128)S(1)}) custom-call(f32[9,16,16,128]{3,2,1,0:T(8,128)S(1)} %shard_map.73.before, f32[9,16,16,128]{3,2,1,0:T(8,128)S(1)} %shard_map.74.own, f32[9,16,16,128]{3,2,1,0:T(8,128)S(1)} %shard_map.75.after), custom_call_target="tpu_custom_call" | custom-call | flops 19464192 | bytes 5242880 | tf_op jit(solution)/shard_map/pallas_call | solution.py:117
  51.5 1.1 %copy-done.2 = f32[9,256,128]{2,1,0:T(8,128)} copy-done((f32[9,256,128]{2,1,0:T(8,128)}, f32[9,256,128]{2,1,0:T(8,128)S(1)}, u32[]{:S(2)}) %copy-start.2) | copy-done | bytes 1179672
  52.6 1.1 %copy.8 = f32[9,256,32]{1,2,0:T(8,128)} copy(f32[9,256,32]{2,1,0:T(8,128)S(1)} %get-tuple-element.13) | data formatting | bytes 589824 | tf_op jit(solution)/shard_map/pallas_call | solution.py:117
  53.7 1.7 %collective-permute-start.8 = (f32[9,256,32]{1,2,0:T(8,128)}, f32[9,256,32]{1,2,0:T(8,128)}, u32[]{:S(2)}, u32[]{:S(2)}) collective-permute-start(f32[9,256,32]{1,2,0:T(8,128)} %copy.8), channel_id=1, source_target_pairs={{0,4},{4,0},{1,5},{5,1},{2,6},{6,2},{3,7},{7,3},{8,12},{12,8},{9,1... | collective-permute-start | bytes 884744 | tf_op jit(solution)/shard_map/ppermute | solution.py:309
  55.4 1.3 %shard_map.77 = (f32[64,512]{1,0:T(8,128)S(1)}, s32[1,1024]{1,0:T(1,128)S(1)}) custom-call(s32[1,1024]{1,0:T(1,128)S(1)} %bitcast.16, s32[3,1024]{1,0:T(4,128)S(1)} %pad_add_fusion.refs_1_, f32[3,1024]{1,0:T(4,128)S(1)} %copy-done.4), custom_call_target="tpu_custom_call" | custom-call | flops 83886080 | bytes 163840 | tf_op jit(solution)/shard_map/pallas_call | solution.py:214
  56.7 17.5 %all_to_all.10 = f32[8,8,512]{2,1,0:T(8,128)S(1)} all-to-all(f32[8,8,512]{2,1,0:T(8,128)S(1)} %bitcast.14), channel_id=1, replica_groups=mesh['gx'=4,'gy'=2,'gz'=4] {'gx','gy'}, dimensions={0} | all-to-all | bytes 262144 | tf_op jit(solution)/shard_map/all_to_all | solution.py:329
  74.1 3.9 %shard_map.78 = (bf16[256,4096]{1,0:T(8,128)(2,1)S(1)}, bf16[256,4096]{1,0:T(8,128)(2,1)S(1)}, f32[128,4096]{1,0:T(8,128)}) custom-call(f32[8,4096]{1,0:T(8,128)S(1)} %bitcast.12), custom_call_target="tpu_custom_call" | custom-call | flops 8192000 | bytes 6553600 | tf_op jit(solution)/shard_map/pallas_call | solution.py:251
  78.0 1.3 %copy-done.1 = bf16[256,4096]{1,0:T(8,128)(2,1)} copy-done((bf16[256,4096]{1,0:T(8,128)(2,1)}, bf16[256,4096]{1,0:T(8,128)(2,1)S(1)}, u32[]{:S(2)}) %copy-start.1) | copy-done | bytes 2097176
  79.3 1.3 %copy.9.strips = f32[9,256,32]{2,1,0:T(8,128)S(1)} copy(f32[9,256,32]{1,2,0:T(8,128)} %collective-permute-done.8) | data formatting | bytes 589824 | tf_op jit(solution)/shard_map/ppermute | solution.py:309
  80.6 1.3 %copy-done.3 = f32[9,256,128]{2,1,0:T(8,128)S(1)} copy-done((f32[9,256,128]{2,1,0:T(8,128)S(1)}, f32[9,256,128]{2,1,0:T(8,128)}, u32[]{:S(2)}) %copy-start.3) | copy-done | bytes 1179672
  81.9 12.1 %shard_map.79 = f32[8,4096]{1,0:T(8,128)S(1)} custom-call(f32[9,256,128]{2,1,0:T(8,128)S(1)} %copy-done.3, f32[9,256,32]{2,1,0:T(8,128)S(1)} %copy.9.strips, f32[128,160]{1,0:T(8,128)S(1)} %copy-done.6, bf16[256,4096]{1,0:T(8,128)(2,1)S(1)} %get-tuple-element.15.w_high, bf16[256,4096]{1,0:T(8,128)(2,1)} %copy-done.1, f32[128,4096]{1,0:T(8,128)} %get-tuple-element.17.w_y), custom_call_target="tpu_custom_call" | custom-call | flops 4831838208 | bytes 8388608 | tf_op jit(solution)/shard_map/pallas_call | solution.py:171
  94.0 9.7 %all_to_all.11 = f32[8,8,512]{2,1,0:T(8,128)S(1)} all-to-all(f32[8,8,512]{2,1,0:T(8,128)S(1)} %bitcast.13), channel_id=1, replica_groups=mesh['gx'=4,'gy'=2,'gz'=4] {'gx','gy'}, dimensions={0} | all-to-all | bytes 262144 | tf_op jit(solution)/shard_map/all_to_all | solution.py:341
  103.8 1.3 %shard_map.80 = f32[6,1024]{1,0:T(8,128)} custom-call(f32[64,512]{1,0:T(8,128)S(1)} %bitcast.15, s32[1,1024]{1,0:T(1,128)S(1)} %bitcast.17, s32[1,1024]{1,0:T(1,128)S(1)} %get-tuple-element.18.refs_2_), custom_call_target="tpu_custom_call" | custom-call | flops 201326592 | bytes 102400 | tf_op jit(solution)/shard_map/pallas_call | solution.py:287
  (27 shorter events, 1.7 us)
Async XLA Ops:
  0.0 15.2 %collective-permute-start = (f32[3,16,16,128]{3,2,1,0:T(8,128)}, f32[3,16,16,128]{3,2,1,0:T(8,128)S(1)}, u32[]{:S(2)}, u32[]{:S(2)}) collective-permute-start(f32[3,16,16,128]{3,2,1,0:T(8,128)} %own.1), channel_id=1, source_target_pairs={{0,8},{8,16},{16,24},{24,0},{1,9},{9,17},{17,25},{25,1},{2,10},{10... | collective-permute-start | bytes 1179656 | tf_op jit(solution)/shard_map/ppermute | solution.py:30
  3.0 19.2 %collective-permute-start.5 = (f32[3,16,16,128]{3,2,1,0:T(8,128)}, f32[3,16,16,128]{3,2,1,0:T(8,128)S(1)}, u32[]{:S(2)}, u32[]{:S(2)}) collective-permute-start(f32[3,16,16,128]{3,2,1,0:T(8,128)} %own.1), channel_id=1, source_target_pairs={{8,0},{16,8},{24,16},{0,24},{9,1},{17,9},{25,17},{1,25},{10,2},{18... | collective-permute-start | bytes 1179656 | tf_op jit(solution)/shard_map/ppermute | solution.py:30
  5.1 17.7 %collective-permute-start.4 = (f32[3,16,16,128]{3,2,1,0:T(8,128)}, f32[3,16,16,128]{3,2,1,0:T(8,128)S(1)}, u32[]{:S(2)}, u32[]{:S(2)}) collective-permute-start(f32[3,16,16,128]{3,2,1,0:T(8,128)} %own.1), channel_id=1, source_target_pairs={{1,0},{2,1},{3,2},{0,3},{5,4},{6,5},{7,6},{4,7},{9,8},{10,9},{11,1... | collective-permute-start | bytes 1179656 | tf_op jit(solution)/shard_map/ppermute | solution.py:30
  5.7 17.0 %collective-permute-start.3 = (f32[3,16,16,128]{3,2,1,0:T(8,128)}, f32[3,16,16,128]{3,2,1,0:T(8,128)S(1)}, u32[]{:S(2)}, u32[]{:S(2)}) collective-permute-start(f32[3,16,16,128]{3,2,1,0:T(8,128)} %own.1), channel_id=1, source_target_pairs={{0,1},{1,2},{2,3},{3,0},{4,5},{5,6},{6,7},{7,4},{8,9},{9,10},{10,1... | collective-permute-start | bytes 1179656 | tf_op jit(solution)/shard_map/ppermute | solution.py:30
  15.2 10.8 %collective-permute-start.2 = (f32[3,16,16,128]{3,2,1,0:T(8,128)S(1)}, f32[3,16,16,128]{3,2,1,0:T(8,128)S(1)}, u32[]{:S(2)}, u32[]{:S(2)}) collective-permute-start(f32[3,16,16,128]{3,2,1,0:T(8,128)S(1)} %collective-permute-done.own), channel_id=1, source_target_pairs={{1,0},{2,1},{3,2},{0,3},{5,4},{6,5},{7,6},{4,7},{9,8},{10,9},{11,1... | collective-permute-start | bytes 1179656 | tf_op jit(solution)/shard_map/ppermute | solution.py:30
  15.3 11.4 %collective-permute-start.1 = (f32[3,16,16,128]{3,2,1,0:T(8,128)S(1)}, f32[3,16,16,128]{3,2,1,0:T(8,128)S(1)}, u32[]{:S(2)}, u32[]{:S(2)}) collective-permute-start(f32[3,16,16,128]{3,2,1,0:T(8,128)S(1)} %collective-permute-done.own), channel_id=1, source_target_pairs={{0,1},{1,2},{2,3},{3,0},{4,5},{5,6},{6,7},{7,4},{8,9},{9,10},{10,1... | collective-permute-start | bytes 1179656 | tf_op jit(solution)/shard_map/ppermute | solution.py:30
  22.2 10.1 %collective-permute-start.7 = (f32[3,16,16,128]{3,2,1,0:T(8,128)S(1)}, f32[3,16,16,128]{3,2,1,0:T(8,128)S(1)}, u32[]{:S(2)}, u32[]{:S(2)}) collective-permute-start(f32[3,16,16,128]{3,2,1,0:T(8,128)S(1)} %collective-permute-done.5.own), channel_id=1, source_target_pairs={{1,0},{2,1},{3,2},{0,3},{5,4},{6,5},{7,6},{4,7},{9,8},{10,9},{11,1... | collective-permute-start | bytes 1179656 | tf_op jit(solution)/shard_map/ppermute | solution.py:30
  22.8 12.3 %collective-permute-start.6 = (f32[3,16,16,128]{3,2,1,0:T(8,128)S(1)}, f32[3,16,16,128]{3,2,1,0:T(8,128)S(1)}, u32[]{:S(2)}, u32[]{:S(2)}) collective-permute-start(f32[3,16,16,128]{3,2,1,0:T(8,128)S(1)} %collective-permute-done.5.own), channel_id=1, source_target_pairs={{0,1},{1,2},{2,3},{3,0},{4,5},{5,6},{6,7},{7,4},{8,9},{9,10},{10,1... | collective-permute-start | bytes 1179656 | tf_op jit(solution)/shard_map/ppermute | solution.py:30
  22.8 1.0 copy-start
  51.5 1.1 %copy-start.2 = (f32[9,256,128]{2,1,0:T(8,128)}, f32[9,256,128]{2,1,0:T(8,128)S(1)}, u32[]{:S(2)}) copy-start(f32[9,256,128]{2,1,0:T(8,128)S(1)} %get-tuple-element.12.own) | copy-start | bytes 3538948
  52.6 2.8 %copy-start.7 = (s32[1024]{0:T(1024)S(1)}, s32[1024]{0:T(1024)}, u32[]{:S(2)}) copy-start(s32[1024]{0:T(1024)} %param.10) | copy-start | bytes 12292
  52.6 2.8 %copy-start.8 = (s32[1024]{0:T(1024)S(1)}, s32[1024]{0:T(1024)}, u32[]{:S(2)}) copy-start(s32[1024]{0:T(1024)} %param.9) | copy-start | bytes 12292
  52.6 2.8 %copy-start.9 = (s32[1024]{0:T(1024)S(1)}, s32[1024]{0:T(1024)}, u32[]{:S(2)}) copy-start(s32[1024]{0:T(1024)} %param.11) | copy-start | bytes 12292
  52.6 2.8 %copy-start.4 = (f32[3,1024]{1,0:T(4,128)S(1)}, f32[3,1024]{1,0:T(4,128)}, u32[]{:S(2)}) copy-start(f32[3,1024]{1,0:T(4,128)} %refs_2_.1) | copy-start | bytes 36868
  52.6 2.8 %copy-start.5 = (s32[1024,1]{0,1:T(1,128)S(1)}, s32[1024,1]{0,1:T(1,128)}, u32[]{:S(2)}) copy-start(s32[1024,1]{0,1:T(1,128)} %param.8) | copy-start | bytes 12292
  53.7 27.0 %copy-start.6 = (f32[128,160]{1,0:T(8,128)S(1)}, f32[128,160]{1,0:T(8,128)}, u32[]{:S(2)}) copy-start(f32[128,160]{1,0:T(8,128)} %constant.2.clone.band) | copy-start | bytes 245764
  53.7 25.6 %collective-permute-start.8 = (f32[9,256,32]{1,2,0:T(8,128)}, f32[9,256,32]{1,2,0:T(8,128)}, u32[]{:S(2)}, u32[]{:S(2)}) collective-permute-start(f32[9,256,32]{1,2,0:T(8,128)} %copy.8), channel_id=1, source_target_pairs={{0,4},{4,0},{1,5},{5,1},{2,6},{6,2},{3,7},{7,3},{8,12},{12,8},{9,1... | collective-permute-start | bytes 884744 | tf_op jit(solution)/shard_map/ppermute | solution.py:309
  78.0 1.3 %copy-start.1 = (bf16[256,4096]{1,0:T(8,128)(2,1)}, bf16[256,4096]{1,0:T(8,128)(2,1)S(1)}, u32[]{:S(2)}) copy-start(bf16[256,4096]{1,0:T(8,128)(2,1)S(1)} %get-tuple-element.16.w_low) | copy-start | bytes 6291460
  80.6 1.3 %copy-start.3 = (f32[9,256,128]{2,1,0:T(8,128)S(1)}, f32[9,256,128]{2,1,0:T(8,128)}, u32[]{:S(2)}) copy-start(f32[9,256,128]{2,1,0:T(8,128)} %copy-done.2) | copy-start | bytes 3538948

commit v3 on v2

v3 whole, which is shorter than its diff:
```python
import math

import jax
import jax.numpy as jnp
import numpy as np
from jax import lax
from jax.experimental import pallas as pl
from jax.experimental.pallas import tpu as pltpu
from jax.sharding import PartitionSpec as P

FW = 32
PAIRS = ((0, 0), (0, 1), (0, 2), (1, 1), (1, 2), (2, 2))
ROWS = 8
BLOCK = 256
F32 = jnp.float32
BF16 = jnp.bfloat16
WHOLE = pl.BlockSpec(memory_space=pltpu.VMEM)
PARAMS = pltpu.CompilerParams(vmem_limit_bytes=24 * 1024 * 1024)


def taps():
    radius = FW // 2
    values = [math.exp(-6.0 * (m - radius) ** 2 / FW**2) for m in range(2 * radius + 1)]
    return [v / sum(values) for v in values]


def neighbours(x, axis):
    devices = lax.axis_size(axis)
    up = [(i, (i + 1) % devices) for i in range(devices)]
    down = [(j, i) for i, j in up]
    return lax.ppermute(x, axis, up), lax.ppermute(x, axis, down)


def symmetric(values, centre):
    radius = FW // 2
    g = taps()
    totals = [g[radius] * values[centre]]
    for m in range(1, radius + 1):
        term = g[radius + m] * (values[centre - m] + values[centre + m])
        if m < 4:
            totals.append(term)
        else:
            totals[m % 4] = totals[m % 4] + term
    return (totals[0] + totals[1]) + (totals[2] + totals[3])


def split2(x):
    high = x.astype(BF16)
    return high, (x - high.astype(F32)).astype(BF16)


def split3(x):
    high, rest = x.astype(BF16), None
    rest = x - high.astype(F32)
    middle = rest.astype(BF16)
    return high, middle, (rest - middle.astype(F32)).astype(BF16)


def z_kernel(before, own, after, out, wide):
    layers, size_x = own.shape[1], own.shape[2]
    radius = FW // 2

    for part, (ref, skip) in enumerate(((before, layers - radius), (own, 0), (after, 0))):
        place = (0, radius, radius + layers)[part]

        def products(z, carry, ref=ref, skip=skip, place=place):
            u = [ref[k, z + skip] for k in range(3)]
            for k in range(3):
                wide[k, z + place] = u[k]
            for k, (a, b) in enumerate(PAIRS):
                wide[3 + k, z + place] = u[a] * u[b]
            return carry

        lax.fori_loop(0, layers if part == 1 else radius, products, 0)

    def filtered(f, carry):
        for x in range(0, size_x, 8):
            values = [wide[f, z, x : x + 8] for z in range(layers + 2 * radius)]
            for z in range(layers):
                out[f, z, x : x + 8] = symmetric(values, z + radius)
        return carry

    lax.fori_loop(0, 9, filtered, 0)


def along_z(before, own, after):
    _, z, x, y = own.shape
    return pl.pallas_call(
        z_kernel,
        out_shape=jax.ShapeDtypeStruct((9, z, x, y), F32),
        in_specs=[WHOLE] * 3,
        out_specs=WHOLE,
        scratch_shapes=[pltpu.VMEM((9, z + FW, x, y), F32)],
        compiler_params=PARAMS,
        cost_estimate=pl.CostEstimate(flops=9 * z * x * y * 66, bytes_accessed=21 * z * x * y * 4, transcendentals=0),
    )(before, own, after)


def x_kernel(before, own, after, out, strips, wide):
    layers, size_x, size_y = own.shape[1:]
    radius = FW // 2
    rows = layers * size_x

    def filtered(f, carry):
        for z in range(layers):
            wide[z, 0:radius] = before[f, z, size_x - radius :]
            wide[z, radius : radius + size_x] = own[f, z]
            wide[z, radius + size_x :] = after[f, z, :radius]
        for z in range(layers):
            values = [wide[z, i : i + 8] for i in range(size_x + FW - 7)]
            for x in range(0, size_x, 8):
                out[f, z * size_x + x : z * size_x + x + 8] = symmetric(values, x + radius)
        for n in range(0, rows, 128):
            turned = out[f, n : n + 128].T
            strips[f, :radius, n : n + 128] = turned[:radius]
            strips[f, radius:, n : n + 128] = turned[size_y - radius :]
        return carry

    lax.fori_loop(0, 9, filtered, 0)


def along_x(before, own, after):
    _, z, x, y = own.shape
    return pl.pallas_call(
        x_kernel,
        out_shape=(
            jax.ShapeDtypeStruct((9, z * x, y), F32),
            jax.ShapeDtypeStruct((9, FW, z * x), F32),
        ),
        in_specs=[WHOLE] * 3,
        out_specs=(WHOLE, WHOLE),
        scratch_shapes=[pltpu.VMEM((z, x + FW, y), F32)],
        compiler_params=PARAMS,
        cost_estimate=pl.CostEstimate(flops=9 * z * x * y * 66, bytes_accessed=40 * z * x * y * 4, transcendentals=0),
    )(before, own, after)


def y_kernel(band, fields, asked, out, busy):
    def filtered(f, carry):
        out[f] = lax.dot_general(
            band[...], fields[f], (((1,), (1,)), ((), ())),
            precision=lax.Precision.HIGHEST, preferred_element_type=F32,
        )
        return carry

    lax.fori_loop(0, 9, filtered, 0)
    groups, _, capacity = asked.shape
    for n in range(busy.shape[0]):
        group, start = divmod(n * BLOCK, capacity)
        busy[n] = jnp.max(asked[group, 0:1, start : start + BLOCK]).astype(jnp.int32)


def along_y(band, fields, asked):
    _, cells, size_y = fields.shape
    return pl.pallas_call(
        y_kernel,
        out_shape=(
            jax.ShapeDtypeStruct((9, size_y, cells), F32),
            jax.ShapeDtypeStruct((asked.shape[0] * asked.shape[2] // BLOCK,), jnp.int32),
        ),
        in_specs=[WHOLE] * 3,
        out_specs=(WHOLE, pl.BlockSpec(memory_space=pltpu.SMEM)),
        compiler_params=PARAMS,
        cost_estimate=pl.CostEstimate(flops=9 * 12 * size_y * size_y * cells, bytes_accessed=18 * cells * size_y * 4, transcendentals=0),
    )(band, fields, asked)


def hat(size, row, offset):
    distance = lax.broadcasted_iota(jnp.int32, (size, row.shape[1]), 0) - row
    return jnp.where(distance == 0, 1.0 - offset, jnp.where(distance == 1, offset, 0.0))


def sample_kernel(sizes, busy, partial, strips, band, asked, out, field_high, field_low):
    size_z, size_x, size_y = sizes
    capacity = asked.shape[2]

    def smooth(f):
        return partial[f] + jnp.dot(
            band[...], strips[f], precision=lax.Precision.HIGHEST, preferred_element_type=F32
        )

    mean = [smooth(k) for k in range(3)]
    for k, (a, b) in enumerate(PAIRS):
        high, low = split2(smooth(3 + k) - mean[a] * mean[b])
        field_high[k * size_y : (k + 1) * size_y] = high
        field_low[k * size_y : (k + 1) * size_y] = low

    blocks = capacity // BLOCK

    def sample(n, carry):
        group = n // blocks
        here = pl.ds(pl.multiple_of((n % blocks) * BLOCK, BLOCK), BLOCK)

        @pl.when(busy[n] == 0)
        def _():
            out[group, :, here] = jnp.zeros((ROWS, BLOCK), F32)

        @pl.when(busy[n] != 0)
        def _():
            cell = jnp.maximum(asked[group, 0:1, here].astype(jnp.int32) - 1, 0)
            wx, wy, wz = (asked[group, k : k + 1, here] for k in (1, 2, 3))
            in_z = hat(size_z, cell // (size_x * size_y), wz)
            in_x = hat(size_x, (cell // size_y) % size_x, wx)
            in_y = hat(size_y, cell % size_y, wy)
            high, low = split2(jnp.concatenate([in_z[z : z + 1] * in_x for z in range(size_z)], axis=0))
            wide = jnp.dot(field_high[...], high, preferred_element_type=F32)
            wide = wide + jnp.dot(field_low[...], high, preferred_element_type=F32)
            wide = wide + jnp.dot(field_high[...], low, preferred_element_type=F32)
            for k in range(6):
                part = wide[k * size_y : (k + 1) * size_y] * in_y
                out[group, k : k + 1, here] = jnp.sum(part, axis=0, keepdims=True)
            out[group, 6:ROWS, here] = jnp.zeros((ROWS - 6, BLOCK), F32)

        return carry

    lax.fori_loop(0, busy.shape[0], sample, 0)


def samples(busy, partial, strips, band, asked, sizes):
    _, size_y, cells = partial.shape
    groups, _, capacity = asked.shape

    def kernel(*refs):
        sample_kernel(sizes, *refs)

    return pl.pallas_call(
        kernel,
        out_shape=jax.ShapeDtypeStruct((groups, ROWS, capacity), F32),
        in_specs=[pl.BlockSpec(memory_space=pltpu.SMEM)] + [WHOLE] * 4,
        out_specs=WHOLE,
        scratch_shapes=[pltpu.VMEM((6 * size_y, cells), BF16), pltpu.VMEM((6 * size_y, cells), BF16)],
        compiler_params=PARAMS,
        cost_estimate=pl.CostEstimate(flops=6 * size_y * cells * groups * capacity * 6, bytes_accessed=8 * 1024 * 1024, transcendentals=0),
    )(busy, partial, strips, band, asked)


def route_kernel(sizes, owners, capacity, owner, cell_x, cell_y, cell_z, weights, out, rank_out):
    count = owner.shape[1]
    _, size_x, size_y = sizes
    target = owner[...]
    named = lax.broadcasted_iota(jnp.int32, (owners, count), 0) == target
    earlier = lax.broadcasted_iota(jnp.int32, (count, count), 0) < lax.broadcasted_iota(jnp.int32, (count, count), 1)
    before = jnp.dot(
        jnp.where(named, 1.0, 0.0).astype(BF16), jnp.where(earlier, 1.0, 0.0).astype(BF16),
        preferred_element_type=F32,
    )
    rank = jnp.sum(jnp.where(named, before, 0.0), axis=0, keepdims=True).astype(jnp.int32)
    rank_out[...] = rank
    slot = lax.broadcasted_iota(jnp.int32, (capacity, count), 0) == rank
    slot = jnp.where(slot, 1.0, 0.0).astype(BF16)
    cell = (cell_z[...] * size_x + cell_x[...]) * size_y + cell_y[...] + 1
    record = jnp.concatenate([cell.astype(F32), weights[...], jnp.zeros((4, count), F32)], axis=0)
    total = jnp.zeros((owners * 8, capacity), F32)
    for part in split3(record):
        part = part.astype(F32)
        spread = jnp.concatenate(
            [jnp.where(target == o, part, 0.0) for o in range(owners)], axis=0
        ).astype(BF16)
        total = total + lax.dot_general(spread, slot, (((1,), (1,)), ((), ())), preferred_element_type=F32)
    for o in range(owners):
        out[o] = total[o * 8 : o * 8 + 4]


def route(owner, cell_x, cell_y, cell_z, weights, sizes, owners, capacity):
    count = owner.shape[1]

    def kernel(*refs):
        route_kernel(sizes, owners, capacity, *refs)

    return pl.pallas_call(
        kernel,
        out_shape=(
            jax.ShapeDtypeStruct((owners, 4, capacity), F32),
            jax.ShapeDtypeStruct((1, count), jnp.int32),
        ),
        in_specs=[WHOLE] * 5,
        out_specs=(WHOLE, WHOLE),
        compiler_params=PARAMS,
        cost_estimate=pl.CostEstimate(flops=10 * count * count * owners, bytes_accessed=count * 4 * 40, transcendentals=0),
    )(owner, cell_x, cell_y, cell_z, weights)


def return_kernel(owners, back, owner, rank, out):
    capacity = back.shape[1]
    count = owner.shape[1]
    slot = lax.broadcasted_iota(jnp.int32, (capacity, count), 0) == rank[...]
    slot = jnp.where(slot, 1.0, 0.0).astype(BF16)
    picked = jnp.zeros((owners * ROWS, count), F32)
    for part in split3(back[...]):
        picked = picked + jnp.dot(part, slot, preferred_element_type=F32)
    target = owner[...]
    total = jnp.zeros((ROWS, count), F32)
    for o in range(owners):
        total = total + jnp.where(target == o, picked[o * ROWS : (o + 1) * ROWS], 0.0)
    out[...] = total[:6]


def returned(back, owner, rank, owners):
    count = owner.shape[1]

    def kernel(*refs):
        return_kernel(owners, *refs)

    return pl.pallas_call(
        kernel,
        out_shape=jax.ShapeDtypeStruct((6, count), F32),
        in_specs=[WHOLE] * 3,
        out_specs=WHOLE,
        compiler_params=PARAMS,
        cost_estimate=pl.CostEstimate(flops=6 * owners * ROWS * back.shape[1] * count, bytes_accessed=count * 100, transcendentals=0),
    )(back, owner, rank)


def y_band(size_y):
    radius = FW // 2
    place = np.concatenate([np.arange(size_y + radius), np.arange(-radius, 0)])
    offset = place[None, :] - np.arange(size_y)[:, None] + radius
    g = np.array(taps())
    band = np.where((offset >= 0) & (offset <= FW), g[np.clip(offset, 0, FW)], 0.0)
    return band[:, :size_y].astype(np.float32), band[:, size_y:].astype(np.float32)


def y_strips(edges):
    radius = FW // 2
    devices = lax.axis_size("gy")
    if devices == 2:
        return lax.ppermute(edges, "gy", [(0, 1), (1, 0)])
    up = [(i, (i + 1) % devices) for i in range(devices)]
    down = [(j, i) for i, j in up]
    after = lax.ppermute(edges[:, :radius], "gy", down)
    before = lax.ppermute(edges[:, radius:], "gy", up)
    return jnp.concatenate([after, before], axis=1)


def on_device(velocity, owner, cell_x, cell_y, cell_z, query_weights):
    _, size_z, size_x, size_y = velocity.shape
    owners = lax.axis_size("gx") * lax.axis_size("gy")
    count = owner.shape[0]
    capacity = 4 * count // owners

    sizes = (size_z, size_x, size_y)
    folded = capacity % BLOCK != 0

    left, right = neighbours(velocity, "gx")
    own_halo = neighbours(velocity, "gz")

    target = owner.reshape(1, count)
    sent, rank = route(
        target, cell_x.reshape(1, count), cell_y.reshape(1, count), cell_z.reshape(1, count), query_weights,
        sizes, owners, capacity,
    )
    asked = lax.all_to_all(sent, ("gx", "gy"), split_axis=0, concat_axis=0, tiled=True)
    left, asked = lax.optimization_barrier((left, asked))
    if folded:
        asked = asked.transpose(1, 0, 2).reshape(1, 4, owners * capacity)

    left_halo = neighbours(left, "gz")
    right_halo = neighbours(right, "gz")
    own_z = along_z(own_halo[0], velocity, own_halo[1])
    left_z = along_z(left_halo[0], left, left_halo[1])
    right_z = along_z(right_halo[0], right, right_halo[1])
    fields, edges = along_x(left_z, own_z, right_z)
    band_own, band_strips = y_band(size_y)
    strips = y_strips(edges)
    partial, busy = along_y(jnp.asarray(band_own), fields, asked)
    values = samples(busy, partial, strips, jnp.asarray(band_strips), asked, sizes)
    if folded:
        values = values.reshape(ROWS, owners, capacity).transpose(1, 0, 2)
    back = lax.all_to_all(values, ("gx", "gy"), split_axis=0, concat_axis=0, tiled=True)
    return returned(back.reshape(owners * ROWS, capacity), target, rank, owners)


def solution(mesh):
    placed = (
        P(None, "gz", "gx", "gy"),
        P(("gx", "gy", "gz"), None),
        P(("gx", "gy", "gz")),
        P(("gx", "gy", "gz")),
        P(("gx", "gy", "gz")),
        P(None, ("gx", "gy", "gz")),
    )
    return jax.shard_map(
        on_device,
        mesh=mesh,
        in_specs=placed,
        out_specs=P(None, ("gx", "gy", "gz")),
        check_vma=False,
    )
```

time: 105 us -> 79.4 us (0.76)
  Pallas kernels: 39.6 us -> 22.1 us
  blocking collectives: 27.2 us -> 13.1 us
  starting transfers between devices: 8.48 us -> 13.2 us
  waiting for transfers between devices: 22.7 us -> 25.9 us
  local copies, waits for them, and re-layouts: 7.02 us -> 4.47 us
    all_to_all x1 -> x0, blocking collectives: 17.5 us -> none  [on_device(): lax.all_to_all(sent.reshape(owners, ROWS, capacity), ('gx', 'gy'), split_...]
    pallas_call x1, Pallas kernels: 14.2 us -> 2.82 us  [along_x(): pl.pallas_call(x_kernel, out_shape=(jax.ShapeDtypeStruct((9, z * x, y), F...]
    ppermute x8, waiting for transfers between devices: 22.7 us -> 12 us  [neighbours(): return (lax.ppermute(x, axis, up), lax.ppermute(x, axis, down))]
    all_to_all x0 -> x1, waiting for transfers between devices: none -> 9.7 us  [on_device(): lax.all_to_all(sent, ('gx', 'gy'), split_axis=0, concat_axis=0, tiled=True)]
    pallas_call x3, Pallas kernels: 17.2 us -> 11.2 us  [the longest x1 6.05 us: samples(): pl.pallas_call(kernel, out_shape=jax.ShapeDtypeStruct((groups, ROWS, capa...]
    ppermute x1, waiting for transfers between devices: 0.01 us -> 4.26 us  [y_strips(): return lax.ppermute(edges, 'gy', [(0, 1), (1, 0)])]
    all_to_all x0 -> x1, starting transfers between devices: none -> 3.95 us  [on_device(): lax.all_to_all(sent, ('gx', 'gy'), split_axis=0, concat_axis=0, tiled=True)]
    all_to_all x1, blocking collectives: 9.74 us -> 13.1 us  [on_device(): lax.all_to_all(values, ('gx', 'gy'), split_axis=0, concat_axis=0, tiled=T...]
  transfers between devices with their start and end apart: 9 -> 10, of which waited for: 5 -> 6; matrix products, arithmetic and copies ran while one was open for 0% -> 0% of each run, Pallas kernels for 9% -> 12%
where the time goes in v3:
time: 79.4 us; the launch traced here: 78.9 us
  waiting for transfers between devices  25.9 us (33%)
  Pallas kernels  22.1 us (28%)
  starting transfers between devices  13.2 us (17%)
  blocking collectives  13.1 us (16%)
  local copies, waits for them, and re-layouts  4.47 us (6%)
    all_to_all x1, blocking collectives, on_device(): lax.all_to_all(values, ('gx', 'gy'), split_axis=0, concat_axis=0, tiled=T...  13.1 us
    ppermute x8, waiting for transfers between devices, neighbours(): return (lax.ppermute(x, axis, up), lax.ppermute(x, axis, down))  12 us
    all_to_all x1, waiting for transfers between devices, on_device(): lax.all_to_all(sent, ('gx', 'gy'), split_axis=0, concat_axis=0, tiled=True)  9.7 us
    ppermute x8, starting transfers between devices, neighbours(): return (lax.ppermute(x, axis, up), lax.ppermute(x, axis, down))  8.09 us
    pallas_call x3, Pallas kernels, along_z(): pl.pallas_call(z_kernel, out_shape=jax.ShapeDtypeStruct((9, z, x, y), F32...  6.82 us
    pallas_call x1, Pallas kernels, samples(): pl.pallas_call(kernel, out_shape=jax.ShapeDtypeStruct((groups, ROWS, capa...  6.05 us
    unnamed x18, local copies, waits for them, and re-layouts  4.47 us
    ppermute x1, waiting for transfers between devices, y_strips(): return lax.ppermute(edges, 'gy', [(0, 1), (1, 0)])  4.26 us
  transfers between devices with their start and end apart: 10, of which 6 were waited for; matrix products, arithmetic and copies ran while one was open for 0% of the time, Pallas kernels for 12%

profile of v3, /device:TPU:0, one launch (start us, length us, event | category | flops | bytes accessed | tf_op | source)
XLA Modules:
  0.0 78.9 jit_solution(16480440050540712778)
XLA Ops:
  0.0 3.0 %collective-permute-start = (f32[3,16,16,128]{3,2,1,0:T(8,128)}, f32[3,16,16,128]{3,2,1,0:T(8,128)S(1)}, u32[]{:S(2)}, u32[]{:S(2)}) collective-permute-start(f32[3,16,16,128]{3,2,1,0:T(8,128)} %own.1), channel_id=1, source_target_pairs={{0,8},{8,16},{16,24},{24,0},{1,9},{9,17},{17,25},{25,1},{2,10},{10... | collective-permute-start | bytes 1179656 | tf_op jit(solution)/shard_map/ppermute | solution.py:31
  3.0 2.0 %collective-permute-start.5 = (f32[3,16,16,128]{3,2,1,0:T(8,128)}, f32[3,16,16,128]{3,2,1,0:T(8,128)S(1)}, u32[]{:S(2)}, u32[]{:S(2)}) collective-permute-start(f32[3,16,16,128]{3,2,1,0:T(8,128)} %own.1), channel_id=1, source_target_pairs={{8,0},{16,8},{24,16},{0,24},{9,1},{17,9},{25,17},{1,25},{10,2},{18... | collective-permute-start | bytes 1179656 | tf_op jit(solution)/shard_map/ppermute | solution.py:31
  5.7 0.7 copy-done.1
  6.5 0.7 copy-done.2
  7.1 0.7 copy-done.3
  9.2 1.9 %shard_map.82 = (f32[8,4,512]{2,1,0:T(4,128)}, s32[1,1024]{1,0:T(1,128)S(1)}) custom-call(s32[1,1024]{1,0:T(1,128)S(1)} %bitcast.9, s32[1,1024]{1,0:T(1,128)S(1)} %bitcast.6, s32[1,1024]{1,0:T(1,128)S(1)} %bitcast.7, s32[1,1024]{1,0:T(1,128)S(1)} %bitcast.8, f32[3,1024]{1,0:T(4,128)S(1)} %copy-done.1), custom_call_target="tpu_custom_call" | custom-call | flops 83886080 | bytes 163840 | tf_op jit(solution)/shard_map/pallas_call | solution.py:270
  11.1 3.9 %all-to-all-start = ((f32[8,4,512]{2,1,0:T(4,128)}), f32[8,4,512]{2,1,0:T(4,128)S(1)}, u32[]{:S(2)}, u32[]{:S(2)}) async-start(f32[8,4,512]{2,1,0:T(4,128)} %get-tuple-element.13), calls=%async_computation | async-start | bytes 131072 | tf_op jit(solution)/shard_map/all_to_all | solution.py:352
  15.0 9.7 %all-to-all-done.asked.refs_4_ = f32[8,4,512]{2,1,0:T(4,128)S(1)} async-done(((f32[8,4,512]{2,1,0:T(4,128)}), f32[8,4,512]{2,1,0:T(4,128)S(1)}, u32[]{:S(2)}, u32[]{:S(2)}) %all-to-all-start) | async-done | bytes 65568 | tf_op jit(solution)/shard_map/all_to_all | solution.py:352
  25.4 1.7 %collective-permute-start.7 = (f32[3,16,16,128]{3,2,1,0:T(8,128)S(1)}, f32[3,16,16,128]{3,2,1,0:T(8,128)S(1)}, u32[]{:S(2)}, u32[]{:S(2)}) collective-permute-start(f32[3,16,16,128]{3,2,1,0:T(8,128)S(1)} %collective-permute-done.5.own), channel_id=1, source_target_pairs={{1,0},{2,1},{3,2},{0,3},{5,4},{6,5},{7,6},{4,7},{9,8},{10,9},{11,1... | collective-permute-start | bytes 1179656 | tf_op jit(solution)/shard_map/ppermute | solution.py:31
  27.1 1.0 %copy-done = f32[3,16,16,128]{3,2,1,0:T(8,128)S(1)} copy-done((f32[3,16,16,128]{3,2,1,0:T(8,128)S(1)}, f32[3,16,16,128]{3,2,1,0:T(8,128)}, u32[]{:S(2)}) %copy-start) | copy-done | bytes 393240
  28.1 2.3 %shard_map.84.own = f32[9,16,16,128]{3,2,1,0:T(8,128)S(1)} custom-call(f32[3,16,16,128]{3,2,1,0:T(8,128)S(1)} %collective-permute-done.3.before, f32[3,16,16,128]{3,2,1,0:T(8,128)S(1)} %copy-done, f32[3,16,16,128]{3,2,1,0:T(8,128)S(1)} %collective-permute-done.4.after), custom_call_target="tpu_custom_call" | custom-call | flops 19464192 | bytes 2752512 | tf_op jit(solution)/shard_map/pallas_call | solution.py:88
  30.4 4.1 %collective-permute-done.2.after = f32[3,16,16,128]{3,2,1,0:T(8,128)S(1)} collective-permute-done((f32[3,16,16,128]{3,2,1,0:T(8,128)S(1)}, f32[3,16,16,128]{3,2,1,0:T(8,128)S(1)}, u32[]{:S(2)}, u32[]{:S(2)}) %collective-permute-start.2) | collective-permute-done | bytes 393248 | tf_op jit(solution)/shard_map/ppermute | solution.py:31
  34.5 2.2 %collective-permute-done.1.before = f32[3,16,16,128]{3,2,1,0:T(8,128)S(1)} collective-permute-done((f32[3,16,16,128]{3,2,1,0:T(8,128)S(1)}, f32[3,16,16,128]{3,2,1,0:T(8,128)S(1)}, u32[]{:S(2)}, u32[]{:S(2)}) %collective-permute-start.1) | collective-permute-done | bytes 393248 | tf_op jit(solution)/shard_map/ppermute | solution.py:31
  36.7 2.3 %shard_map.83.before = f32[9,16,16,128]{3,2,1,0:T(8,128)S(1)} custom-call(f32[3,16,16,128]{3,2,1,0:T(8,128)S(1)} %collective-permute-done.1.before, f32[3,16,16,128]{3,2,1,0:T(8,128)S(1)} %collective-permute-done.own, f32[3,16,16,128]{3,2,1,0:T(8,128)S(1)} %collective-permute-done.2.after), custom_call_target="tpu_custom_call" | custom-call | flops 19464192 | bytes 2752512 | tf_op jit(solution)/shard_map/pallas_call | solution.py:88
  39.0 4.0 %collective-permute-done.7.after = f32[3,16,16,128]{3,2,1,0:T(8,128)S(1)} collective-permute-done((f32[3,16,16,128]{3,2,1,0:T(8,128)S(1)}, f32[3,16,16,128]{3,2,1,0:T(8,128)S(1)}, u32[]{:S(2)}, u32[]{:S(2)}) %collective-permute-start.7) | collective-permute-done | bytes 393248 | tf_op jit(solution)/shard_map/ppermute | solution.py:31
  42.9 1.7 %collective-permute-done.6.before = f32[3,16,16,128]{3,2,1,0:T(8,128)S(1)} collective-permute-done((f32[3,16,16,128]{3,2,1,0:T(8,128)S(1)}, f32[3,16,16,128]{3,2,1,0:T(8,128)S(1)}, u32[]{:S(2)}, u32[]{:S(2)}) %collective-permute-start.6) | collective-permute-done | bytes 393248 | tf_op jit(solution)/shard_map/ppermute | solution.py:31
  44.7 2.3 %shard_map.85.after = f32[9,16,16,128]{3,2,1,0:T(8,128)S(1)} custom-call(f32[3,16,16,128]{3,2,1,0:T(8,128)S(1)} %collective-permute-done.6.before, f32[3,16,16,128]{3,2,1,0:T(8,128)S(1)} %collective-permute-done.5.own, f32[3,16,16,128]{3,2,1,0:T(8,128)S(1)} %collective-permute-done.7.after), custom_call_target="tpu_custom_call" | custom-call | flops 19464192 | bytes 2752512 | tf_op jit(solution)/shard_map/pallas_call | solution.py:88
  46.9 2.8 %shard_map.86 = (f32[9,256,128]{2,1,0:T(8,128)S(1)}, f32[9,32,256]{2,1,0:T(8,128)S(1)}) custom-call(f32[9,16,16,128]{3,2,1,0:T(8,128)S(1)} %shard_map.83.before, f32[9,16,16,128]{3,2,1,0:T(8,128)S(1)} %shard_map.84.own, f32[9,16,16,128]{3,2,1,0:T(8,128)S(1)} %shard_map.85.after), custom_call_target="tpu_custom_call" | custom-call | flops 19464192 | bytes 5242880 | tf_op jit(solution)/shard_map/pallas_call | solution.py:124
  49.8 1.1 %collective-permute-start.8 = (f32[9,32,256]{2,1,0:T(8,128)S(1)}, f32[9,32,256]{2,1,0:T(8,128)S(1)}, u32[]{:S(2)}, u32[]{:S(2)}) collective-permute-start(f32[9,32,256]{2,1,0:T(8,128)S(1)} %get-tuple-element.19), channel_id=1, source_target_pairs={{0,4},{4,0},{1,5},{5,1},{2,6},{6,2},{3,7},{7,3},{8,12},{12,8},{9,1... | collective-permute-start | bytes 884744 | tf_op jit(solution)/shard_map/ppermute | solution.py:327
  50.9 3.2 %shard_map.87 = (f32[9,128,256]{2,1,0:T(8,128)S(1)}, s32[16]{0:T(128)S(1)}) custom-call(f32[128,128]{1,0:T(8,128)S(1)} %copy-done.8, f32[9,256,128]{2,1,0:T(8,128)S(1)} %get-tuple-element.15.fields, f32[8,4,512]{2,1,0:T(4,128)S(1)} %all-to-all-done.asked.refs_4_), custom_call_target="tpu_custom_call" | custom-call | flops 452984832 | bytes 2359296 | tf_op jit(solution)/shard_map/pallas_call | solution.py:155
  54.2 4.3 %collective-permute-done.8.refs_2_ = f32[9,32,256]{2,1,0:T(8,128)S(1)} collective-permute-done((f32[9,32,256]{2,1,0:T(8,128)S(1)}, f32[9,32,256]{2,1,0:T(8,128)S(1)}, u32[]{:S(2)}, u32[]{:S(2)}) %collective-permute-start.8) | collective-permute-done | bytes 294944 | tf_op jit(solution)/shard_map/ppermute | solution.py:327
  58.4 6.0 %shard_map.88 = f32[8,8,512]{2,1,0:T(8,128)S(1)} custom-call(s32[16]{0:T(128)S(1)} %get-tuple-element.17.refs_0_, f32[9,128,256]{2,1,0:T(8,128)S(1)} %get-tuple-element.18.refs_1_, f32[9,32,256]{2,1,0:T(8,128)S(1)} %collective-permute-done.8.refs_2_, f32[128,32]{1,0:T(8,128)S(1)} %copy-done.7, f32[8,4,512]{2,1,0:T(4,128)S(1)} %all-to-all-done.asked.refs_4_), custom_call_target="tpu_custom_call" | custom-call | flops 4831838208 | bytes 8388608 | tf_op jit(solution)/shard_map/pallas_call | solution.py:226
  64.5 13.1 %all_to_all.10 = f32[8,8,512]{2,1,0:T(8,128)S(1)} all-to-all(f32[8,8,512]{2,1,0:T(8,128)S(1)} %shard_map.88), channel_id=1, replica_groups=mesh['gx'=4,'gy'=2,'gz'=4] {'gx','gy'}, dimensions={0} | all-to-all | bytes 262144 | tf_op jit(solution)/shard_map/all_to_all | solution.py:369
  77.5 1.3 %shard_map.89 = f32[6,1024]{1,0:T(8,128)} custom-call(f32[64,512]{1,0:T(8,128)S(1)} %bitcast.5, s32[1,1024]{1,0:T(1,128)S(1)} %bitcast.10, s32[1,1024]{1,0:T(1,128)S(1)} %get-tuple-element.20.refs_2_), custom_call_target="tpu_custom_call" | custom-call | flops 201326592 | bytes 102400 | tf_op jit(solution)/shard_map/pallas_call | solution.py:304
  (23 shorter events, 2.7 us)
Async XLA Ops:
  0.0 24.7 %collective-permute-start = (f32[3,16,16,128]{3,2,1,0:T(8,128)}, f32[3,16,16,128]{3,2,1,0:T(8,128)S(1)}, u32[]{:S(2)}, u32[]{:S(2)}) collective-permute-start(f32[3,16,16,128]{3,2,1,0:T(8,128)} %own.1), channel_id=1, source_target_pairs={{0,8},{8,16},{16,24},{24,0},{1,9},{9,17},{17,25},{25,1},{2,10},{10... | collective-permute-start | bytes 1179656 | tf_op jit(solution)/shard_map/ppermute | solution.py:31
  3.0 22.3 %collective-permute-start.5 = (f32[3,16,16,128]{3,2,1,0:T(8,128)}, f32[3,16,16,128]{3,2,1,0:T(8,128)S(1)}, u32[]{:S(2)}, u32[]{:S(2)}) collective-permute-start(f32[3,16,16,128]{3,2,1,0:T(8,128)} %own.1), channel_id=1, source_target_pairs={{8,0},{16,8},{24,16},{0,24},{9,1},{17,9},{25,17},{1,25},{10,2},{18... | collective-permute-start | bytes 1179656 | tf_op jit(solution)/shard_map/ppermute | solution.py:31
  5.1 22.0 %collective-permute-start.4 = (f32[3,16,16,128]{3,2,1,0:T(8,128)}, f32[3,16,16,128]{3,2,1,0:T(8,128)S(1)}, u32[]{:S(2)}, u32[]{:S(2)}) collective-permute-start(f32[3,16,16,128]{3,2,1,0:T(8,128)} %own.1), channel_id=1, source_target_pairs={{1,0},{2,1},{3,2},{0,3},{5,4},{6,5},{7,6},{4,7},{9,8},{10,9},{11,1... | collective-permute-start | bytes 1179656 | tf_op jit(solution)/shard_map/ppermute | solution.py:31
  5.7 0.7 copy-start.1
  6.5 0.7 copy-start.2
  7.1 0.7 copy-start.3
  7.8 0.7 copy-start.4
  8.5 0.7 copy-start.5
  11.1 13.7 %all-to-all-start = ((f32[8,4,512]{2,1,0:T(4,128)}), f32[8,4,512]{2,1,0:T(4,128)S(1)}, u32[]{:S(2)}, u32[]{:S(2)}) async-start(f32[8,4,512]{2,1,0:T(4,128)} %get-tuple-element.13), calls=%async_computation | async-start | bytes 131072 | tf_op jit(solution)/shard_map/all_to_all | solution.py:352
  15.0 12.1 %collective-permute-start.3 = (f32[3,16,16,128]{3,2,1,0:T(8,128)}, f32[3,16,16,128]{3,2,1,0:T(8,128)S(1)}, u32[]{:S(2)}, u32[]{:S(2)}) collective-permute-start(f32[3,16,16,128]{3,2,1,0:T(8,128)} %own.1), channel_id=1, source_target_pairs={{0,1},{1,2},{2,3},{3,0},{4,5},{5,6},{6,7},{7,4},{8,9},{9,10},{10,1... | collective-permute-start | bytes 1179656 | tf_op jit(solution)/shard_map/ppermute | solution.py:31
  24.7 9.8 %collective-permute-start.2 = (f32[3,16,16,128]{3,2,1,0:T(8,128)S(1)}, f32[3,16,16,128]{3,2,1,0:T(8,128)S(1)}, u32[]{:S(2)}, u32[]{:S(2)}) collective-permute-start(f32[3,16,16,128]{3,2,1,0:T(8,128)S(1)} %collective-permute-done.own), channel_id=1, source_target_pairs={{1,0},{2,1},{3,2},{0,3},{5,4},{6,5},{7,6},{4,7},{9,8},{10,9},{11,1... | collective-permute-start | bytes 1179656 | tf_op jit(solution)/shard_map/ppermute | solution.py:31
  25.3 11.3 %collective-permute-start.1 = (f32[3,16,16,128]{3,2,1,0:T(8,128)S(1)}, f32[3,16,16,128]{3,2,1,0:T(8,128)S(1)}, u32[]{:S(2)}, u32[]{:S(2)}) collective-permute-start(f32[3,16,16,128]{3,2,1,0:T(8,128)S(1)} %collective-permute-done.own), channel_id=1, source_target_pairs={{0,1},{1,2},{2,3},{3,0},{4,5},{5,6},{6,7},{7,4},{8,9},{9,10},{10,1... | collective-permute-start | bytes 1179656 | tf_op jit(solution)/shard_map/ppermute | solution.py:31
  25.4 17.6 %collective-permute-start.7 = (f32[3,16,16,128]{3,2,1,0:T(8,128)S(1)}, f32[3,16,16,128]{3,2,1,0:T(8,128)S(1)}, u32[]{:S(2)}, u32[]{:S(2)}) collective-permute-start(f32[3,16,16,128]{3,2,1,0:T(8,128)S(1)} %collective-permute-done.5.own), channel_id=1, source_target_pairs={{1,0},{2,1},{3,2},{0,3},{5,4},{6,5},{7,6},{4,7},{9,8},{10,9},{11,1... | collective-permute-start | bytes 1179656 | tf_op jit(solution)/shard_map/ppermute | solution.py:31
  27.1 17.6 %collective-permute-start.6 = (f32[3,16,16,128]{3,2,1,0:T(8,128)S(1)}, f32[3,16,16,128]{3,2,1,0:T(8,128)S(1)}, u32[]{:S(2)}, u32[]{:S(2)}) collective-permute-start(f32[3,16,16,128]{3,2,1,0:T(8,128)S(1)} %collective-permute-done.5.own), channel_id=1, source_target_pairs={{0,1},{1,2},{2,3},{3,0},{4,5},{5,6},{6,7},{7,4},{8,9},{9,10},{10,1... | collective-permute-start | bytes 1179656 | tf_op jit(solution)/shard_map/ppermute | solution.py:31
  27.1 1.0 %copy-start = (f32[3,16,16,128]{3,2,1,0:T(8,128)S(1)}, f32[3,16,16,128]{3,2,1,0:T(8,128)}, u32[]{:S(2)}) copy-start(f32[3,16,16,128]{3,2,1,0:T(8,128)} %own.1) | copy-start | bytes 1179652
  46.9 4.0 %copy-start.8 = (f32[128,128]{1,0:T(8,128)S(1)}, f32[128,128]{1,0:T(8,128)}, u32[]{:S(2)}) copy-start(f32[128,128]{1,0:T(8,128)} %constant.4.clone.band) | copy-start | bytes 196612
  49.8 8.6 %copy-start.7 = (f32[128,32]{1,0:T(8,128)S(1)}, f32[128,32]{1,0:T(8,128)}, u32[]{:S(2)}) copy-start(f32[128,32]{1,0:T(8,128)} %constant.5.clone.refs_3_) | copy-start | bytes 49156
  49.8 8.6 %collective-permute-start.8 = (f32[9,32,256]{2,1,0:T(8,128)S(1)}, f32[9,32,256]{2,1,0:T(8,128)S(1)}, u32[]{:S(2)}, u32[]{:S(2)}) collective-permute-start(f32[9,32,256]{2,1,0:T(8,128)S(1)} %get-tuple-element.19), channel_id=1, source_target_pairs={{0,4},{4,0},{1,5},{5,1},{2,6},{6,2},{3,7},{7,3},{8,12},{12,8},{9,1... | collective-permute-start | bytes 884744 | tf_op jit(solution)/shard_map/ppermute | solution.py:327
  58.4 19.1 %copy-start.6 = (s32[1024,1]{0,1:T(1,128)S(1)}, s32[1024,1]{0,1:T(1,128)}, u32[]{:S(2)}) copy-start(s32[1024,1]{0,1:T(1,128)} %param.9) | copy-start | bytes 12292

commit v4 on v3

v4 whole, which is shorter than its diff:
```python
import math

import jax
import jax.numpy as jnp
import numpy as np
from jax import lax
from jax.experimental import pallas as pl
from jax.experimental.pallas import tpu as pltpu
from jax.sharding import PartitionSpec as P

FW = 32
PAIRS = ((0, 0), (0, 1), (0, 2), (1, 1), (1, 2), (2, 2))
ROWS = 8
BLOCK = 256
F32 = jnp.float32
BF16 = jnp.bfloat16
WHOLE = pl.BlockSpec(memory_space=pltpu.VMEM)
PARAMS = pltpu.CompilerParams(vmem_limit_bytes=24 * 1024 * 1024)


def taps():
    radius = FW // 2
    values = [math.exp(-6.0 * (m - radius) ** 2 / FW**2) for m in range(2 * radius + 1)]
    return [v / sum(values) for v in values]


def shifted(x, axis, step):
    devices = lax.axis_size(axis)
    return lax.ppermute(x, axis, [(i, (i + step) % devices) for i in range(devices)])


def neighbours(x, axis):
    return shifted(x, axis, 1), shifted(x, axis, -1)


def after(x, *others):
    return lax.optimization_barrier((x, others))[0]


def relayed(brick):
    previous, following = neighbours(brick, "gz")
    return previous, brick, following


def symmetric(values, centre):
    radius = FW // 2
    g = taps()
    totals = [g[radius] * values[centre]]
    for m in range(1, radius + 1):
        term = g[radius + m] * (values[centre - m] + values[centre + m])
        if m < 4:
            totals.append(term)
        else:
            totals[m % 4] = totals[m % 4] + term
    return (totals[0] + totals[1]) + (totals[2] + totals[3])


def split2(x):
    high = x.astype(BF16)
    return high, (x - high.astype(F32)).astype(BF16)


def split3(x):
    high, rest = x.astype(BF16), None
    rest = x - high.astype(F32)
    middle = rest.astype(BF16)
    return high, middle, (rest - middle.astype(F32)).astype(BF16)


def form_products(before, own, after, wide):
    layers = own.shape[1]
    radius = FW // 2
    for part, (ref, skip) in enumerate(((before, layers - radius), (own, 0), (after, 0))):
        place = (0, radius, radius + layers)[part]

        def products(z, carry, ref=ref, skip=skip, place=place):
            u = [ref[k, z + skip] for k in range(3)]
            for k in range(3):
                wide[k, z + place] = u[k]
            for k, (a, b) in enumerate(PAIRS):
                wide[3 + k, z + place] = u[a] * u[b]
            return carry

        lax.fori_loop(0, layers if part == 1 else radius, products, 0, unroll=4)


def z_kernel(before, own, after, out, wide):
    layers, size_x = own.shape[1], own.shape[2]
    radius = FW // 2
    form_products(before, own, after, wide)

    def filtered(f, carry):
        for x in range(0, size_x, 8):
            values = [wide[f, z, x : x + 8] for z in range(layers + 2 * radius)]
            for z in range(layers):
                out[f, z, x : x + 8] = symmetric(values, z + radius)
        return carry

    lax.fori_loop(0, 9, filtered, 0)


def along_z(before, own, after):
    _, z, x, y = own.shape
    return pl.pallas_call(
        z_kernel,
        out_shape=jax.ShapeDtypeStruct((9, z, x, y), F32),
        in_specs=[WHOLE] * 3,
        out_specs=WHOLE,
        scratch_shapes=[pltpu.VMEM((9, z + FW, x, y), F32)],
        compiler_params=PARAMS,
        cost_estimate=pl.CostEstimate(flops=9 * z * x * y * 66, bytes_accessed=21 * z * x * y * 4, transcendentals=0),
    )(before, own, after)


def near_kernel(before, own, after, out, wide):
    layers, size_x = own.shape[1:3]
    half = before.shape[2]
    empty = jnp.zeros((size_x - half, own.shape[3]), F32)
    for z in range(layers):
        wide[z, : size_x - half] = empty
        wide[z, 2 * size_x + half :] = empty

    def filtered(f, carry):
        for z in range(layers):
            wide[z, size_x - half : size_x] = before[f, z]
            wide[z, size_x : 2 * size_x] = own[f, z]
            wide[z, 2 * size_x : 2 * size_x + half] = after[f, z]
        for z in range(layers):
            values = [wide[z, i : i + 8] for i in range(3 * size_x - 7)]
            for x in range(0, size_x, 8):
                out[f, z * size_x + x : z * size_x + x + 8] = symmetric(values, x + size_x)
        return carry

    lax.fori_loop(0, 9, filtered, 0)


def along_x_near(before, own, after):
    _, z, x, y = own.shape
    return pl.pallas_call(
        near_kernel,
        out_shape=jax.ShapeDtypeStruct((9, z * x, y), F32),
        in_specs=[WHOLE] * 3,
        out_specs=WHOLE,
        scratch_shapes=[pltpu.VMEM((z, 3 * x, y), F32)],
        compiler_params=PARAMS,
        cost_estimate=pl.CostEstimate(flops=9 * z * x * y * 66, bytes_accessed=30 * z * x * y * 4, transcendentals=0),
    )(before, own, after)


def far_kernel(leading, last, before, own, after, near, out, *rest):
    strips = rest[0] if last else None
    wide, padded = rest[-2:]
    layers, half, size_y = own.shape[1:]
    radius = FW // 2
    size_x = near.shape[1] // layers
    g = taps()
    form_products(before, own, after, wide)
    empty = jnp.zeros((half, size_y), F32)
    for z in range(layers):
        if leading:
            padded[z, half:] = empty
        else:
            padded[z, :half] = empty

    def filtered(f, carry):
        values = [wide[f, z] for z in range(layers + 2 * radius)]
        for z in range(layers):
            if leading:
                padded[z, :half] = symmetric(values, z + radius)
            else:
                padded[z, half:] = symmetric(values, z + radius)
        for z in range(layers):
            start = z * size_x
            if leading:
                added = [g[k] * padded[z, k : k + half] for k in range(half)]
            else:
                added = [g[2 * radius - k] * padded[z, half - k : 2 * half - k] for k in range(half)]
                start = start + half
            while len(added) > 1:
                added = [p + q for p, q in zip(added[::2], added[1::2])] + added[len(added) // 2 * 2 :]
            other = z * size_x + (half if leading else 0)
            out[f, start : start + half] = near[f, start : start + half] + added[0]
            out[f, other : other + half] = near[f, other : other + half]
        if last:
            for n in range(0, layers * size_x, 128):
                turned = out[f, n : n + 128].T
                strips[f, :radius, n : n + 128] = turned[:radius]
                strips[f, radius:, n : n + 128] = turned[size_y - radius :]
        return carry

    lax.fori_loop(0, 9, filtered, 0)


def along_x_far(leading, last, before, own, after, near):
    _, z, half, y = own.shape
    cells = near.shape[1]

    def kernel(*refs):
        far_kernel(leading, last, *refs)

    out_shape = jax.ShapeDtypeStruct((9, cells, y), F32)
    out_spec = WHOLE
    if last:
        out_shape = (out_shape, jax.ShapeDtypeStruct((9, FW, cells), F32))
        out_spec = (WHOLE, WHOLE)
    return pl.pallas_call(
        kernel,
        out_shape=out_shape,
        in_specs=[WHOLE] * 4,
        out_specs=out_spec,
        scratch_shapes=[pltpu.VMEM((9, z + FW, half, y), F32), pltpu.VMEM((z, 2 * half, y), F32)],
        compiler_params=PARAMS,
        cost_estimate=pl.CostEstimate(flops=9 * z * half * y * 90, bytes_accessed=40 * z * half * y * 4, transcendentals=0),
    )(before, own, after, near)


def hat(size, row, offset):
    distance = lax.broadcasted_iota(jnp.int32, (size, row.shape[1]), 0) - row
    return jnp.where(distance == 0, 1.0 - offset, jnp.where(distance == 1, offset, 0.0))


def y_kernel(sizes, band, fields, asked, out, w_high, w_low, w_y):
    size_z, size_x, size_y = sizes

    def filtered(f, carry):
        out[f] = lax.dot_general(
            band[...], fields[f], (((1,), (1,)), ((), ())),
            precision=lax.Precision.HIGHEST, preferred_element_type=F32,
        )
        return carry

    lax.fori_loop(0, 9, filtered, 0)
    blocks = asked.shape[2] // BLOCK

    def weights(n, carry):
        group = n // blocks
        here = pl.ds(pl.multiple_of((n % blocks) * BLOCK, BLOCK), BLOCK)
        there = pl.ds(pl.multiple_of(n * BLOCK, BLOCK), BLOCK)
        cell = asked[group, 0:1, here].astype(jnp.int32)
        wx, wy, wz = (asked[group, k : k + 1, here] for k in (1, 2, 3))
        in_z = hat(size_z, cell // (size_x * size_y), wz)
        in_x = hat(size_x, (cell // size_y) % size_x, wx)
        w_y[:, there] = hat(size_y, cell % size_y, wy)
        for z in range(size_z):
            high, low = split2(in_z[z : z + 1] * in_x)
            w_high[z * size_x : (z + 1) * size_x, there] = high
            w_low[z * size_x : (z + 1) * size_x, there] = low
        return carry

    lax.fori_loop(0, asked.shape[0] * blocks, weights, 0)


def along_y(band, fields, asked, sizes):
    _, cells, size_y = fields.shape
    count = asked.shape[0] * asked.shape[2]

    def kernel(*refs):
        y_kernel(sizes, *refs)

    return pl.pallas_call(
        kernel,
        out_shape=(
            jax.ShapeDtypeStruct((9, size_y, cells), F32),
            jax.ShapeDtypeStruct((cells, count), BF16),
            jax.ShapeDtypeStruct((cells, count), BF16),
            jax.ShapeDtypeStruct((size_y, count), F32),
        ),
        in_specs=[WHOLE] * 3,
        out_specs=(WHOLE,) * 4,
        compiler_params=PARAMS,
        cost_estimate=pl.CostEstimate(flops=9 * 12 * size_y * size_y * cells, bytes_accessed=18 * cells * size_y * 4, transcendentals=0),
    )(band, fields, asked)


def sample_kernel(partial, strips, band, w_high, w_low, w_y, out, field_high, field_low):
    size_y = partial.shape[1]
    blocks = out.shape[2] // BLOCK

    def smooth(f):
        return partial[f] + jnp.dot(
            band[...], strips[f], precision=lax.Precision.HIGHEST, preferred_element_type=F32
        )

    mean = [smooth(k) for k in range(3)]
    for k, (a, b) in enumerate(PAIRS):
        high, low = split2(smooth(3 + k) - mean[a] * mean[b])
        field_high[k * size_y : (k + 1) * size_y] = high
        field_low[k * size_y : (k + 1) * size_y] = low

    def sample(n, carry):
        group = n // blocks
        here = pl.ds(pl.multiple_of((n % blocks) * BLOCK, BLOCK), BLOCK)
        there = pl.ds(pl.multiple_of(n * BLOCK, BLOCK), BLOCK)
        high = w_high[:, there]
        wide = jnp.dot(field_high[...], high, preferred_element_type=F32)
        wide = wide + jnp.dot(field_low[...], high, preferred_element_type=F32)
        wide = wide + jnp.dot(field_high[...], w_low[:, there], preferred_element_type=F32)
        in_y = w_y[:, there]
        for k in range(6):
            part = wide[k * size_y : (k + 1) * size_y] * in_y
            out[group, k : k + 1, here] = jnp.sum(part, axis=0, keepdims=True)
        out[group, 6:ROWS, here] = jnp.zeros((ROWS - 6, BLOCK), F32)
        return carry

    lax.fori_loop(0, out.shape[0] * blocks, sample, 0, unroll=4)


def samples(partial, strips, band, w_high, w_low, w_y, groups):
    _, size_y, cells = partial.shape
    count = w_y.shape[1]
    return pl.pallas_call(
        sample_kernel,
        out_shape=jax.ShapeDtypeStruct((groups, ROWS, count // groups), F32),
        in_specs=[WHOLE] * 6,
        out_specs=WHOLE,
        scratch_shapes=[pltpu.VMEM((6 * size_y, cells), BF16), pltpu.VMEM((6 * size_y, cells), BF16)],
        compiler_params=PARAMS,
        cost_estimate=pl.CostEstimate(flops=6 * size_y * cells * count * 6, bytes_accessed=8 * 1024 * 1024, transcendentals=0),
    )(partial, strips, band, w_high, w_low, w_y)


def route_kernel(owners, capacity, record, owner, out, rank_out):
    count = record.shape[1]
    target = owner[...]
    named = lax.broadcasted_iota(jnp.int32, (owners, count), 0) == target
    earlier = lax.broadcasted_iota(jnp.int32, (count, count), 0) < lax.broadcasted_iota(jnp.int32, (count, count), 1)
    before = jnp.dot(
        jnp.where(named, 1.0, 0.0).astype(BF16), jnp.where(earlier, 1.0, 0.0).astype(BF16),
        preferred_element_type=F32,
    )
    rank = jnp.sum(jnp.where(named, before, 0.0), axis=0, keepdims=True).astype(jnp.int32)
    rank_out[...] = rank
    slot = lax.broadcasted_iota(jnp.int32, (capacity, count), 0) == rank
    slot = jnp.where(slot, 1.0, 0.0).astype(BF16)
    values = jnp.concatenate([record[...], jnp.zeros((4, count), F32)], axis=0)
    total = jnp.zeros((owners * 8, capacity), F32)
    for part in split3(values):
        part = part.astype(F32)
        spread = jnp.concatenate(
            [jnp.where(target == o, part, 0.0) for o in range(owners)], axis=0
        ).astype(BF16)
        total = total + lax.dot_general(spread, slot, (((1,), (1,)), ((), ())), preferred_element_type=F32)
    for o in range(owners):
        out[o] = total[o * 8 : o * 8 + 4]


def route(record, owner, owners, capacity):
    count = record.shape[1]

    def kernel(*refs):
        route_kernel(owners, capacity, *refs)

    return pl.pallas_call(
        kernel,
        out_shape=(
            jax.ShapeDtypeStruct((owners, 4, capacity), F32),
            jax.ShapeDtypeStruct((1, count), jnp.int32),
        ),
        in_specs=[WHOLE] * 2,
        out_specs=(WHOLE, WHOLE),
        compiler_params=PARAMS,
        cost_estimate=pl.CostEstimate(flops=10 * count * count * owners, bytes_accessed=count * 4 * 40, transcendentals=0),
    )(record, owner)


def return_kernel(owners, back, owner, rank, out):
    capacity = back.shape[1]
    count = owner.shape[1]
    slot = lax.broadcasted_iota(jnp.int32, (capacity, count), 0) == rank[...]
    slot = jnp.where(slot, 1.0, 0.0).astype(BF16)
    picked = jnp.zeros((owners * ROWS, count), F32)
    for part in split3(back[...]):
        picked = picked + jnp.dot(part, slot, preferred_element_type=F32)
    target = owner[...]
    total = jnp.zeros((ROWS, count), F32)
    for o in range(owners):
        total = total + jnp.where(target == o, picked[o * ROWS : (o + 1) * ROWS], 0.0)
    out[...] = total[:6]


def returned(back, owner, rank, owners):
    count = owner.shape[1]

    def kernel(*refs):
        return_kernel(owners, *refs)

    return pl.pallas_call(
        kernel,
        out_shape=jax.ShapeDtypeStruct((6, count), F32),
        in_specs=[WHOLE] * 3,
        out_specs=WHOLE,
        compiler_params=PARAMS,
        cost_estimate=pl.CostEstimate(flops=6 * owners * ROWS * back.shape[1] * count, bytes_accessed=count * 100, transcendentals=0),
    )(back, owner, rank)


def y_band(size_y):
    radius = FW // 2
    place = np.concatenate([np.arange(size_y + radius), np.arange(-radius, 0)])
    offset = place[None, :] - np.arange(size_y)[:, None] + radius
    g = np.array(taps())
    band = np.where((offset >= 0) & (offset <= FW), g[np.clip(offset, 0, FW)], 0.0)
    return band[:, :size_y].astype(np.float32), band[:, size_y:].astype(np.float32)


def y_strips(edges):
    radius = FW // 2
    devices = lax.axis_size("gy")
    if devices == 2:
        return lax.ppermute(edges, "gy", [(0, 1), (1, 0)])
    following = shifted(edges[:, :radius], "gy", -1)
    previous = shifted(edges[:, radius:], "gy", 1)
    return jnp.concatenate([following, previous], axis=1)


def on_device(velocity, owner, cell_x, cell_y, cell_z, query_weights):
    _, size_z, size_x, size_y = velocity.shape
    owners = lax.axis_size("gx") * lax.axis_size("gy")
    count = owner.shape[0]
    capacity = 4 * count // owners

    sizes = (size_z, size_x, size_y)
    folded = capacity % BLOCK != 0

    sizes = (size_z, size_x, size_y)
    half = size_x // 2
    folded = capacity % BLOCK != 0

    head, tail = velocity[:, :, :half], velocity[:, :, half:]
    near_left, near_right = shifted(tail, "gx", 1), shifted(head, "gx", -1)
    own_halo = neighbours(velocity, "gz")
    far_left = shifted(after(head, near_left), "gx", 1)
    far_right = shifted(after(tail, near_right), "gx", -1)

    cell = (cell_z * size_x + cell_x) * size_y + cell_y
    record = jnp.concatenate([cell.astype(F32).reshape(1, count), query_weights], axis=0)
    target = owner.reshape(1, count)
    sent, rank = route(record, target, owners, capacity)
    asked = lax.all_to_all(sent, ("gx", "gy"), split_axis=0, concat_axis=0, tiled=True)

    near_left = relayed(after(near_left, own_halo, sent))
    near_right = relayed(near_right)
    far_left = relayed(after(far_left, asked))
    far_right = relayed(far_right)
    if folded:
        asked = asked.transpose(1, 0, 2).reshape(1, 4, owners * capacity)
    own_z = along_z(own_halo[0], velocity, own_halo[1])
    left_z = along_z(*near_left)
    right_z = along_z(*near_right)
    fields = along_x_near(left_z, own_z, right_z)
    fields = along_x_far(True, False, *far_left, fields)
    fields, edges = along_x_far(False, True, *far_right, fields)
    band_own, band_strips = y_band(size_y)
    strips = y_strips(edges)
    partial, *weights = along_y(jnp.asarray(band_own), fields, asked, sizes)
    values = samples(partial, strips, jnp.asarray(band_strips), *weights, asked.shape[0])
    if folded:
        values = values.reshape(ROWS, owners, capacity).transpose(1, 0, 2)
    back = lax.all_to_all(values, ("gx", "gy"), split_axis=0, concat_axis=0, tiled=True)
    return returned(back.reshape(owners * ROWS, capacity), target, rank, owners)


def solution(mesh):
    placed = (
        P(None, "gz", "gx", "gy"),
        P(("gx", "gy", "gz"), None),
        P(("gx", "gy", "gz")),
        P(("gx", "gy", "gz")),
        P(("gx", "gy", "gz")),
        P(None, ("gx", "gy", "gz")),
    )
    return jax.shard_map(
        on_device,
        mesh=mesh,
        in_specs=placed,
        out_specs=P(None, ("gx", "gy", "gz")),
        check_vma=False,
    )
```

time: 79.4 us -> 76.1 us (0.958)
  waiting for transfers between devices: 25.9 us -> 17 us
  starting transfers between devices: 13.2 us -> 21.2 us
  blocking collectives: 13.1 us -> 9.74 us
  local copies, waits for them, and re-layouts: 4.47 us -> 1.75 us
  Pallas kernels: 22.1 us -> 24.4 us
  other arithmetic: 0 us -> 1.45 us
    ppermute x8 -> x14, starting transfers between devices: 8.09 us -> 16.3 us  [shifted(): lax.ppermute(x, axis, [(i, (i + step) % devices) for i in range(devices)])]
    ppermute x8 -> x14, waiting for transfers between devices: 12 us -> 5.47 us  [shifted(): lax.ppermute(x, axis, [(i, (i + step) % devices) for i in range(devices)])]
    pallas_call x3 -> x5, Pallas kernels: 12.1 us -> 16.7 us  [the longest x1 6.76 us: samples(): pl.pallas_call(sample_kernel, out_shape=jax.ShapeDtypeStruct((groups, ROW...]
    unnamed x18 -> x10, local copies, waits for them, and re-layouts: 4.47 us -> 0.71 us
    all_to_all x1, blocking collectives: 13.1 us -> 9.74 us  [on_device(): lax.all_to_all(values, ('gx', 'gy'), split_axis=0, concat_axis=0, tiled=T...]
    all_to_all x1, waiting for transfers between devices: 9.7 us -> 6.83 us  [on_device(): lax.all_to_all(sent, ('gx', 'gy'), split_axis=0, concat_axis=0, tiled=True)]
    pallas_call x3, Pallas kernels: 6.82 us -> 4.5 us  [along_z(): pl.pallas_call(z_kernel, out_shape=jax.ShapeDtypeStruct((9, z, x, y), F32...]
    slice x0 -> x1, local copies, waits for them, and re-layouts: none -> 1.05 us  [on_device(): head, tail = (velocity[:, :, :half], velocity[:, :, half:])]
  transfers between devices with their start and end apart: 10 -> 16, of which waited for: 6 -> 5; matrix products, arithmetic and copies ran while one was open for 0% -> 3% of each run, Pallas kernels for 12% -> 18%
where the time goes in v4:
time: 76.1 us; the launch traced here: 75.7 us
  Pallas kernels  24.4 us (32%)
  starting transfers between devices  21.2 us (28%)
  waiting for transfers between devices  17 us (22%)
  blocking collectives  9.74 us (13%)
  local copies, waits for them, and re-layouts  1.75 us (2%)
  other arithmetic  1.45 us (2%)
    ppermute x14, starting transfers between devices, shifted(): lax.ppermute(x, axis, [(i, (i + step) % devices) for i in range(devices)])  16.3 us
    all_to_all x1, blocking collectives, on_device(): lax.all_to_all(values, ('gx', 'gy'), split_axis=0, concat_axis=0, tiled=T...  9.74 us
    all_to_all x1, waiting for transfers between devices, on_device(): lax.all_to_all(sent, ('gx', 'gy'), split_axis=0, concat_axis=0, tiled=True)  6.83 us
    pallas_call x1, Pallas kernels, samples(): pl.pallas_call(sample_kernel, out_shape=jax.ShapeDtypeStruct((groups, ROW...  6.76 us
    ppermute x14, waiting for transfers between devices, shifted(): lax.ppermute(x, axis, [(i, (i + step) % devices) for i in range(devices)])  5.47 us
    ppermute x1, waiting for transfers between devices, y_strips(): return lax.ppermute(edges, 'gy', [(0, 1), (1, 0)])  4.67 us
    pallas_call x3, Pallas kernels, along_z(): pl.pallas_call(z_kernel, out_shape=jax.ShapeDtypeStruct((9, z, x, y), F32...  4.5 us
    all_to_all x1, starting transfers between devices, on_device(): lax.all_to_all(sent, ('gx', 'gy'), split_axis=0, concat_axis=0, tiled=True)  4.45 us
  transfers between devices with their start and end apart: 16, of which 5 were waited for; matrix products, arithmetic and copies ran while one was open for 3% of the time, Pallas kernels for 18%

profile of v4, /device:TPU:0, one launch (start us, length us, event | category | flops | bytes accessed | tf_op | source)
XLA Modules:
  0.0 75.7 jit_solution(16248727436015944830)
XLA Ops:
  0.5 2.0 %collective-permute-start.9 = (f32[3,16,16,128]{3,2,1,0:T(8,128)}, f32[3,16,16,128]{3,2,1,0:T(8,128)S(1)}, u32[]{:S(2)}, u32[]{:S(2)}) collective-permute-start(f32[3,16,16,128]{3,2,1,0:T(8,128)} %own.1), channel_id=1, source_target_pairs={{0,3},{1,0},{2,1},{3,2},{4,7},{5,4},{6,5},{7,6},{8,11},{9,8},{10,9... | collective-permute-start | bytes 1179656 | tf_op jit(solution)/shard_map/ppermute | solution.py:29
  2.5 1.0 %fusion = (f32[3,16,8,128]{3,2,1,0:T(8,128)S(1)}, f32[3,16,8,128]{3,2,1,0:T(8,128)S(1)}) fusion(f32[3,16,16,128]{3,2,1,0:T(8,128)} %own.1), kind=kLoop, calls=%fused_computation.2 | loop fusion | bytes 786432 | tf_op jit(solution)/shard_map/slice | solution.py:429
  3.5 4.4 %collective-permute-start = (f32[3,16,8,128]{3,2,1,0:T(8,128)S(1)}, f32[3,16,8,128]{3,2,1,0:T(8,128)S(1)}, u32[]{:S(2)}, u32[]{:S(2)}) collective-permute-start(f32[3,16,8,128]{3,2,1,0:T(8,128)S(1)} %get-tuple-element.18), channel_id=1, source_target_pairs={{0,24},{8,0},{16,8},{24,16},{1,25},{9,1},{17,9},{25,17},{2,26},{10... | collective-permute-start | bytes 589832 | tf_op jit(solution)/shard_map/ppermute | solution.py:29
  8.6 0.7 pad_maximum_fusion.refs_0_
  9.4 3.8 %collective-permute-done.own = f32[3,16,8,128]{3,2,1,0:T(8,128)S(1)} collective-permute-done((f32[3,16,8,128]{3,2,1,0:T(8,128)S(1)}, f32[3,16,8,128]{3,2,1,0:T(8,128)S(1)}, u32[]{:S(2)}, u32[]{:S(2)}) %collective-permute-start) | collective-permute-done | bytes 196640 | tf_op jit(solution)/shard_map/ppermute | solution.py:29
  13.2 4.3 %collective-permute-start.1 = (f32[3,16,8,128]{3,2,1,0:T(8,128)S(1)}, f32[3,16,8,128]{3,2,1,0:T(8,128)S(1)}, u32[]{:S(2)}, u32[]{:S(2)}) collective-permute-start(f32[3,16,8,128]{3,2,1,0:T(8,128)S(1)} %get-tuple-element.17), channel_id=1, source_target_pairs={{0,24},{8,0},{16,8},{24,16},{1,25},{9,1},{17,9},{25,17},{2,26},{10... | collective-permute-start | bytes 589832 | tf_op jit(solution)/shard_map/ppermute | solution.py:29
  18.1 1.4 %collective-permute-start.5 = (f32[3,16,8,128]{3,2,1,0:T(8,128)S(1)}, f32[3,16,8,128]{3,2,1,0:T(8,128)S(1)}, u32[]{:S(2)}, u32[]{:S(2)}) collective-permute-start(f32[3,16,8,128]{3,2,1,0:T(8,128)S(1)} %get-tuple-element.18), channel_id=1, source_target_pairs={{0,8},{8,16},{16,24},{24,0},{1,9},{9,17},{17,25},{25,1},{2,10},{10... | collective-permute-start | bytes 589832 | tf_op jit(solution)/shard_map/ppermute | solution.py:29
  20.2 1.9 %shard_map.82 = (f32[8,4,512]{2,1,0:T(4,128)}, s32[1,1024]{1,0:T(1,128)S(1)}) custom-call(f32[4,1024]{1,0:T(4,128)S(1)} %pad_maximum_fusion.refs_0_, s32[1,1024]{1,0:T(1,128)S(1)} %bitcast.4), custom_call_target="tpu_custom_call" | custom-call | flops 83886080 | bytes 163840 | tf_op jit(solution)/shard_map/pallas_call | solution.py:353
  22.6 1.4 %collective-permute-start.11 = (f32[3,16,8,128]{3,2,1,0:T(8,128)S(1)}, f32[3,16,8,128]{3,2,1,0:T(8,128)S(1)}, u32[]{:S(2)}, u32[]{:S(2)}) collective-permute-start(f32[3,16,8,128]{3,2,1,0:T(8,128)S(1)} %collective-permute-done.4.own), channel_id=1, source_target_pairs={{0,3},{1,0},{2,1},{3,2},{4,7},{5,4},{6,5},{7,6},{8,11},{9,8},{10,9... | collective-permute-start | bytes 589832 | tf_op jit(solution)/shard_map/ppermute | solution.py:29
  24.0 4.4 %all-to-all-start = ((f32[8,4,512]{2,1,0:T(4,128)}), f32[8,4,512]{2,1,0:T(4,128)S(1)}, u32[]{:S(2)}, u32[]{:S(2)}) async-start(f32[8,4,512]{2,1,0:T(4,128)} %get-tuple-element.19), calls=%async_computation | async-start | bytes 131072 | tf_op jit(solution)/shard_map/all_to_all | solution.py:439
  28.6 6.8 %all-to-all-done.refs_2_ = f32[8,4,512]{2,1,0:T(4,128)S(1)} async-done(((f32[8,4,512]{2,1,0:T(4,128)}), f32[8,4,512]{2,1,0:T(4,128)S(1)}, u32[]{:S(2)}, u32[]{:S(2)}) %all-to-all-start) | async-done | bytes 65568 | tf_op jit(solution)/shard_map/all_to_all | solution.py:439
  35.9 1.3 %collective-permute-start.3 = (f32[3,16,8,128]{3,2,1,0:T(8,128)S(1)}, f32[3,16,8,128]{3,2,1,0:T(8,128)S(1)}, u32[]{:S(2)}, u32[]{:S(2)}) collective-permute-start(f32[3,16,8,128]{3,2,1,0:T(8,128)S(1)} %collective-permute-done.1.refs_1_), channel_id=1, source_target_pairs={{0,3},{1,0},{2,1},{3,2},{4,7},{5,4},{6,5},{7,6},{8,11},{9,8},{10,9... | collective-permute-start | bytes 589832 | tf_op jit(solution)/shard_map/ppermute | solution.py:29
  37.2 1.1 %shard_map.85.after = f32[9,16,8,128]{3,2,1,0:T(8,128)S(1)} custom-call(f32[3,16,8,128]{3,2,1,0:T(8,128)S(1)} %collective-permute-done.12.before, f32[3,16,8,128]{3,2,1,0:T(8,128)S(1)} %collective-permute-done.own, f32[3,16,8,128]{3,2,1,0:T(8,128)S(1)} %collective-permute-done.13.after), custom_call_target="tpu_custom_call" | custom-call | flops 9732096 | bytes 1376256 | tf_op jit(solution)/shard_map/pallas_call | solution.py:104
  38.4 2.2 %shard_map.84.own = f32[9,16,16,128]{3,2,1,0:T(8,128)S(1)} custom-call(f32[3,16,16,128]{3,2,1,0:T(8,128)S(1)} %collective-permute-done.8.before, f32[3,16,16,128]{3,2,1,0:T(8,128)S(1)} %copy-done, f32[3,16,16,128]{3,2,1,0:T(8,128)S(1)} %collective-permute-done.9.after), custom_call_target="tpu_custom_call" | custom-call | flops 19464192 | bytes 2752512 | tf_op jit(solution)/shard_map/pallas_call | solution.py:104
  40.6 1.2 %shard_map.83.before = f32[9,16,8,128]{3,2,1,0:T(8,128)S(1)} custom-call(f32[3,16,8,128]{3,2,1,0:T(8,128)S(1)} %collective-permute-done.10.before, f32[3,16,8,128]{3,2,1,0:T(8,128)S(1)} %collective-permute-done.4.own, f32[3,16,8,128]{3,2,1,0:T(8,128)S(1)} %collective-permute-done.11.after), custom_call_target="tpu_custom_call" | custom-call | flops 9732096 | bytes 1376256 | tf_op jit(solution)/shard_map/pallas_call | solution.py:104
  41.8 2.1 %shard_map.86.refs_3_ = f32[9,256,128]{2,1,0:T(8,128)S(1)} custom-call(f32[9,16,8,128]{3,2,1,0:T(8,128)S(1)} %shard_map.83.before, f32[9,16,16,128]{3,2,1,0:T(8,128)S(1)} %shard_map.84.own, f32[9,16,8,128]{3,2,1,0:T(8,128)S(1)} %shard_map.85.after), custom_call_target="tpu_custom_call" | custom-call | flops 19464192 | bytes 3932160 | tf_op jit(solution)/shard_map/pallas_call | solution.py:139
  43.9 1.5 %shard_map.87.refs_3_ = f32[9,256,128]{2,1,0:T(8,128)S(1)} custom-call(f32[3,16,8,128]{3,2,1,0:T(8,128)S(1)} %collective-permute-done.6.refs_0_, f32[3,16,8,128]{3,2,1,0:T(8,128)S(1)} %collective-permute-done.5.refs_1_, f32[3,16,8,128]{3,2,1,0:T(8,128)S(1)} %collective-permute-done.7.refs_2_, f32[9,256,128]{2,1,0:T(8,128)S(1)} %shard_map.86.refs_3_), custom_call_target="tpu_custom_call" | custom-call | flops 13271040 | bytes 2621440 | tf_op jit(solution)/shard_map/pallas_call | solution.py:206
  45.4 1.0 %collective-permute-done.2.refs_0_ = f32[3,16,8,128]{3,2,1,0:T(8,128)S(1)} collective-permute-done((f32[3,16,8,128]{3,2,1,0:T(8,128)S(1)}, f32[3,16,8,128]{3,2,1,0:T(8,128)S(1)}, u32[]{:S(2)}, u32[]{:S(2)}) %collective-permute-start.2) | collective-permute-done | bytes 196640 | tf_op jit(solution)/shard_map/ppermute | solution.py:29
  46.3 2.4 %shard_map.88 = (f32[9,256,128]{2,1,0:T(8,128)S(1)}, f32[9,32,256]{2,1,0:T(8,128)S(1)}) custom-call(f32[3,16,8,128]{3,2,1,0:T(8,128)S(1)} %collective-permute-done.2.refs_0_, f32[3,16,8,128]{3,2,1,0:T(8,128)S(1)} %collective-permute-done.1.refs_1_, f32[3,16,8,128]{3,2,1,0:T(8,128)S(1)} %collective-permute-done.3.refs_2_, f32[9,256,128]{2,1,0:T(8,128)S(1)} %shard_map.87.refs_3_), custom_call_target="tpu_custom_call" | custom-call | flops 13271040 | bytes 2621440 | tf_op jit(solution)/shard_map/pallas_call | solution.py:206
  49.2 4.0 %shard_map.89 = (f32[9,128,256]{2,1,0:T(8,128)S(1)}, bf16[256,4096]{1,0:T(8,128)(2,1)S(1)}, bf16[256,4096]{1,0:T(8,128)(2,1)S(1)}, f32[128,4096]{1,0:T(8,128)S(1)}) custom-call(f32[128,128]{1,0:T(8,128)S(1)} %copy-done.4, f32[9,256,128]{2,1,0:T(8,128)S(1)} %get-tuple-element.22.refs_1_, f32[8,4,512]{2,1,0:T(4,128)S(1)} %all-to-all-done.refs_2_), custom_call_target="tpu_custom_call" | custom-call | flops 452984832 | bytes 2359296 | tf_op jit(solution)/shard_map/pallas_call | solution.py:260
  53.2 4.7 %collective-permute-done.14.strips = f32[9,32,256]{2,1,0:T(8,128)S(1)} collective-permute-done((f32[9,32,256]{2,1,0:T(8,128)S(1)}, f32[9,32,256]{2,1,0:T(8,128)S(1)}, u32[]{:S(2)}, u32[]{:S(2)}) %collective-permute-start.14) | collective-permute-done | bytes 294944 | tf_op jit(solution)/shard_map/ppermute | solution.py:410
  57.9 6.8 %shard_map.90 = f32[8,8,512]{2,1,0:T(8,128)S(1)} custom-call(f32[9,128,256]{2,1,0:T(8,128)S(1)} %get-tuple-element.23.partial, f32[9,32,256]{2,1,0:T(8,128)S(1)} %collective-permute-done.14.strips, f32[128,32]{1,0:T(8,128)S(1)} %copy-done.3, bf16[256,4096]{1,0:T(8,128)(2,1)S(1)} %get-tuple-element.25.w_high, bf16[256,4096]{1,0:T(8,128)(2,1)S(1)} %get-tuple-element.26.w_low, ...), custom_call_target="tpu_custom_call" | custom-call | flops 4831838208 | bytes 8388608 | tf_op jit(solution)/shard_map/pallas_call | solution.py:311
  64.6 9.7 %all_to_all.10 = f32[8,8,512]{2,1,0:T(8,128)S(1)} all-to-all(f32[8,8,512]{2,1,0:T(8,128)S(1)} %shard_map.90), channel_id=1, replica_groups=mesh['gx'=4,'gy'=2,'gz'=4] {'gx','gy'}, dimensions={0} | all-to-all | bytes 262144 | tf_op jit(solution)/shard_map/all_to_all | solution.py:459
  74.4 1.3 %shard_map.91 = f32[6,1024]{1,0:T(8,128)} custom-call(f32[64,512]{1,0:T(8,128)S(1)} %bitcast.3, s32[1,1024]{1,0:T(1,128)S(1)} %bitcast.5, s32[1,1024]{1,0:T(1,128)S(1)} %get-tuple-element.28.refs_2_), custom_call_target="tpu_custom_call" | custom-call | flops 201326592 | bytes 102400 | tf_op jit(solution)/shard_map/pallas_call | solution.py:387
  (32 shorter events, 4.1 us)
Async XLA Ops:
  0.0 38.4 %copy-start = (f32[3,16,16,128]{3,2,1,0:T(8,128)S(1)}, f32[3,16,16,128]{3,2,1,0:T(8,128)}, u32[]{:S(2)}) copy-start(f32[3,16,16,128]{3,2,1,0:T(8,128)} %own.1) | copy-start | bytes 1179652
  0.0 22.1 %collective-permute-start.8 = (f32[3,16,16,128]{3,2,1,0:T(8,128)}, f32[3,16,16,128]{3,2,1,0:T(8,128)S(1)}, u32[]{:S(2)}, u32[]{:S(2)}) collective-permute-start(f32[3,16,16,128]{3,2,1,0:T(8,128)} %own.1), channel_id=1, source_target_pairs={{0,1},{1,2},{2,3},{3,0},{4,5},{5,6},{6,7},{7,4},{8,9},{9,10},{10,1... | collective-permute-start | bytes 1179656 | tf_op jit(solution)/shard_map/ppermute | solution.py:29
  0.5 22.2 %collective-permute-start.9 = (f32[3,16,16,128]{3,2,1,0:T(8,128)}, f32[3,16,16,128]{3,2,1,0:T(8,128)S(1)}, u32[]{:S(2)}, u32[]{:S(2)}) collective-permute-start(f32[3,16,16,128]{3,2,1,0:T(8,128)} %own.1), channel_id=1, source_target_pairs={{0,3},{1,0},{2,1},{3,2},{4,7},{5,4},{6,5},{7,6},{8,11},{9,8},{10,9... | collective-permute-start | bytes 1179656 | tf_op jit(solution)/shard_map/ppermute | solution.py:29
  3.5 9.7 %collective-permute-start = (f32[3,16,8,128]{3,2,1,0:T(8,128)S(1)}, f32[3,16,8,128]{3,2,1,0:T(8,128)S(1)}, u32[]{:S(2)}, u32[]{:S(2)}) collective-permute-start(f32[3,16,8,128]{3,2,1,0:T(8,128)S(1)} %get-tuple-element.18), channel_id=1, source_target_pairs={{0,24},{8,0},{16,8},{24,16},{1,25},{9,1},{17,9},{25,17},{2,26},{10... | collective-permute-start | bytes 589832 | tf_op jit(solution)/shard_map/ppermute | solution.py:29
  7.9 10.2 %collective-permute-start.4 = (f32[3,16,8,128]{3,2,1,0:T(8,128)S(1)}, f32[3,16,8,128]{3,2,1,0:T(8,128)S(1)}, u32[]{:S(2)}, u32[]{:S(2)}) collective-permute-start(f32[3,16,8,128]{3,2,1,0:T(8,128)S(1)} %get-tuple-element.17), channel_id=1, source_target_pairs={{0,8},{8,16},{16,24},{24,0},{1,9},{9,17},{17,25},{25,1},{2,10},{10... | collective-permute-start | bytes 589832 | tf_op jit(solution)/shard_map/ppermute | solution.py:29
  13.2 22.2 %collective-permute-start.1 = (f32[3,16,8,128]{3,2,1,0:T(8,128)S(1)}, f32[3,16,8,128]{3,2,1,0:T(8,128)S(1)}, u32[]{:S(2)}, u32[]{:S(2)}) collective-permute-start(f32[3,16,8,128]{3,2,1,0:T(8,128)S(1)} %get-tuple-element.17), channel_id=1, source_target_pairs={{0,24},{8,0},{16,8},{24,16},{1,25},{9,1},{17,9},{25,17},{2,26},{10... | collective-permute-start | bytes 589832 | tf_op jit(solution)/shard_map/ppermute | solution.py:29
  18.1 10.4 %collective-permute-start.5 = (f32[3,16,8,128]{3,2,1,0:T(8,128)S(1)}, f32[3,16,8,128]{3,2,1,0:T(8,128)S(1)}, u32[]{:S(2)}, u32[]{:S(2)}) collective-permute-start(f32[3,16,8,128]{3,2,1,0:T(8,128)S(1)} %get-tuple-element.18), channel_id=1, source_target_pairs={{0,8},{8,16},{16,24},{24,0},{1,9},{9,17},{17,25},{25,1},{2,10},{10... | collective-permute-start | bytes 589832 | tf_op jit(solution)/shard_map/ppermute | solution.py:29
  19.5 15.9 %collective-permute-start.13 = (f32[3,16,8,128]{3,2,1,0:T(8,128)S(1)}, f32[3,16,8,128]{3,2,1,0:T(8,128)S(1)}, u32[]{:S(2)}, u32[]{:S(2)}) collective-permute-start(f32[3,16,8,128]{3,2,1,0:T(8,128)S(1)} %collective-permute-done.own), channel_id=1, source_target_pairs={{0,3},{1,0},{2,1},{3,2},{4,7},{5,4},{6,5},{7,6},{8,11},{9,8},{10,9... | collective-permute-start | bytes 589832 | tf_op jit(solution)/shard_map/ppermute | solution.py:29
  19.5 0.7 copy-start.1
  22.1 13.8 %collective-permute-start.12 = (f32[3,16,8,128]{3,2,1,0:T(8,128)S(1)}, f32[3,16,8,128]{3,2,1,0:T(8,128)S(1)}, u32[]{:S(2)}, u32[]{:S(2)}) collective-permute-start(f32[3,16,8,128]{3,2,1,0:T(8,128)S(1)} %collective-permute-done.own), channel_id=1, source_target_pairs={{0,1},{1,2},{2,3},{3,0},{4,5},{5,6},{6,7},{7,4},{8,9},{9,10},{10,1... | collective-permute-start | bytes 589832 | tf_op jit(solution)/shard_map/ppermute | solution.py:29
  22.6 14.6 %collective-permute-start.11 = (f32[3,16,8,128]{3,2,1,0:T(8,128)S(1)}, f32[3,16,8,128]{3,2,1,0:T(8,128)S(1)}, u32[]{:S(2)}, u32[]{:S(2)}) collective-permute-start(f32[3,16,8,128]{3,2,1,0:T(8,128)S(1)} %collective-permute-done.4.own), channel_id=1, source_target_pairs={{0,3},{1,0},{2,1},{3,2},{4,7},{5,4},{6,5},{7,6},{8,11},{9,8},{10,9... | collective-permute-start | bytes 589832 | tf_op jit(solution)/shard_map/ppermute | solution.py:29
  24.0 11.4 %all-to-all-start = ((f32[8,4,512]{2,1,0:T(4,128)}), f32[8,4,512]{2,1,0:T(4,128)S(1)}, u32[]{:S(2)}, u32[]{:S(2)}) async-start(f32[8,4,512]{2,1,0:T(4,128)} %get-tuple-element.19), calls=%async_computation | async-start | bytes 131072 | tf_op jit(solution)/shard_map/all_to_all | solution.py:439
  28.5 12.1 %collective-permute-start.10 = (f32[3,16,8,128]{3,2,1,0:T(8,128)S(1)}, f32[3,16,8,128]{3,2,1,0:T(8,128)S(1)}, u32[]{:S(2)}, u32[]{:S(2)}) collective-permute-start(f32[3,16,8,128]{3,2,1,0:T(8,128)S(1)} %collective-permute-done.4.own), channel_id=1, source_target_pairs={{0,1},{1,2},{2,3},{3,0},{4,5},{5,6},{6,7},{7,4},{8,9},{9,10},{10,1... | collective-permute-start | bytes 589832 | tf_op jit(solution)/shard_map/ppermute | solution.py:29
  35.4 8.5 %collective-permute-start.7 = (f32[3,16,8,128]{3,2,1,0:T(8,128)S(1)}, f32[3,16,8,128]{3,2,1,0:T(8,128)S(1)}, u32[]{:S(2)}, u32[]{:S(2)}) collective-permute-start(f32[3,16,8,128]{3,2,1,0:T(8,128)S(1)} %collective-permute-done.5.refs_1_), channel_id=1, source_target_pairs={{0,3},{1,0},{2,1},{3,2},{4,7},{5,4},{6,5},{7,6},{8,11},{9,8},{10,9... | collective-permute-start | bytes 589832 | tf_op jit(solution)/shard_map/ppermute | solution.py:29
  35.4 8.5 %collective-permute-start.6 = (f32[3,16,8,128]{3,2,1,0:T(8,128)S(1)}, f32[3,16,8,128]{3,2,1,0:T(8,128)S(1)}, u32[]{:S(2)}, u32[]{:S(2)}) collective-permute-start(f32[3,16,8,128]{3,2,1,0:T(8,128)S(1)} %collective-permute-done.5.refs_1_), channel_id=1, source_target_pairs={{0,1},{1,2},{2,3},{3,0},{4,5},{5,6},{6,7},{7,4},{8,9},{9,10},{10,1... | collective-permute-start | bytes 589832 | tf_op jit(solution)/shard_map/ppermute | solution.py:29
  35.9 9.5 %collective-permute-start.3 = (f32[3,16,8,128]{3,2,1,0:T(8,128)S(1)}, f32[3,16,8,128]{3,2,1,0:T(8,128)S(1)}, u32[]{:S(2)}, u32[]{:S(2)}) collective-permute-start(f32[3,16,8,128]{3,2,1,0:T(8,128)S(1)} %collective-permute-done.1.refs_1_), channel_id=1, source_target_pairs={{0,3},{1,0},{2,1},{3,2},{4,7},{5,4},{6,5},{7,6},{8,11},{9,8},{10,9... | collective-permute-start | bytes 589832 | tf_op jit(solution)/shard_map/ppermute | solution.py:29
  37.2 9.1 %collective-permute-start.2 = (f32[3,16,8,128]{3,2,1,0:T(8,128)S(1)}, f32[3,16,8,128]{3,2,1,0:T(8,128)S(1)}, u32[]{:S(2)}, u32[]{:S(2)}) collective-permute-start(f32[3,16,8,128]{3,2,1,0:T(8,128)S(1)} %collective-permute-done.1.refs_1_), channel_id=1, source_target_pairs={{0,1},{1,2},{2,3},{3,0},{4,5},{5,6},{6,7},{7,4},{8,9},{9,10},{10,1... | collective-permute-start | bytes 589832 | tf_op jit(solution)/shard_map/ppermute | solution.py:29
  45.4 3.8 %copy-start.4 = (f32[128,128]{1,0:T(8,128)S(1)}, f32[128,128]{1,0:T(8,128)}, u32[]{:S(2)}) copy-start(f32[128,128]{1,0:T(8,128)} %constant.8.clone.refs_0_) | copy-start | bytes 196612
  48.7 9.1 %copy-start.3 = (f32[128,32]{1,0:T(8,128)S(1)}, f32[128,32]{1,0:T(8,128)}, u32[]{:S(2)}) copy-start(f32[128,32]{1,0:T(8,128)} %constant.9.clone.band) | copy-start | bytes 49156
  48.7 9.1 %collective-permute-start.14 = (f32[9,32,256]{2,1,0:T(8,128)S(1)}, f32[9,32,256]{2,1,0:T(8,128)S(1)}, u32[]{:S(2)}, u32[]{:S(2)}) collective-permute-start(f32[9,32,256]{2,1,0:T(8,128)S(1)} %get-tuple-element.24), channel_id=1, source_target_pairs={{0,4},{4,0},{1,5},{5,1},{2,6},{6,2},{3,7},{7,3},{8,12},{12,8},{9,1... | collective-permute-start | bytes 884744 | tf_op jit(solution)/shard_map/ppermute | solution.py:410
  57.9 16.5 %copy-start.2 = (s32[1024,1]{0,1:T(1,128)S(1)}, s32[1024,1]{0,1:T(1,128)}, u32[]{:S(2)}) copy-start(s32[1024,1]{0,1:T(1,128)} %param.9) | copy-start | bytes 12292

commit v5 on v4

--- a/solution.py
+++ b/solution.py
@@ -112,106 +112,86 @@
     )(before, own, after)
 
 
-def near_kernel(before, own, after, out, wide):
+def first_kernel(own, right, out, wide):
     layers, size_x = own.shape[1:3]
-    half = before.shape[2]
-    empty = jnp.zeros((size_x - half, own.shape[3]), F32)
+    radius = FW // 2
+    empty = jnp.zeros((radius, own.shape[3]), F32)
     for z in range(layers):
-        wide[z, : size_x - half] = empty
-        wide[z, 2 * size_x + half :] = empty
+        wide[z, :radius] = empty
 
     def filtered(f, carry):
         for z in range(layers):
-            wide[z, size_x - half : size_x] = before[f, z]
-            wide[z, size_x : 2 * size_x] = own[f, z]
-            wide[z, 2 * size_x : 2 * size_x + half] = after[f, z]
+            wide[z, radius : radius + size_x] = own[f, z]
+            wide[z, radius + size_x :] = right[f, z, :radius]
         for z in range(layers):
-            values = [wide[z, i : i + 8] for i in range(3 * size_x - 7)]
+            values = [wide[z, i : i + 8] for i in range(size_x + FW - 7)]
             for x in range(0, size_x, 8):
-                out[f, z * size_x + x : z * size_x + x + 8] = symmetric(values, x + size_x)
+                out[f, z * size_x + x : z * size_x + x + 8] = symmetric(values, x + radius)
         return carry
 
     lax.fori_loop(0, 9, filtered, 0)
 
 
-def along_x_near(before, own, after):
+def along_x_first(own, right):
     _, z, x, y = own.shape
     return pl.pallas_call(
-        near_kernel,
+        first_kernel,
         out_shape=jax.ShapeDtypeStruct((9, z * x, y), F32),
-        in_specs=[WHOLE] * 3,
+        in_specs=[WHOLE] * 2,
         out_specs=WHOLE,
-        scratch_shapes=[pltpu.VMEM((z, 3 * x, y), F32)],
+        scratch_shapes=[pltpu.VMEM((z, x + FW, y), F32)],
         compiler_params=PARAMS,
         cost_estimate=pl.CostEstimate(flops=9 * z * x * y * 66, bytes_accessed=30 * z * x * y * 4, transcendentals=0),
-    )(before, own, after)
-
-
-def far_kernel(leading, last, before, own, after, near, out, *rest):
-    strips = rest[0] if last else None
-    wide, padded = rest[-2:]
-    layers, half, size_y = own.shape[1:]
-    radius = FW // 2
-    size_x = near.shape[1] // layers
+    )(own, right)
+
+
+def last_kernel(before, own, after, partial, out, strips, wide, padded):
+    layers, size_x, size_y = own.shape[1:]
+    radius = FW // 2
     g = taps()
     form_products(before, own, after, wide)
-    empty = jnp.zeros((half, size_y), F32)
+    empty = jnp.zeros((size_x, size_y), F32)
     for z in range(layers):
-        if leading:
-            padded[z, half:] = empty
-        else:
-            padded[z, :half] = empty
+        padded[z, size_x:] = empty
 
     def filtered(f, carry):
-        values = [wide[f, z] for z in range(layers + 2 * radius)]
+        for x in range(0, size_x, 8):
+            values = [wide[f, z, x : x + 8] for z in range(layers + 2 * radius)]
+            for z in range(layers):
+                padded[z, x : x + 8] = symmetric(values, z + radius)
         for z in range(layers):
-            if leading:
-                padded[z, :half] = symmetric(values, z + radius)
-            else:
-                padded[z, half:] = symmetric(values, z + radius)
-        for z in range(layers):
-            start = z * size_x
-            if leading:
-                added = [g[k] * padded[z, k : k + half] for k in range(half)]
-            else:
-                added = [g[2 * radius - k] * padded[z, half - k : 2 * half - k] for k in range(half)]
-                start = start + half
-            while len(added) > 1:
-                added = [p + q for p, q in zip(added[::2], added[1::2])] + added[len(added) // 2 * 2 :]
-            other = z * size_x + (half if leading else 0)
-            out[f, start : start + half] = near[f, start : start + half] + added[0]
-            out[f, other : other + half] = near[f, other : other + half]
-        if last:
-            for n in range(0, layers * size_x, 128):
-                turned = out[f, n : n + 128].T
-                strips[f, :radius, n : n + 128] = turned[:radius]
-                strips[f, radius:, n : n + 128] = turned[size_y - radius :]
+            for x in range(0, size_x, 8):
+                added = [
+                    g[radius - size_x + k] * padded[z, x + k : x + k + 8]
+                    for k in range(size_x - radius, size_x - x)
+                ]
+                while len(added) > 1:
+                    added = [p + q for p, q in zip(added[::2], added[1::2])] + added[len(added) // 2 * 2 :]
+                row = z * size_x + x
+                out[f, row : row + 8] = partial[f, row : row + 8] + added[0]
+        for n in range(0, layers * size_x, 128):
+            turned = out[f, n : n + 128].T
+            strips[f, :radius, n : n + 128] = turned[:radius]
+            strips[f, radius:, n : n + 128] = turned[size_y - radius :]
         return carry
 
     lax.fori_loop(0, 9, filtered, 0)
 
 
-def along_x_far(leading, last, before, own, after, near):
-    _, z, half, y = own.shape
-    cells = near.shape[1]
-
-    def kernel(*refs):
-        far_kernel(leading, last, *refs)
-
-    out_shape = jax.ShapeDtypeStruct((9, cells, y), F32)
-    out_spec = WHOLE
-    if last:
-        out_shape = (out_shape, jax.ShapeDtypeStruct((9, FW, cells), F32))
-        out_spec = (WHOLE, WHOLE)
-    return pl.pallas_call(
-        kernel,
-        out_shape=out_shape,
+def along_x_last(before, own, after, partial):
+    _, z, x, y = own.shape
+    return pl.pallas_call(
+        last_kernel,
+        out_shape=(
+            jax.ShapeDtypeStruct((9, z * x, y), F32),
+            jax.ShapeDtypeStruct((9, FW, z * x), F32),
+        ),
         in_specs=[WHOLE] * 4,
-        out_specs=out_spec,
-        scratch_shapes=[pltpu.VMEM((9, z + FW, half, y), F32), pltpu.VMEM((z, 2 * half, y), F32)],
-        compiler_params=PARAMS,
-        cost_estimate=pl.CostEstimate(flops=9 * z * half * y * 90, bytes_accessed=40 * z * half * y * 4, transcendentals=0),
-    )(before, own, after, near)
+        out_specs=(WHOLE, WHOLE),
+        scratch_shapes=[pltpu.VMEM((9, z + FW, x, y), F32), pltpu.VMEM((z, 2 * x, y), F32)],
+        compiler_params=PARAMS,
+        cost_estimate=pl.CostEstimate(flops=9 * z * x * y * 100, bytes_accessed=40 * z * x * y * 4, transcendentals=0),
+    )(before, own, after, partial)
 
 
 def hat(size, row, offset):
@@ -319,9 +299,9 @@
     )(partial, strips, band, w_high, w_low, w_y)
 
 
-def route_kernel(owners, capacity, record, owner, out, rank_out):
+def route_kernel(owners, capacity, record, out, rank_out):
     count = record.shape[1]
-    target = owner[...]
+    target = record[0:1].astype(jnp.int32)
     named = lax.broadcasted_iota(jnp.int32, (owners, count), 0) == target
     earlier = lax.broadcasted_iota(jnp.int32, (count, count), 0) < lax.broadcasted_iota(jnp.int32, (count, count), 1)
     before = jnp.dot(
@@ -329,22 +309,22 @@
         preferred_element_type=F32,
     )
     rank = jnp.sum(jnp.where(named, before, 0.0), axis=0, keepdims=True).astype(jnp.int32)
-    rank_out[...] = rank
+    rank_out[0:1] = rank
+    rank_out[1:2] = target
     slot = lax.broadcasted_iota(jnp.int32, (capacity, count), 0) == rank
     slot = jnp.where(slot, 1.0, 0.0).astype(BF16)
-    values = jnp.concatenate([record[...], jnp.zeros((4, count), F32)], axis=0)
     total = jnp.zeros((owners * 8, capacity), F32)
-    for part in split3(values):
+    for part in split3(record[...]):
         part = part.astype(F32)
         spread = jnp.concatenate(
             [jnp.where(target == o, part, 0.0) for o in range(owners)], axis=0
         ).astype(BF16)
         total = total + lax.dot_general(spread, slot, (((1,), (1,)), ((), ())), preferred_element_type=F32)
     for o in range(owners):
-        out[o] = total[o * 8 : o * 8 + 4]
-
-
-def route(record, owner, owners, capacity):
+        out[o] = total[o * 8 + 1 : o * 8 + 5]
+
+
+def route(record, owners, capacity):
     count = record.shape[1]
 
     def kernel(*refs):
@@ -354,32 +334,32 @@
         kernel,
         out_shape=(
             jax.ShapeDtypeStruct((owners, 4, capacity), F32),
-            jax.ShapeDtypeStruct((1, count), jnp.int32),
+            jax.ShapeDtypeStruct((2, count), jnp.int32),
         ),
-        in_specs=[WHOLE] * 2,
+        in_specs=[WHOLE],
         out_specs=(WHOLE, WHOLE),
         compiler_params=PARAMS,
         cost_estimate=pl.CostEstimate(flops=10 * count * count * owners, bytes_accessed=count * 4 * 40, transcendentals=0),
-    )(record, owner)
-
-
-def return_kernel(owners, back, owner, rank, out):
+    )(record)
+
+
+def return_kernel(owners, back, place, out):
     capacity = back.shape[1]
-    count = owner.shape[1]
-    slot = lax.broadcasted_iota(jnp.int32, (capacity, count), 0) == rank[...]
+    count = place.shape[1]
+    slot = lax.broadcasted_iota(jnp.int32, (capacity, count), 0) == place[0:1]
     slot = jnp.where(slot, 1.0, 0.0).astype(BF16)
     picked = jnp.zeros((owners * ROWS, count), F32)
     for part in split3(back[...]):
         picked = picked + jnp.dot(part, slot, preferred_element_type=F32)
-    target = owner[...]
+    target = place[1:2]
     total = jnp.zeros((ROWS, count), F32)
     for o in range(owners):
         total = total + jnp.where(target == o, picked[o * ROWS : (o + 1) * ROWS], 0.0)
     out[...] = total[:6]
 
 
-def returned(back, owner, rank, owners):
-    count = owner.shape[1]
+def returned(back, place, owners):
+    count = place.shape[1]
 
     def kernel(*refs):
         return_kernel(owners, *refs)
@@ -387,11 +367,11 @@
     return pl.pallas_call(
         kernel,
         out_shape=jax.ShapeDtypeStruct((6, count), F32),
-        in_specs=[WHOLE] * 3,
+        in_specs=[WHOLE] * 2,
         out_specs=WHOLE,
         compiler_params=PARAMS,
         cost_estimate=pl.CostEstimate(flops=6 * owners * ROWS * back.shape[1] * count, bytes_accessed=count * 100, transcendentals=0),
-    )(back, owner, rank)
+    )(back, place)
 
 
 def y_band(size_y):
@@ -423,33 +403,27 @@
     folded = capacity % BLOCK != 0
 
     sizes = (size_z, size_x, size_y)
-    half = size_x // 2
     folded = capacity % BLOCK != 0
 
-    head, tail = velocity[:, :, :half], velocity[:, :, half:]
-    near_left, near_right = shifted(tail, "gx", 1), shifted(head, "gx", -1)
+    row = lax.broadcasted_iota(jnp.int32, (8, count), 0)
+    cell = (cell_z * size_x + cell_x) * size_y + cell_y
+    record = jnp.pad(query_weights, ((2, 3), (0, 0)))
+    record = jnp.where(row == 1, cell[None].astype(F32), record)
+    record = jnp.where(row == 0, owner.reshape(1, count).astype(F32), record)
+    sent, place = route(record, owners, capacity)
+
+    asked = lax.all_to_all(sent, ("gx", "gy"), split_axis=0, concat_axis=0, tiled=True)
+
+    right = shifted(velocity, "gx", -1)
+    left = shifted(after(velocity, record), "gx", 1)
     own_halo = neighbours(velocity, "gz")
-    far_left = shifted(after(head, near_left), "gx", 1)
-    far_right = shifted(after(tail, near_right), "gx", -1)
-
-    cell = (cell_z * size_x + cell_x) * size_y + cell_y
-    record = jnp.concatenate([cell.astype(F32).reshape(1, count), query_weights], axis=0)
-    target = owner.reshape(1, count)
-    sent, rank = route(record, target, owners, capacity)
-    asked = lax.all_to_all(sent, ("gx", "gy"), split_axis=0, concat_axis=0, tiled=True)
-
-    near_left = relayed(after(near_left, own_halo, sent))
-    near_right = relayed(near_right)
-    far_left = relayed(after(far_left, asked))
-    far_right = relayed(far_right)
+    right = relayed(right)
+    left = relayed(after(left, asked))
     if folded:
         asked = asked.transpose(1, 0, 2).reshape(1, 4, owners * capacity)
     own_z = along_z(own_halo[0], velocity, own_halo[1])
-    left_z = along_z(*near_left)
-    right_z = along_z(*near_right)
-    fields = along_x_near(left_z, own_z, right_z)
-    fields = along_x_far(True, False, *far_left, fields)
-    fields, edges = along_x_far(False, True, *far_right, fields)
+    right_z = along_z(*right)
+    fields, edges = along_x_last(*left, along_x_first(own_z, right_z))
     band_own, band_strips = y_band(size_y)
     strips = y_strips(edges)
     partial, *weights = along_y(jnp.asarray(band_own), fields, asked, sizes)
@@ -457,7 +431,7 @@
     if folded:
         values = values.reshape(ROWS, owners, capacity).transpose(1, 0, 2)
     back = lax.all_to_all(values, ("gx", "gy"), split_axis=0, concat_axis=0, tiled=True)
-    return returned(back.reshape(owners * ROWS, capacity), target, rank, owners)
+    return returned(back.reshape(owners * ROWS, capacity), place, owners)
 
 
 def solution(mesh):

time: 76.1 us -> 73.5 us (0.966)
  starting transfers between devices: 21.2 us -> 16.1 us
  blocking collectives: 9.74 us -> 12.9 us
  waiting for transfers between devices: 17 us -> 16.1 us
    ppermute x14 -> x8, starting transfers between devices: 16.3 us -> 8.34 us  [shifted(): lax.ppermute(x, axis, [(i, (i + step) % devices) for i in range(devices)])]
    all_to_all x1, blocking collectives: 9.74 us -> 12.9 us  [on_device(): lax.all_to_all(values, ('gx', 'gy'), split_axis=0, concat_axis=0, tiled=T...]
    ppermute x1, waiting for transfers between devices: 4.67 us -> 1.93 us  [y_strips(): return lax.ppermute(edges, 'gy', [(0, 1), (1, 0)])]
    ppermute x1, starting transfers between devices: 0.45 us -> 2.09 us  [y_strips(): return lax.ppermute(edges, 'gy', [(0, 1), (1, 0)])]
    all_to_all x1, starting transfers between devices: 4.45 us -> 5.68 us  [on_device(): lax.all_to_all(sent, ('gx', 'gy'), split_axis=0, concat_axis=0, tiled=True)]
    ppermute x14 -> x8, waiting for transfers between devices: 5.47 us -> 6.58 us  [shifted(): lax.ppermute(x, axis, [(i, (i + step) % devices) for i in range(devices)])]
    slice x1 -> x0, local copies, waits for them, and re-layouts: 1.05 us -> none  [on_device(): head, tail = (velocity[:, :, :half], velocity[:, :, half:])]
    select_n x0 -> x1, other arithmetic: none -> 0.79 us  [on_device(): record = jnp.where(row == 0, owner.reshape(1, count).astype(F32), record)]
  transfers between devices with their start and end apart: 16 -> 10, of which waited for: 5 -> 5; matrix products, arithmetic and copies ran while one was open for 3% -> 3% of each run, Pallas kernels for 18% -> 17%
where the time goes in v5:
time: 73.5 us; the launch traced here: 73 us
  Pallas kernels  24.6 us (33%)
  starting transfers between devices  16.1 us (22%)
  waiting for transfers between devices  16.1 us (22%)
  blocking collectives  12.9 us (18%)
  other arithmetic  2.21 us (3%)
  local copies, waits for them, and re-layouts  1.01 us (1%)
    all_to_all x1, blocking collectives, on_device(): lax.all_to_all(values, ('gx', 'gy'), split_axis=0, concat_axis=0, tiled=T...  12.9 us
    ppermute x8, starting transfers between devices, shifted(): lax.ppermute(x, axis, [(i, (i + step) % devices) for i in range(devices)])  8.34 us
    all_to_all x1, waiting for transfers between devices, on_device(): lax.all_to_all(sent, ('gx', 'gy'), split_axis=0, concat_axis=0, tiled=True)  7.59 us
    pallas_call x1, Pallas kernels, samples(): pl.pallas_call(sample_kernel, out_shape=jax.ShapeDtypeStruct((groups, ROW...  6.76 us
    ppermute x8, waiting for transfers between devices, shifted(): lax.ppermute(x, axis, [(i, (i + step) % devices) for i in range(devices)])  6.58 us
    all_to_all x1, starting transfers between devices, on_device(): lax.all_to_all(sent, ('gx', 'gy'), split_axis=0, concat_axis=0, tiled=True)  5.68 us
    pallas_call x2, Pallas kernels, along_z(): pl.pallas_call(z_kernel, out_shape=jax.ShapeDtypeStruct((9, z, x, y), F32...  4.4 us
    pallas_call x1, Pallas kernels, along_x_last(): pl.pallas_call(last_kernel, out_shape=(jax.ShapeDtypeStruct((9, z * x, y)...  4.16 us
  transfers between devices with their start and end apart: 10, of which 5 were waited for; matrix products, arithmetic and copies ran while one was open for 3% of the time, Pallas kernels for 17%

profile of v5, /device:TPU:0, one launch (start us, length us, event | category | flops | bytes accessed | tf_op | source)
XLA Modules:
  0.0 73.0 jit_solution(15240527953676676479)
XLA Ops:
  0.0 5.0 %collective-permute-start.5 = (f32[3,16,16,128]{3,2,1,0:T(8,128)}, f32[3,16,16,128]{3,2,1,0:T(8,128)S(1)}, u32[]{:S(2)}, u32[]{:S(2)}) collective-permute-start(f32[3,16,16,128]{3,2,1,0:T(8,128)} %own.1), channel_id=1, source_target_pairs={{0,24},{8,0},{16,8},{24,16},{1,25},{9,1},{17,9},{25,17},{2,26},{10... | collective-permute-start | bytes 1179656 | tf_op jit(solution)/shard_map/ppermute | solution.py:29
  5.1 0.7 convert_element_type.17
  5.7 0.7 add_convert_fusion
  6.5 0.8 %select_select_fusion.refs_0_ = f32[8,1024]{1,0:T(8,128)S(1)} fusion(f32[3,1024]{1,0:T(4,128)} %param.13, f32[1024]{0:T(1024)S(1)} %add_convert_fusion, f32[1024]{0:T(1024)S(1)} %bitcast.3, pred[8]{0:T(512)(128)(4,1)S(1)} %get-tuple-element.25, pred[8]{0:T(512)(128)(4,1)S(1)} %get-tuple-element.26), kind=kLoop, calls=%fused_computation | loop fusion | flops 16384 | bytes 53264 | tf_op jit(solution)/shard_map/jit(_where)/select_n | solution.py:412
  7.3 0.7 %collective-permute-start.4 = (f32[3,16,16,128]{3,2,1,0:T(8,128)}, f32[3,16,16,128]{3,2,1,0:T(8,128)S(1)}, u32[]{:S(2)}, u32[]{:S(2)}) collective-permute-start(f32[3,16,16,128]{3,2,1,0:T(8,128)} %own.1), channel_id=1, source_target_pairs={{0,3},{1,0},{2,1},{3,2},{4,7},{5,4},{6,5},{7,6},{8,11},{9,8},{10,9... | collective-permute-start | bytes 1179656 | tf_op jit(solution)/shard_map/ppermute | solution.py:29
  8.0 1.9 %shard_map.82 = (f32[8,4,512]{2,1,0:T(4,128)}, s32[2,1024]{1,0:T(2,128)S(1)}) custom-call(f32[8,1024]{1,0:T(8,128)S(1)} %select_select_fusion.refs_0_), custom_call_target="tpu_custom_call" | custom-call | flops 83886080 | bytes 163840 | tf_op jit(solution)/shard_map/pallas_call | solution.py:333
  9.9 5.7 %all-to-all-start = ((f32[8,4,512]{2,1,0:T(4,128)}), f32[8,4,512]{2,1,0:T(4,128)S(1)}, u32[]{:S(2)}, u32[]{:S(2)}) async-start(f32[8,4,512]{2,1,0:T(4,128)} %get-tuple-element.16), calls=%async_computation | async-start | bytes 131072 | tf_op jit(solution)/shard_map/all_to_all | solution.py:415
  15.6 1.7 %collective-permute-start.7 = (f32[3,16,16,128]{3,2,1,0:T(8,128)S(1)}, f32[3,16,16,128]{3,2,1,0:T(8,128)S(1)}, u32[]{:S(2)}, u32[]{:S(2)}) collective-permute-start(f32[3,16,16,128]{3,2,1,0:T(8,128)S(1)} %collective-permute-done.5.own), channel_id=1, source_target_pairs={{0,3},{1,0},{2,1},{3,2},{4,7},{5,4},{6,5},{7,6},{8,11},{9,8},{10,9... | collective-permute-start | bytes 1179656 | tf_op jit(solution)/shard_map/ppermute | solution.py:29
  17.3 7.6 %all-to-all-done.refs_2_ = f32[8,4,512]{2,1,0:T(4,128)S(1)} async-done(((f32[8,4,512]{2,1,0:T(4,128)}), f32[8,4,512]{2,1,0:T(4,128)S(1)}, u32[]{:S(2)}, u32[]{:S(2)}) %all-to-all-start) | async-done | bytes 65568 | tf_op jit(solution)/shard_map/all_to_all | solution.py:415
  24.9 0.8 %collective-permute-start.2 = (f32[3,16,16,128]{3,2,1,0:T(8,128)S(1)}, f32[3,16,16,128]{3,2,1,0:T(8,128)S(1)}, u32[]{:S(2)}, u32[]{:S(2)}) collective-permute-start(f32[3,16,16,128]{3,2,1,0:T(8,128)S(1)} %collective-permute-done.own), channel_id=1, source_target_pairs={{0,3},{1,0},{2,1},{3,2},{4,7},{5,4},{6,5},{7,6},{8,11},{9,8},{10,9... | collective-permute-start | bytes 1179656 | tf_op jit(solution)/shard_map/ppermute | solution.py:29
  25.8 0.2 collective-permute-done.3.before
  26.0 1.0 %copy-done = f32[3,16,16,128]{3,2,1,0:T(8,128)S(1)} copy-done((f32[3,16,16,128]{3,2,1,0:T(8,128)S(1)}, f32[3,16,16,128]{3,2,1,0:T(8,128)}, u32[]{:S(2)}) %copy-start) | copy-done | bytes 393240
  27.0 2.2 %shard_map.83.own = f32[9,16,16,128]{3,2,1,0:T(8,128)S(1)} custom-call(f32[3,16,16,128]{3,2,1,0:T(8,128)S(1)} %collective-permute-done.3.before, f32[3,16,16,128]{3,2,1,0:T(8,128)S(1)} %copy-done, f32[3,16,16,128]{3,2,1,0:T(8,128)S(1)} %collective-permute-done.4.after), custom_call_target="tpu_custom_call" | custom-call | flops 19464192 | bytes 2752512 | tf_op jit(solution)/shard_map/pallas_call | solution.py:104
  29.2 5.2 %collective-permute-done.6.before = f32[3,16,16,128]{3,2,1,0:T(8,128)S(1)} collective-permute-done((f32[3,16,16,128]{3,2,1,0:T(8,128)S(1)}, f32[3,16,16,128]{3,2,1,0:T(8,128)S(1)}, u32[]{:S(2)}, u32[]{:S(2)}) %collective-permute-start.6) | collective-permute-done | bytes 393248 | tf_op jit(solution)/shard_map/ppermute | solution.py:29
  34.4 2.2 %shard_map.84.right = f32[9,16,16,128]{3,2,1,0:T(8,128)S(1)} custom-call(f32[3,16,16,128]{3,2,1,0:T(8,128)S(1)} %collective-permute-done.6.before, f32[3,16,16,128]{3,2,1,0:T(8,128)S(1)} %collective-permute-done.5.own, f32[3,16,16,128]{3,2,1,0:T(8,128)S(1)} %collective-permute-done.7.after), custom_call_target="tpu_custom_call" | custom-call | flops 19464192 | bytes 2752512 | tf_op jit(solution)/shard_map/pallas_call | solution.py:104
  36.6 2.1 %shard_map.85.partial = f32[9,256,128]{2,1,0:T(8,128)S(1)} custom-call(f32[9,16,16,128]{3,2,1,0:T(8,128)S(1)} %shard_map.83.own, f32[9,16,16,128]{3,2,1,0:T(8,128)S(1)} %shard_map.84.right), custom_call_target="tpu_custom_call" | custom-call | flops 19464192 | bytes 3932160 | tf_op jit(solution)/shard_map/pallas_call | solution.py:137
  38.7 1.1 %collective-permute-done.1.before = f32[3,16,16,128]{3,2,1,0:T(8,128)S(1)} collective-permute-done((f32[3,16,16,128]{3,2,1,0:T(8,128)S(1)}, f32[3,16,16,128]{3,2,1,0:T(8,128)S(1)}, u32[]{:S(2)}, u32[]{:S(2)}) %collective-permute-start.1) | collective-permute-done | bytes 393248 | tf_op jit(solution)/shard_map/ppermute | solution.py:29
  39.9 4.2 %shard_map.86 = (f32[9,256,128]{2,1,0:T(8,128)S(1)}, f32[9,32,256]{2,1,0:T(8,128)S(1)}) custom-call(f32[3,16,16,128]{3,2,1,0:T(8,128)S(1)} %collective-permute-done.1.before, f32[3,16,16,128]{3,2,1,0:T(8,128)S(1)} %collective-permute-done.own, f32[3,16,16,128]{3,2,1,0:T(8,128)S(1)} %collective-permute-done.2.after, f32[9,256,128]{2,1,0:T(8,128)S(1)} %shard_map.85.partial), custom_call_target="tpu_custom_call" | custom-call | flops 29491200 | bytes 5242880 | tf_op jit(solution)/shard_map/pallas_call | solution.py:183
  44.0 2.1 %collective-permute-start.8 = (f32[9,32,256]{2,1,0:T(8,128)S(1)}, f32[9,32,256]{2,1,0:T(8,128)S(1)}, u32[]{:S(2)}, u32[]{:S(2)}) collective-permute-start(f32[9,32,256]{2,1,0:T(8,128)S(1)} %get-tuple-element.20), channel_id=1, source_target_pairs={{0,4},{4,0},{1,5},{5,1},{2,6},{6,2},{3,7},{7,3},{8,12},{12,8},{9,1... | collective-permute-start | bytes 884744 | tf_op jit(solution)/shard_map/ppermute | solution.py:390
  46.1 4.0 %shard_map.87 = (f32[9,128,256]{2,1,0:T(8,128)S(1)}, bf16[256,4096]{1,0:T(8,128)(2,1)S(1)}, bf16[256,4096]{1,0:T(8,128)(2,1)S(1)}, f32[128,4096]{1,0:T(8,128)S(1)}) custom-call(f32[128,128]{1,0:T(8,128)S(1)} %copy-done.2, f32[9,256,128]{2,1,0:T(8,128)S(1)} %get-tuple-element.18.refs_1_, f32[8,4,512]{2,1,0:T(4,128)S(1)} %all-to-all-done.refs_2_), custom_call_target="tpu_custom_call" | custom-call | flops 452984832 | bytes 2359296 | tf_op jit(solution)/shard_map/pallas_call | solution.py:240
  50.1 1.9 %collective-permute-done.8.strips = f32[9,32,256]{2,1,0:T(8,128)S(1)} collective-permute-done((f32[9,32,256]{2,1,0:T(8,128)S(1)}, f32[9,32,256]{2,1,0:T(8,128)S(1)}, u32[]{:S(2)}, u32[]{:S(2)}) %collective-permute-start.8) | collective-permute-done | bytes 294944 | tf_op jit(solution)/shard_map/ppermute | solution.py:390
  52.1 6.8 %shard_map.88 = f32[8,8,512]{2,1,0:T(8,128)S(1)} custom-call(f32[9,128,256]{2,1,0:T(8,128)S(1)} %get-tuple-element.19.partial, f32[9,32,256]{2,1,0:T(8,128)S(1)} %collective-permute-done.8.strips, f32[128,32]{1,0:T(8,128)S(1)} %copy-done.1, bf16[256,4096]{1,0:T(8,128)(2,1)S(1)} %get-tuple-element.21.w_high, bf16[256,4096]{1,0:T(8,128)(2,1)S(1)} %get-tuple-element.22.w_low, ...), custom_call_target="tpu_custom_call" | custom-call | flops 4831838208 | bytes 8388608 | tf_op jit(solution)/shard_map/pallas_call | solution.py:291
  58.8 12.9 %all_to_all.10 = f32[8,8,512]{2,1,0:T(8,128)S(1)} all-to-all(f32[8,8,512]{2,1,0:T(8,128)S(1)} %shard_map.88), channel_id=1, replica_groups=mesh['gx'=4,'gy'=2,'gz'=4] {'gx','gy'}, dimensions={0} | all-to-all | bytes 262144 | tf_op jit(solution)/shard_map/all_to_all | solution.py:433
  71.7 1.3 %shard_map.89 = f32[6,1024]{1,0:T(8,128)} custom-call(f32[64,512]{1,0:T(8,128)S(1)} %bitcast.2, s32[2,1024]{1,0:T(2,128)S(1)} %get-tuple-element.24.refs_1_), custom_call_target="tpu_custom_call" | custom-call | flops 201326592 | bytes 102400 | tf_op jit(solution)/shard_map/pallas_call | solution.py:367
  (15 shorter events, 0.0 us)
Async XLA Ops:
  0.0 15.6 %collective-permute-start.5 = (f32[3,16,16,128]{3,2,1,0:T(8,128)}, f32[3,16,16,128]{3,2,1,0:T(8,128)S(1)}, u32[]{:S(2)}, u32[]{:S(2)}) collective-permute-start(f32[3,16,16,128]{3,2,1,0:T(8,128)} %own.1), channel_id=1, source_target_pairs={{0,24},{8,0},{16,8},{24,16},{1,25},{9,1},{17,9},{25,17},{2,26},{10... | collective-permute-start | bytes 1179656 | tf_op jit(solution)/shard_map/ppermute | solution.py:29
  7.3 17.7 %collective-permute-start = (f32[3,16,16,128]{3,2,1,0:T(8,128)}, f32[3,16,16,128]{3,2,1,0:T(8,128)S(1)}, u32[]{:S(2)}, u32[]{:S(2)}) collective-permute-start(f32[3,16,16,128]{3,2,1,0:T(8,128)} %own.1), channel_id=1, source_target_pairs={{0,8},{8,16},{16,24},{24,0},{1,9},{9,17},{17,25},{25,1},{2,10},{10... | collective-permute-start | bytes 1179656 | tf_op jit(solution)/shard_map/ppermute | solution.py:29
  7.3 18.5 %collective-permute-start.4 = (f32[3,16,16,128]{3,2,1,0:T(8,128)}, f32[3,16,16,128]{3,2,1,0:T(8,128)S(1)}, u32[]{:S(2)}, u32[]{:S(2)}) collective-permute-start(f32[3,16,16,128]{3,2,1,0:T(8,128)} %own.1), channel_id=1, source_target_pairs={{0,3},{1,0},{2,1},{3,2},{4,7},{5,4},{6,5},{7,6},{8,11},{9,8},{10,9... | collective-permute-start | bytes 1179656 | tf_op jit(solution)/shard_map/ppermute | solution.py:29
  9.9 15.0 %all-to-all-start = ((f32[8,4,512]{2,1,0:T(4,128)}), f32[8,4,512]{2,1,0:T(4,128)S(1)}, u32[]{:S(2)}, u32[]{:S(2)}) async-start(f32[8,4,512]{2,1,0:T(4,128)} %get-tuple-element.16), calls=%async_computation | async-start | bytes 131072 | tf_op jit(solution)/shard_map/all_to_all | solution.py:415
  15.6 10.4 %collective-permute-start.3 = (f32[3,16,16,128]{3,2,1,0:T(8,128)}, f32[3,16,16,128]{3,2,1,0:T(8,128)S(1)}, u32[]{:S(2)}, u32[]{:S(2)}) collective-permute-start(f32[3,16,16,128]{3,2,1,0:T(8,128)} %own.1), channel_id=1, source_target_pairs={{0,1},{1,2},{2,3},{3,0},{4,5},{5,6},{6,7},{7,4},{8,9},{9,10},{10,1... | collective-permute-start | bytes 1179656 | tf_op jit(solution)/shard_map/ppermute | solution.py:29
  15.6 13.6 %collective-permute-start.7 = (f32[3,16,16,128]{3,2,1,0:T(8,128)S(1)}, f32[3,16,16,128]{3,2,1,0:T(8,128)S(1)}, u32[]{:S(2)}, u32[]{:S(2)}) collective-permute-start(f32[3,16,16,128]{3,2,1,0:T(8,128)S(1)} %collective-permute-done.5.own), channel_id=1, source_target_pairs={{0,3},{1,0},{2,1},{3,2},{4,7},{5,4},{6,5},{7,6},{8,11},{9,8},{10,9... | collective-permute-start | bytes 1179656 | tf_op jit(solution)/shard_map/ppermute | solution.py:29
  17.3 17.1 %collective-permute-start.6 = (f32[3,16,16,128]{3,2,1,0:T(8,128)S(1)}, f32[3,16,16,128]{3,2,1,0:T(8,128)S(1)}, u32[]{:S(2)}, u32[]{:S(2)}) collective-permute-start(f32[3,16,16,128]{3,2,1,0:T(8,128)S(1)} %collective-permute-done.5.own), channel_id=1, source_target_pairs={{0,1},{1,2},{2,3},{3,0},{4,5},{5,6},{6,7},{7,4},{8,9},{9,10},{10,1... | collective-permute-start | bytes 1179656 | tf_op jit(solution)/shard_map/ppermute | solution.py:29
  24.9 13.8 %collective-permute-start.2 = (f32[3,16,16,128]{3,2,1,0:T(8,128)S(1)}, f32[3,16,16,128]{3,2,1,0:T(8,128)S(1)}, u32[]{:S(2)}, u32[]{:S(2)}) collective-permute-start(f32[3,16,16,128]{3,2,1,0:T(8,128)S(1)} %collective-permute-done.own), channel_id=1, source_target_pairs={{0,3},{1,0},{2,1},{3,2},{4,7},{5,4},{6,5},{7,6},{8,11},{9,8},{10,9... | collective-permute-start | bytes 1179656 | tf_op jit(solution)/shard_map/ppermute | solution.py:29
  25.8 14.1 %collective-permute-start.1 = (f32[3,16,16,128]{3,2,1,0:T(8,128)S(1)}, f32[3,16,16,128]{3,2,1,0:T(8,128)S(1)}, u32[]{:S(2)}, u32[]{:S(2)}) collective-permute-start(f32[3,16,16,128]{3,2,1,0:T(8,128)S(1)} %collective-permute-done.own), channel_id=1, source_target_pairs={{0,1},{1,2},{2,3},{3,0},{4,5},{5,6},{6,7},{7,4},{8,9},{9,10},{10,1... | collective-permute-start | bytes 1179656 | tf_op jit(solution)/shard_map/ppermute | solution.py:29
  26.0 1.0 %copy-start = (f32[3,16,16,128]{3,2,1,0:T(8,128)S(1)}, f32[3,16,16,128]{3,2,1,0:T(8,128)}, u32[]{:S(2)}) copy-start(f32[3,16,16,128]{3,2,1,0:T(8,128)} %own.1) | copy-start | bytes 1179652
  38.7 7.4 %copy-start.2 = (f32[128,128]{1,0:T(8,128)S(1)}, f32[128,128]{1,0:T(8,128)}, u32[]{:S(2)}) copy-start(f32[128,128]{1,0:T(8,128)} %constant.15.clone.refs_0_) | copy-start | bytes 196612
  44.0 8.0 %copy-start.1 = (f32[128,32]{1,0:T(8,128)S(1)}, f32[128,32]{1,0:T(8,128)}, u32[]{:S(2)}) copy-start(f32[128,32]{1,0:T(8,128)} %constant.16.clone.band) | copy-start | bytes 49156
  44.0 8.0 %collective-permute-start.8 = (f32[9,32,256]{2,1,0:T(8,128)S(1)}, f32[9,32,256]{2,1,0:T(8,128)S(1)}, u32[]{:S(2)}, u32[]{:S(2)}) collective-permute-start(f32[9,32,256]{2,1,0:T(8,128)S(1)} %get-tuple-element.20), channel_id=1, source_target_pairs={{0,4},{4,0},{1,5},{5,1},{2,6},{6,2},{3,7},{7,3},{8,12},{12,8},{9,1... | collective-permute-start | bytes 884744 | tf_op jit(solution)/shard_map/ppermute | solution.py:390

commit v6 on v5

--- a/solution.py
+++ b/solution.py
@@ -67,7 +67,7 @@
     return high, middle, (rest - middle.astype(F32)).astype(BF16)
 
 
-def form_products(before, own, after, wide):
+def form_products(before, own, after, wide, fields=tuple(range(9))):
     layers = own.shape[1]
     radius = FW // 2
     for part, (ref, skip) in enumerate(((before, layers - radius), (own, 0), (after, 0))):
@@ -75,10 +75,9 @@
 
         def products(z, carry, ref=ref, skip=skip, place=place):
             u = [ref[k, z + skip] for k in range(3)]
-            for k in range(3):
-                wide[k, z + place] = u[k]
-            for k, (a, b) in enumerate(PAIRS):
-                wide[3 + k, z + place] = u[a] * u[b]
+            u = u + [u[a] * u[b] for a, b in PAIRS]
+            for n, f in enumerate(fields):
+                wide[n, z + place] = u[f]
             return carry
 
         lax.fori_loop(0, layers if part == 1 else radius, products, 0, unroll=4)
@@ -145,11 +144,11 @@
     )(own, right)
 
 
-def last_kernel(before, own, after, partial, out, strips, wide, padded):
+def last_kernel(fields, before, own, after, partial, out, strips, wide, padded):
     layers, size_x, size_y = own.shape[1:]
     radius = FW // 2
     g = taps()
-    form_products(before, own, after, wide)
+    form_products(before, own, after, wide, fields)
     empty = jnp.zeros((size_x, size_y), F32)
     for z in range(layers):
         padded[z, size_x:] = empty
@@ -168,29 +167,34 @@
                 while len(added) > 1:
                     added = [p + q for p, q in zip(added[::2], added[1::2])] + added[len(added) // 2 * 2 :]
                 row = z * size_x + x
-                out[f, row : row + 8] = partial[f, row : row + 8] + added[0]
+                out[f, row : row + 8] = partial[fields[0] + f, row : row + 8] + added[0]
         for n in range(0, layers * size_x, 128):
             turned = out[f, n : n + 128].T
             strips[f, :radius, n : n + 128] = turned[:radius]
             strips[f, radius:, n : n + 128] = turned[size_y - radius :]
         return carry
 
-    lax.fori_loop(0, 9, filtered, 0)
-
-
-def along_x_last(before, own, after, partial):
+    lax.fori_loop(0, len(fields), filtered, 0)
+
+
+def along_x_last(fields, before, own, after, partial):
     _, z, x, y = own.shape
-    return pl.pallas_call(
-        last_kernel,
+    count = len(fields)
+
+    def kernel(*refs):
+        last_kernel(fields, *refs)
+
+    return pl.pallas_call(
+        kernel,
         out_shape=(
-            jax.ShapeDtypeStruct((9, z * x, y), F32),
-            jax.ShapeDtypeStruct((9, FW, z * x), F32),
+            jax.ShapeDtypeStruct((count, z * x, y), F32),
+            jax.ShapeDtypeStruct((count, FW, z * x), F32),
         ),
         in_specs=[WHOLE] * 4,
         out_specs=(WHOLE, WHOLE),
-        scratch_shapes=[pltpu.VMEM((9, z + FW, x, y), F32), pltpu.VMEM((z, 2 * x, y), F32)],
-        compiler_params=PARAMS,
-        cost_estimate=pl.CostEstimate(flops=9 * z * x * y * 100, bytes_accessed=40 * z * x * y * 4, transcendentals=0),
+        scratch_shapes=[pltpu.VMEM((count, z + FW, x, y), F32), pltpu.VMEM((z, 2 * x, y), F32)],
+        compiler_params=PARAMS,
+        cost_estimate=pl.CostEstimate(flops=count * z * x * y * 100, bytes_accessed=40 * z * x * y * 4, transcendentals=0),
     )(before, own, after, partial)
 
 
@@ -199,17 +203,8 @@
     return jnp.where(distance == 0, 1.0 - offset, jnp.where(distance == 1, offset, 0.0))
 
 
-def y_kernel(sizes, band, fields, asked, out, w_high, w_low, w_y):
+def hat_kernel(sizes, asked, w_high, w_low, w_y):
     size_z, size_x, size_y = sizes
-
-    def filtered(f, carry):
-        out[f] = lax.dot_general(
-            band[...], fields[f], (((1,), (1,)), ((), ())),
-            precision=lax.Precision.HIGHEST, preferred_element_type=F32,
-        )
-        return carry
-
-    lax.fori_loop(0, 9, filtered, 0)
     blocks = asked.shape[2] // BLOCK
 
     def weights(n, carry):
@@ -230,35 +225,63 @@
     lax.fori_loop(0, asked.shape[0] * blocks, weights, 0)
 
 
-def along_y(band, fields, asked, sizes):
-    _, cells, size_y = fields.shape
+def hats(asked, sizes):
+    size_z, size_x, size_y = sizes
     count = asked.shape[0] * asked.shape[2]
 
     def kernel(*refs):
-        y_kernel(sizes, *refs)
+        hat_kernel(sizes, *refs)
 
     return pl.pallas_call(
         kernel,
         out_shape=(
-            jax.ShapeDtypeStruct((9, size_y, cells), F32),
-            jax.ShapeDtypeStruct((cells, count), BF16),
-            jax.ShapeDtypeStruct((cells, count), BF16),
+            jax.ShapeDtypeStruct((size_z * size_x, count), BF16),
+            jax.ShapeDtypeStruct((size_z * size_x, count), BF16),
             jax.ShapeDtypeStruct((size_y, count), F32),
         ),
-        in_specs=[WHOLE] * 3,
-        out_specs=(WHOLE,) * 4,
+        in_specs=[WHOLE],
+        out_specs=(WHOLE,) * 3,
+        compiler_params=PARAMS,
+        cost_estimate=pl.CostEstimate(flops=count * 2000, bytes_accessed=count * 1600, transcendentals=0),
+    )(asked)
+
+
+def y_kernel(band, *refs):
+    *parts, out = refs
+    start = 0
+    for fields in parts:
+
+        def filtered(f, carry, fields=fields, start=start):
+            out[start + f] = lax.dot_general(
+                band[...], fields[f], (((1,), (1,)), ((), ())),
+                precision=lax.Precision.HIGHEST, preferred_element_type=F32,
+            )
+            return carry
+
+        lax.fori_loop(0, fields.shape[0], filtered, 0)
+        start = start + fields.shape[0]
+
+
+def along_y(band, parts):
+    _, cells, size_y = parts[0].shape
+    return pl.pallas_call(
+        y_kernel,
+        out_shape=jax.ShapeDtypeStruct((9, size_y, cells), F32),
+        in_specs=[WHOLE] * (1 + len(parts)),
+        out_specs=WHOLE,
         compiler_params=PARAMS,
         cost_estimate=pl.CostEstimate(flops=9 * 12 * size_y * size_y * cells, bytes_accessed=18 * cells * size_y * 4, transcendentals=0),
-    )(band, fields, asked)
-
-
-def sample_kernel(partial, strips, band, w_high, w_low, w_y, out, field_high, field_low):
+    )(band, *parts)
+
+
+def sample_kernel(partial, first, second, band, w_high, w_low, w_y, out, field_high, field_low):
     size_y = partial.shape[1]
     blocks = out.shape[2] // BLOCK
 
     def smooth(f):
+        strips = first[f] if f < first.shape[0] else second[f - first.shape[0]]
         return partial[f] + jnp.dot(
-            band[...], strips[f], precision=lax.Precision.HIGHEST, preferred_element_type=F32
+            band[...], strips, precision=lax.Precision.HIGHEST, preferred_element_type=F32
         )
 
     mean = [smooth(k) for k in range(3)]
@@ -285,21 +308,21 @@
     lax.fori_loop(0, out.shape[0] * blocks, sample, 0, unroll=4)
 
 
-def samples(partial, strips, band, w_high, w_low, w_y, groups):
+def samples(partial, first, second, band, w_high, w_low, w_y, groups):
     _, size_y, cells = partial.shape
     count = w_y.shape[1]
     return pl.pallas_call(
         sample_kernel,
         out_shape=jax.ShapeDtypeStruct((groups, ROWS, count // groups), F32),
-        in_specs=[WHOLE] * 6,
+        in_specs=[WHOLE] * 7,
         out_specs=WHOLE,
         scratch_shapes=[pltpu.VMEM((6 * size_y, cells), BF16), pltpu.VMEM((6 * size_y, cells), BF16)],
         compiler_params=PARAMS,
         cost_estimate=pl.CostEstimate(flops=6 * size_y * cells * count * 6, bytes_accessed=8 * 1024 * 1024, transcendentals=0),
-    )(partial, strips, band, w_high, w_low, w_y)
-
-
-def route_kernel(owners, capacity, record, out, rank_out):
+    )(partial, first, second, band, w_high, w_low, w_y)
+
+
+def route_kernel(owners, capacity, record, out, slot_out, target_out):
     count = record.shape[1]
     target = record[0:1].astype(jnp.int32)
     named = lax.broadcasted_iota(jnp.int32, (owners, count), 0) == target
@@ -309,10 +332,10 @@
         preferred_element_type=F32,
     )
     rank = jnp.sum(jnp.where(named, before, 0.0), axis=0, keepdims=True).astype(jnp.int32)
-    rank_out[0:1] = rank
-    rank_out[1:2] = target
+    target_out[...] = target
     slot = lax.broadcasted_iota(jnp.int32, (capacity, count), 0) == rank
     slot = jnp.where(slot, 1.0, 0.0).astype(BF16)
+    slot_out[...] = slot
     total = jnp.zeros((owners * 8, capacity), F32)
     for part in split3(record[...]):
         part = part.astype(F32)
@@ -334,32 +357,30 @@
         kernel,
         out_shape=(
             jax.ShapeDtypeStruct((owners, 4, capacity), F32),
-            jax.ShapeDtypeStruct((2, count), jnp.int32),
+            jax.ShapeDtypeStruct((capacity, count), BF16),
+            jax.ShapeDtypeStruct((1, count), jnp.int32),
         ),
         in_specs=[WHOLE],
-        out_specs=(WHOLE, WHOLE),
+        out_specs=(WHOLE,) * 3,
         compiler_params=PARAMS,
         cost_estimate=pl.CostEstimate(flops=10 * count * count * owners, bytes_accessed=count * 4 * 40, transcendentals=0),
     )(record)
 
 
-def return_kernel(owners, back, place, out):
-    capacity = back.shape[1]
-    count = place.shape[1]
-    slot = lax.broadcasted_iota(jnp.int32, (capacity, count), 0) == place[0:1]
-    slot = jnp.where(slot, 1.0, 0.0).astype(BF16)
+def return_kernel(owners, back, slot, owner, out):
+    count = owner.shape[1]
     picked = jnp.zeros((owners * ROWS, count), F32)
     for part in split3(back[...]):
-        picked = picked + jnp.dot(part, slot, preferred_element_type=F32)
-    target = place[1:2]
+        picked = picked + jnp.dot(part, slot[...], preferred_element_type=F32)
+    target = owner[...]
     total = jnp.zeros((ROWS, count), F32)
     for o in range(owners):
         total = total + jnp.where(target == o, picked[o * ROWS : (o + 1) * ROWS], 0.0)
     out[...] = total[:6]
 
 
-def returned(back, place, owners):
-    count = place.shape[1]
+def returned(back, slot, owner, owners):
+    count = owner.shape[1]
 
     def kernel(*refs):
         return_kernel(owners, *refs)
@@ -367,11 +388,11 @@
     return pl.pallas_call(
         kernel,
         out_shape=jax.ShapeDtypeStruct((6, count), F32),
-        in_specs=[WHOLE] * 2,
+        in_specs=[WHOLE] * 3,
         out_specs=WHOLE,
         compiler_params=PARAMS,
         cost_estimate=pl.CostEstimate(flops=6 * owners * ROWS * back.shape[1] * count, bytes_accessed=count * 100, transcendentals=0),
-    )(back, place)
+    )(back, slot, owner)
 
 
 def y_band(size_y):
@@ -410,28 +431,31 @@
     record = jnp.pad(query_weights, ((2, 3), (0, 0)))
     record = jnp.where(row == 1, cell[None].astype(F32), record)
     record = jnp.where(row == 0, owner.reshape(1, count).astype(F32), record)
-    sent, place = route(record, owners, capacity)
-
-    asked = lax.all_to_all(sent, ("gx", "gy"), split_axis=0, concat_axis=0, tiled=True)
+    sent, slot, target = route(record, owners, capacity)
 
     right = shifted(velocity, "gx", -1)
     left = shifted(after(velocity, record), "gx", 1)
     own_halo = neighbours(velocity, "gz")
-    right = relayed(right)
-    left = relayed(after(left, asked))
+    right = relayed(after(right, own_halo, sent))
+    asked = lax.all_to_all(sent, ("gx", "gy"), split_axis=0, concat_axis=0, tiled=True)
+    own_z = along_z(own_halo[0], velocity, own_halo[1])
+    left = relayed(after(left, own_z, asked))
+    partial = along_x_first(own_z, along_z(*right))
     if folded:
         asked = asked.transpose(1, 0, 2).reshape(1, 4, owners * capacity)
-    own_z = along_z(own_halo[0], velocity, own_halo[1])
-    right_z = along_z(*right)
-    fields, edges = along_x_last(*left, along_x_first(own_z, right_z))
+    weights = hats(asked, sizes)
+    partial = after(partial, weights)
     band_own, band_strips = y_band(size_y)
-    strips = y_strips(edges)
-    partial, *weights = along_y(jnp.asarray(band_own), fields, asked, sizes)
-    values = samples(partial, strips, jnp.asarray(band_strips), *weights, asked.shape[0])
+    first, edges = along_x_last(tuple(range(5)), *left, partial)
+    first_strips = y_strips(edges)
+    second, edges = along_x_last(tuple(range(5, 9)), *left, partial)
+    second_strips = y_strips(edges)
+    partial = along_y(jnp.asarray(band_own), (first, second))
+    values = samples(partial, first_strips, second_strips, jnp.asarray(band_strips), *weights, asked.shape[0])
     if folded:
         values = values.reshape(ROWS, owners, capacity).transpose(1, 0, 2)
     back = lax.all_to_all(values, ("gx", "gy"), split_axis=0, concat_axis=0, tiled=True)
-    return returned(back.reshape(owners * ROWS, capacity), place, owners)
+    return returned(back.reshape(owners * ROWS, capacity), slot, target, owners)
 
 
 def solution(mesh):

time: 73.5 us -> 69.7 us (0.948)
  waiting for transfers between devices: 16.1 us -> 9.64 us
  local copies, waits for them, and re-layouts: 1.01 us -> 2.76 us
  Pallas kernels: 24.6 us -> 25.9 us
    ppermute x8, waiting for transfers between devices: 6.58 us -> 3.35 us  [shifted(): lax.ppermute(x, axis, [(i, (i + step) % devices) for i in range(devices)])]
    all_to_all x1, waiting for transfers between devices: 7.59 us -> 4.5 us  [on_device(): lax.all_to_all(sent, ('gx', 'gy'), split_axis=0, concat_axis=0, tiled=True)]
    unnamed x6 -> x10, local copies, waits for them, and re-layouts: 1.01 us -> 2.76 us
    pallas_call x2, Pallas kernels: 4.4 us -> 5.51 us  [along_z(): pl.pallas_call(z_kernel, out_shape=jax.ShapeDtypeStruct((9, z, x, y), F32...]
    ppermute x1 -> x2, waiting for transfers between devices: 1.93 us -> 1.8 us  [y_strips(): return lax.ppermute(edges, 'gy', [(0, 1), (1, 0)])]
    ppermute x1 -> x2, starting transfers between devices: 2.09 us -> 2.16 us  [y_strips(): return lax.ppermute(edges, 'gy', [(0, 1), (1, 0)])]
    pallas_call x2 -> x4, Pallas kernels: 8.15 us -> 8.17 us  [the longest x2 4.19 us: along_x_last(): pl.pallas_call(kernel, out_shape=(jax.ShapeDtypeStruct((count, z * x, y),...]
  transfers between devices with their start and end apart: 10 -> 11, of which waited for: 5 -> 4; matrix products, arithmetic and copies ran while one was open for 3% -> 3% of each run, Pallas kernels for 17% -> 22%
where the time goes in v6:
time: 69.7 us; the launch traced here: 69.2 us
  Pallas kernels  25.9 us (37%)
  starting transfers between devices  16 us (23%)
  blocking collectives  12.6 us (18%)
  waiting for transfers between devices  9.64 us (14%)
  local copies, waits for them, and re-layouts  2.76 us (4%)
  other arithmetic  2.21 us (3%)
    all_to_all x1, blocking collectives, on_device(): lax.all_to_all(values, ('gx', 'gy'), split_axis=0, concat_axis=0, tiled=T...  12.6 us
    ppermute x8, starting transfers between devices, shifted(): lax.ppermute(x, axis, [(i, (i + step) % devices) for i in range(devices)])  7.83 us
    pallas_call x1, Pallas kernels, samples(): pl.pallas_call(sample_kernel, out_shape=jax.ShapeDtypeStruct((groups, ROW...  6.76 us
    all_to_all x1, starting transfers between devices, on_device(): lax.all_to_all(sent, ('gx', 'gy'), split_axis=0, concat_axis=0, tiled=True)  6.01 us
    pallas_call x2, Pallas kernels, along_z(): pl.pallas_call(z_kernel, out_shape=jax.ShapeDtypeStruct((9, z, x, y), F32...  5.51 us
    all_to_all x1, waiting for transfers between devices, on_device(): lax.all_to_all(sent, ('gx', 'gy'), split_axis=0, concat_axis=0, tiled=True)  4.5 us
    pallas_call x2, Pallas kernels, along_x_last(): pl.pallas_call(kernel, out_shape=(jax.ShapeDtypeStruct((count, z * x, y),...  4.19 us
    ppermute x8, waiting for transfers between devices, shifted(): lax.ppermute(x, axis, [(i, (i + step) % devices) for i in range(devices)])  3.35 us
  transfers between devices with their start and end apart: 11, of which 4 were waited for; matrix products, arithmetic and copies ran while one was open for 3% of the time, Pallas kernels for 22%

profile of v6, /device:TPU:0, one launch (start us, length us, event | category | flops | bytes accessed | tf_op | source)
XLA Modules:
  0.0 69.2 jit_solution(4004504969539025809)
XLA Ops:
  0.0 2.4 %collective-permute-start.2 = (f32[3,16,16,128]{3,2,1,0:T(8,128)}, f32[3,16,16,128]{3,2,1,0:T(8,128)S(1)}, u32[]{:S(2)}, u32[]{:S(2)}) collective-permute-start(f32[3,16,16,128]{3,2,1,0:T(8,128)} %own.1), channel_id=1, source_target_pairs={{0,3},{1,0},{2,1},{3,2},{4,7},{5,4},{6,5},{7,6},{8,11},{9,8},{10,9... | collective-permute-start | bytes 1179656 | tf_op jit(solution)/shard_map/ppermute | solution.py:29
  2.4 3.6 %collective-permute-start.5 = (f32[3,16,16,128]{3,2,1,0:T(8,128)}, f32[3,16,16,128]{3,2,1,0:T(8,128)S(1)}, u32[]{:S(2)}, u32[]{:S(2)}) collective-permute-start(f32[3,16,16,128]{3,2,1,0:T(8,128)} %own.1), channel_id=1, source_target_pairs={{0,24},{8,0},{16,8},{24,16},{1,25},{9,1},{17,9},{25,17},{2,26},{10... | collective-permute-start | bytes 1179656 | tf_op jit(solution)/shard_map/ppermute | solution.py:29
  7.4 0.8 %select_select_fusion.refs_0_ = f32[8,1024]{1,0:T(8,128)S(1)} fusion(f32[3,1024]{1,0:T(4,128)} %param.13, f32[1024]{0:T(1024)S(1)} %add_convert_fusion, f32[1024]{0:T(1024)S(1)} %bitcast.3, pred[8]{0:T(512)(128)(4,1)S(1)} %get-tuple-element.33, pred[8]{0:T(512)(128)(4,1)S(1)} %get-tuple-element.34), kind=kLoop, calls=%fused_computation | loop fusion | flops 16384 | bytes 53264 | tf_op jit(solution)/shard_map/jit(_where)/select_n | solution.py:433
  8.2 2.1 %shard_map.83 = (f32[8,4,512]{2,1,0:T(4,128)}, bf16[512,1024]{1,0:T(8,128)(2,1)S(1)}, s32[1,1024]{1,0:T(1,128)S(1)}) custom-call(f32[8,1024]{1,0:T(8,128)S(1)} %select_select_fusion.refs_0_), custom_call_target="tpu_custom_call" | custom-call | flops 83886080 | bytes 163840 | tf_op jit(solution)/shard_map/pallas_call | solution.py:356
  10.3 6.0 %all-to-all-start = ((f32[8,4,512]{2,1,0:T(4,128)}), f32[8,4,512]{2,1,0:T(4,128)S(1)}, u32[]{:S(2)}, u32[]{:S(2)}) async-start(f32[8,4,512]{2,1,0:T(4,128)} %get-tuple-element.20), calls=%async_computation | async-start | bytes 131072 | tf_op jit(solution)/shard_map/all_to_all | solution.py:440
  17.1 0.9 %collective-permute-start.7 = (f32[3,16,16,128]{3,2,1,0:T(8,128)S(1)}, f32[3,16,16,128]{3,2,1,0:T(8,128)}, u32[]{:S(2)}, u32[]{:S(2)}) collective-permute-start(f32[3,16,16,128]{3,2,1,0:T(8,128)S(1)} %collective-permute-done.5.own), channel_id=1, source_target_pairs={{0,3},{1,0},{2,1},{3,2},{4,7},{5,4},{6,5},{7,6},{8,11},{9,8},{10,9... | collective-permute-start | bytes 1179656 | tf_op jit(solution)/shard_map/ppermute | solution.py:29
  18.0 1.0 %copy-done = f32[3,16,16,128]{3,2,1,0:T(8,128)S(1)} copy-done((f32[3,16,16,128]{3,2,1,0:T(8,128)S(1)}, f32[3,16,16,128]{3,2,1,0:T(8,128)}, u32[]{:S(2)}) %copy-start) | copy-done | bytes 393240
  19.0 1.0 %copy-done.2 = f32[3,16,16,128]{3,2,1,0:T(8,128)S(1)} copy-done((f32[3,16,16,128]{3,2,1,0:T(8,128)S(1)}, f32[3,16,16,128]{3,2,1,0:T(8,128)}, u32[]{:S(2)}) %copy-start.2) | copy-done | bytes 393240
  20.0 2.2 %shard_map.82.own = f32[9,16,16,128]{3,2,1,0:T(8,128)S(1)} custom-call(f32[3,16,16,128]{3,2,1,0:T(8,128)S(1)} %copy-done.2, f32[3,16,16,128]{3,2,1,0:T(8,128)S(1)} %copy-done, f32[3,16,16,128]{3,2,1,0:T(8,128)S(1)} %collective-permute-done.2.after), custom_call_target="tpu_custom_call" | custom-call | flops 19464192 | bytes 2752512 | tf_op jit(solution)/shard_map/pallas_call | solution.py:103
  22.2 4.5 %all-to-all-done.refs_0_ = f32[8,4,512]{2,1,0:T(4,128)S(1)} async-done(((f32[8,4,512]{2,1,0:T(4,128)}), f32[8,4,512]{2,1,0:T(4,128)S(1)}, u32[]{:S(2)}, u32[]{:S(2)}) %all-to-all-start) | async-done | bytes 65568 | tf_op jit(solution)/shard_map/all_to_all | solution.py:440
  26.7 0.9 %collective-permute-start.4 = (f32[3,16,16,128]{3,2,1,0:T(8,128)S(1)}, f32[3,16,16,128]{3,2,1,0:T(8,128)S(1)}, u32[]{:S(2)}, u32[]{:S(2)}) collective-permute-start(f32[3,16,16,128]{3,2,1,0:T(8,128)S(1)} %collective-permute-done.refs_1_), channel_id=1, source_target_pairs={{0,3},{1,0},{2,1},{3,2},{4,7},{5,4},{6,5},{7,6},{8,11},{9,8},{10,9... | collective-permute-start | bytes 1179656 | tf_op jit(solution)/shard_map/ppermute | solution.py:29
  27.6 1.5 %shard_map.86 = (bf16[256,4096]{1,0:T(8,128)(2,1)S(1)}, bf16[256,4096]{1,0:T(8,128)(2,1)S(1)}, f32[128,4096]{1,0:T(8,128)S(1)}) custom-call(f32[8,4,512]{2,1,0:T(4,128)S(1)} %all-to-all-done.refs_0_), custom_call_target="tpu_custom_call" | custom-call | flops 8192000 | bytes 6553600 | tf_op jit(solution)/shard_map/pallas_call | solution.py:235
  29.2 3.3 %shard_map.84.right = f32[9,16,16,128]{3,2,1,0:T(8,128)S(1)} custom-call(f32[3,16,16,128]{3,2,1,0:T(8,128)} %collective-permute-done.6.before, f32[3,16,16,128]{3,2,1,0:T(8,128)S(1)} %collective-permute-done.5.own, f32[3,16,16,128]{3,2,1,0:T(8,128)} %collective-permute-done.7.after), custom_call_target="tpu_custom_call" | custom-call | flops 19464192 | bytes 2752512 | tf_op jit(solution)/shard_map/pallas_call | solution.py:103
  32.5 2.1 %shard_map.85.refs_3_ = f32[9,256,128]{2,1,0:T(8,128)S(1)} custom-call(f32[9,16,16,128]{3,2,1,0:T(8,128)S(1)} %shard_map.82.own, f32[9,16,16,128]{3,2,1,0:T(8,128)S(1)} %shard_map.84.right), custom_call_target="tpu_custom_call" | custom-call | flops 19464192 | bytes 3932160 | tf_op jit(solution)/shard_map/pallas_call | solution.py:136
  34.6 2.3 %collective-permute-done.4.refs_2_ = f32[3,16,16,128]{3,2,1,0:T(8,128)S(1)} collective-permute-done((f32[3,16,16,128]{3,2,1,0:T(8,128)S(1)}, f32[3,16,16,128]{3,2,1,0:T(8,128)S(1)}, u32[]{:S(2)}, u32[]{:S(2)}) %collective-permute-start.4) | collective-permute-done | bytes 393248 | tf_op jit(solution)/shard_map/ppermute | solution.py:29
  36.9 1.0 %collective-permute-done.3.refs_0_ = f32[3,16,16,128]{3,2,1,0:T(8,128)S(1)} collective-permute-done((f32[3,16,16,128]{3,2,1,0:T(8,128)S(1)}, f32[3,16,16,128]{3,2,1,0:T(8,128)S(1)}, u32[]{:S(2)}, u32[]{:S(2)}) %collective-permute-start.3) | collective-permute-done | bytes 393248 | tf_op jit(solution)/shard_map/ppermute | solution.py:29
  37.9 2.3 %shard_map.87 = (f32[5,256,128]{2,1,0:T(8,128)S(1)}, f32[5,32,256]{2,1,0:T(8,128)S(1)}) custom-call(f32[3,16,16,128]{3,2,1,0:T(8,128)S(1)} %collective-permute-done.3.refs_0_, f32[3,16,16,128]{3,2,1,0:T(8,128)S(1)} %collective-permute-done.refs_1_, f32[3,16,16,128]{3,2,1,0:T(8,128)S(1)} %collective-permute-done.4.refs_2_, f32[9,256,128]{2,1,0:T(8,128)S(1)} %shard_map.85.refs_3_), custom_call_target="tpu_custom_call" | custom-call | flops 16384000 | bytes 5242880 | tf_op jit(solution)/shard_map/pallas_call | solution.py:187
  40.2 1.4 %collective-permute-start.8 = (f32[5,32,256]{2,1,0:T(8,128)S(1)}, f32[5,32,256]{2,1,0:T(8,128)S(1)}, u32[]{:S(2)}, u32[]{:S(2)}) collective-permute-start(f32[5,32,256]{2,1,0:T(8,128)S(1)} %get-tuple-element.29), channel_id=1, source_target_pairs={{0,4},{4,0},{1,5},{5,1},{2,6},{6,2},{3,7},{7,3},{8,12},{12,8},{9,1... | collective-permute-start | bytes 491528 | tf_op jit(solution)/shard_map/ppermute | solution.py:411
  41.7 1.9 %shard_map.88 = (f32[4,256,128]{2,1,0:T(8,128)S(1)}, f32[4,32,256]{2,1,0:T(8,128)S(1)}) custom-call(f32[3,16,16,128]{3,2,1,0:T(8,128)S(1)} %collective-permute-done.3.refs_0_, f32[3,16,16,128]{3,2,1,0:T(8,128)S(1)} %collective-permute-done.refs_1_, f32[3,16,16,128]{3,2,1,0:T(8,128)S(1)} %collective-permute-done.4.refs_2_, f32[9,256,128]{2,1,0:T(8,128)S(1)} %shard_map.85.refs_3_), custom_call_target="tpu_custom_call" | custom-call | flops 13107200 | bytes 5242880 | tf_op jit(solution)/shard_map/pallas_call | solution.py:187
  44.3 2.5 %shard_map.89.partial = f32[9,128,256]{2,1,0:T(8,128)S(1)} custom-call(f32[128,128]{1,0:T(8,128)S(1)} %copy-done.3, f32[5,256,128]{2,1,0:T(8,128)S(1)} %get-tuple-element.27.refs_0_, f32[4,256,128]{2,1,0:T(8,128)S(1)} %get-tuple-element.28.refs_1_), custom_call_target="tpu_custom_call" | custom-call | flops 452984832 | bytes 2359296 | tf_op jit(solution)/shard_map/pallas_call | solution.py:267
  46.8 1.8 %collective-permute-done.9.second = f32[4,32,256]{2,1,0:T(8,128)S(1)} collective-permute-done((f32[4,32,256]{2,1,0:T(8,128)S(1)}, f32[4,32,256]{2,1,0:T(8,128)S(1)}, u32[]{:S(2)}, u32[]{:S(2)}) %collective-permute-start.9) | collective-permute-done | bytes 131104 | tf_op jit(solution)/shard_map/ppermute | solution.py:411
  48.6 6.8 %shard_map.90 = f32[8,8,512]{2,1,0:T(8,128)S(1)} custom-call(f32[9,128,256]{2,1,0:T(8,128)S(1)} %shard_map.89.partial, f32[5,32,256]{2,1,0:T(8,128)S(1)} %collective-permute-done.8.first, f32[4,32,256]{2,1,0:T(8,128)S(1)} %collective-permute-done.9.second, f32[128,32]{1,0:T(8,128)S(1)} %copy-done.4, bf16[256,4096]{1,0:T(8,128)(2,1)S(1)} %get-tuple-element.23.w_high, ...), custom_call_target="tpu_custom_call" | custom-call | flops 4831838208 | bytes 8388608 | tf_op jit(solution)/shard_map/pallas_call | solution.py:314
  55.3 12.6 %all_to_all.10 = f32[8,8,512]{2,1,0:T(8,128)S(1)} all-to-all(f32[8,8,512]{2,1,0:T(8,128)S(1)} %shard_map.90), channel_id=1, replica_groups=mesh['gx'=4,'gy'=2,'gz'=4] {'gx','gy'}, dimensions={0} | all-to-all | bytes 262144 | tf_op jit(solution)/shard_map/all_to_all | solution.py:457
  68.0 1.3 %shard_map.91 = f32[6,1024]{1,0:T(8,128)} custom-call(f32[64,512]{1,0:T(8,128)S(1)} %bitcast.2, bf16[512,1024]{1,0:T(8,128)(2,1)S(1)} %get-tuple-element.31.refs_1_, s32[1,1024]{1,0:T(1,128)S(1)} %get-tuple-element.32.refs_2_), custom_call_target="tpu_custom_call" | custom-call | flops 201326592 | bytes 102400 | tf_op jit(solution)/shard_map/pallas_call | solution.py:388
  (23 shorter events, 2.9 us)
Async XLA Ops:
  0.0 16.3 %collective-permute-start.2 = (f32[3,16,16,128]{3,2,1,0:T(8,128)}, f32[3,16,16,128]{3,2,1,0:T(8,128)S(1)}, u32[]{:S(2)}, u32[]{:S(2)}) collective-permute-start(f32[3,16,16,128]{3,2,1,0:T(8,128)} %own.1), channel_id=1, source_target_pairs={{0,3},{1,0},{2,1},{3,2},{4,7},{5,4},{6,5},{7,6},{8,11},{9,8},{10,9... | collective-permute-start | bytes 1179656 | tf_op jit(solution)/shard_map/ppermute | solution.py:29
  2.4 13.9 %collective-permute-start.1 = (f32[3,16,16,128]{3,2,1,0:T(8,128)}, f32[3,16,16,128]{3,2,1,0:T(8,128)S(1)}, u32[]{:S(2)}, u32[]{:S(2)}) collective-permute-start(f32[3,16,16,128]{3,2,1,0:T(8,128)} %own.1), channel_id=1, source_target_pairs={{0,1},{1,2},{2,3},{3,0},{4,5},{5,6},{6,7},{7,4},{8,9},{9,10},{10,1... | collective-permute-start | bytes 1179656 | tf_op jit(solution)/shard_map/ppermute | solution.py:29
  2.4 14.7 %collective-permute-start.5 = (f32[3,16,16,128]{3,2,1,0:T(8,128)}, f32[3,16,16,128]{3,2,1,0:T(8,128)S(1)}, u32[]{:S(2)}, u32[]{:S(2)}) collective-permute-start(f32[3,16,16,128]{3,2,1,0:T(8,128)} %own.1), channel_id=1, source_target_pairs={{0,24},{8,0},{16,8},{24,16},{1,25},{9,1},{17,9},{25,17},{2,26},{10... | collective-permute-start | bytes 1179656 | tf_op jit(solution)/shard_map/ppermute | solution.py:29
  8.2 18.5 %collective-permute-start = (f32[3,16,16,128]{3,2,1,0:T(8,128)}, f32[3,16,16,128]{3,2,1,0:T(8,128)S(1)}, u32[]{:S(2)}, u32[]{:S(2)}) collective-permute-start(f32[3,16,16,128]{3,2,1,0:T(8,128)} %own.1), channel_id=1, source_target_pairs={{0,8},{8,16},{16,24},{24,0},{1,9},{9,17},{17,25},{25,1},{2,10},{10... | collective-permute-start | bytes 1179656 | tf_op jit(solution)/shard_map/ppermute | solution.py:29
  10.3 16.4 %all-to-all-start = ((f32[8,4,512]{2,1,0:T(4,128)}), f32[8,4,512]{2,1,0:T(4,128)S(1)}, u32[]{:S(2)}, u32[]{:S(2)}) async-start(f32[8,4,512]{2,1,0:T(4,128)} %get-tuple-element.20), calls=%async_computation | async-start | bytes 131072 | tf_op jit(solution)/shard_map/all_to_all | solution.py:440
  16.4 0.8 %copy-start.1 = (f32[3,16,16,128]{3,2,1,0:T(8,128)}, f32[3,16,16,128]{3,2,1,0:T(8,128)S(1)}, u32[]{:S(2)}) copy-start(f32[3,16,16,128]{3,2,1,0:T(8,128)S(1)} %collective-permute-done.1.before) | copy-start | bytes 1179652
  17.1 12.0 %collective-permute-start.7 = (f32[3,16,16,128]{3,2,1,0:T(8,128)S(1)}, f32[3,16,16,128]{3,2,1,0:T(8,128)}, u32[]{:S(2)}, u32[]{:S(2)}) collective-permute-start(f32[3,16,16,128]{3,2,1,0:T(8,128)S(1)} %collective-permute-done.5.own), channel_id=1, source_target_pairs={{0,3},{1,0},{2,1},{3,2},{4,7},{5,4},{6,5},{7,6},{8,11},{9,8},{10,9... | collective-permute-start | bytes 1179656 | tf_op jit(solution)/shard_map/ppermute | solution.py:29
  18.0 11.1 %collective-permute-start.6 = (f32[3,16,16,128]{3,2,1,0:T(8,128)S(1)}, f32[3,16,16,128]{3,2,1,0:T(8,128)}, u32[]{:S(2)}, u32[]{:S(2)}) collective-permute-start(f32[3,16,16,128]{3,2,1,0:T(8,128)S(1)} %collective-permute-done.5.own), channel_id=1, source_target_pairs={{0,1},{1,2},{2,3},{3,0},{4,5},{5,6},{6,7},{7,4},{8,9},{9,10},{10,1... | collective-permute-start | bytes 1179656 | tf_op jit(solution)/shard_map/ppermute | solution.py:29
  18.0 1.0 %copy-start = (f32[3,16,16,128]{3,2,1,0:T(8,128)S(1)}, f32[3,16,16,128]{3,2,1,0:T(8,128)}, u32[]{:S(2)}) copy-start(f32[3,16,16,128]{3,2,1,0:T(8,128)} %own.1) | copy-start | bytes 1179652
  19.0 1.0 %copy-start.2 = (f32[3,16,16,128]{3,2,1,0:T(8,128)S(1)}, f32[3,16,16,128]{3,2,1,0:T(8,128)}, u32[]{:S(2)}) copy-start(f32[3,16,16,128]{3,2,1,0:T(8,128)} %copy-done.1) | copy-start | bytes 1179652
  26.7 10.1 %collective-permute-start.4 = (f32[3,16,16,128]{3,2,1,0:T(8,128)S(1)}, f32[3,16,16,128]{3,2,1,0:T(8,128)S(1)}, u32[]{:S(2)}, u32[]{:S(2)}) collective-permute-start(f32[3,16,16,128]{3,2,1,0:T(8,128)S(1)} %collective-permute-done.refs_1_), channel_id=1, source_target_pairs={{0,3},{1,0},{2,1},{3,2},{4,7},{5,4},{6,5},{7,6},{8,11},{9,8},{10,9... | collective-permute-start | bytes 1179656 | tf_op jit(solution)/shard_map/ppermute | solution.py:29
  27.6 10.3 %collective-permute-start.3 = (f32[3,16,16,128]{3,2,1,0:T(8,128)S(1)}, f32[3,16,16,128]{3,2,1,0:T(8,128)S(1)}, u32[]{:S(2)}, u32[]{:S(2)}) collective-permute-start(f32[3,16,16,128]{3,2,1,0:T(8,128)S(1)} %collective-permute-done.refs_1_), channel_id=1, source_target_pairs={{0,1},{1,2},{2,3},{3,0},{4,5},{5,6},{6,7},{7,4},{8,9},{9,10},{10,1... | collective-permute-start | bytes 1179656 | tf_op jit(solution)/shard_map/ppermute | solution.py:29
  40.2 4.1 %copy-start.3 = (f32[128,128]{1,0:T(8,128)S(1)}, f32[128,128]{1,0:T(8,128)}, u32[]{:S(2)}) copy-start(f32[128,128]{1,0:T(8,128)} %constant.15.clone.band) | copy-start | bytes 196612
  40.2 8.3 %collective-permute-start.8 = (f32[5,32,256]{2,1,0:T(8,128)S(1)}, f32[5,32,256]{2,1,0:T(8,128)S(1)}, u32[]{:S(2)}, u32[]{:S(2)}) collective-permute-start(f32[5,32,256]{2,1,0:T(8,128)S(1)} %get-tuple-element.29), channel_id=1, source_target_pairs={{0,4},{4,0},{1,5},{5,1},{2,6},{6,2},{3,7},{7,3},{8,12},{12,8},{9,1... | collective-permute-start | bytes 491528 | tf_op jit(solution)/shard_map/ppermute | solution.py:411
  43.5 5.0 %collective-permute-start.9 = (f32[4,32,256]{2,1,0:T(8,128)S(1)}, f32[4,32,256]{2,1,0:T(8,128)S(1)}, u32[]{:S(2)}, u32[]{:S(2)}) collective-permute-start(f32[4,32,256]{2,1,0:T(8,128)S(1)} %get-tuple-element.30), channel_id=1, source_target_pairs={{0,4},{4,0},{1,5},{5,1},{2,6},{6,2},{3,7},{7,3},{8,12},{12,8},{9,1... | collective-permute-start | bytes 393224 | tf_op jit(solution)/shard_map/ppermute | solution.py:411
  44.3 4.3 %copy-start.4 = (f32[128,32]{1,0:T(8,128)S(1)}, f32[128,32]{1,0:T(8,128)}, u32[]{:S(2)}) copy-start(f32[128,32]{1,0:T(8,128)} %constant.16.clone.band) | copy-start | bytes 49156

commit v7 on v6

--- a/solution.py
+++ b/solution.py
@@ -305,7 +305,7 @@
         out[group, 6:ROWS, here] = jnp.zeros((ROWS - 6, BLOCK), F32)
         return carry
 
-    lax.fori_loop(0, out.shape[0] * blocks, sample, 0, unroll=4)
+    lax.fori_loop(0, out.shape[0] * blocks, sample, 0, unroll=16)
 
 
 def samples(partial, first, second, band, w_high, w_low, w_y, groups):
@@ -370,7 +370,7 @@
 def return_kernel(owners, back, slot, owner, out):
     count = owner.shape[1]
     picked = jnp.zeros((owners * ROWS, count), F32)
-    for part in split3(back[...]):
+    for part in split2(back[...]):
         picked = picked + jnp.dot(part, slot[...], preferred_element_type=F32)
     target = owner[...]
     total = jnp.zeros((ROWS, count), F32)
@@ -427,19 +427,20 @@
     folded = capacity % BLOCK != 0
 
     row = lax.broadcasted_iota(jnp.int32, (8, count), 0)
-    cell = (cell_z * size_x + cell_x) * size_y + cell_y
+    flat = (jnp.broadcast_to(k.reshape(1, count), (8, count)) for k in (owner, cell_x, cell_y, cell_z))
+    named, in_x, in_y, in_z = flat
+    cell = (in_z * size_x + in_x) * size_y + in_y
     record = jnp.pad(query_weights, ((2, 3), (0, 0)))
-    record = jnp.where(row == 1, cell[None].astype(F32), record)
-    record = jnp.where(row == 0, owner.reshape(1, count).astype(F32), record)
+    record = jnp.where(row > 1, record, jnp.where(row == 1, cell, named).astype(F32))
     sent, slot, target = route(record, owners, capacity)
 
     right = shifted(velocity, "gx", -1)
     left = shifted(after(velocity, record), "gx", 1)
-    own_halo = neighbours(velocity, "gz")
-    right = relayed(after(right, own_halo, sent))
+    own_halo = shifted(velocity, "gz", 1), shifted(after(velocity, record), "gz", -1)
+    right = relayed(right)
     asked = lax.all_to_all(sent, ("gx", "gy"), split_axis=0, concat_axis=0, tiled=True)
     own_z = along_z(own_halo[0], velocity, own_halo[1])
-    left = relayed(after(left, own_z, asked))
+    left = (shifted(after(left, own_z, asked), "gz", 1), left, shifted(own_halo[1], "gx", 1))
     partial = along_x_first(own_z, along_z(*right))
     if folded:
         asked = asked.transpose(1, 0, 2).reshape(1, 4, owners * capacity)

time: 69.7 us -> 66.5 us (0.954)
  blocking collectives: 12.6 us -> 10.7 us
  Pallas kernels: 25.9 us -> 25.1 us
  starting transfers between devices: 16 us -> 16.7 us
    all_to_all x1, waiting for transfers between devices: 4.5 us -> 1.71 us  [on_device(): lax.all_to_all(sent, ('gx', 'gy'), split_axis=0, concat_axis=0, tiled=True)]
    ppermute x8, waiting for transfers between devices: 3.35 us -> 5.63 us  [shifted(): lax.ppermute(x, axis, [(i, (i + step) % devices) for i in range(devices)])]
    all_to_all x1, blocking collectives: 12.6 us -> 10.7 us  [on_device(): lax.all_to_all(values, ('gx', 'gy'), split_axis=0, concat_axis=0, tiled=T...]
    convert_element_type x2 -> x0, other arithmetic: 1.42 us -> none  [the longest x1 0.73 us: on_device(): record = jnp.where(row == 1, cell[None].astype(F32), record)]
    add x0 -> x1, other arithmetic: none -> 0.72 us  [on_device(): cell = (in_z * size_x + in_x) * size_y + in_y]
  transfers between devices with their start and end apart: 11 -> 11, of which waited for: 4 -> 5; matrix products, arithmetic and copies ran while one was open for 3% -> 2% of each run, Pallas kernels for 22% -> 24%
where the time goes in v7:
time: 66.5 us; the launch traced here: 66 us
  Pallas kernels  25.1 us (38%)
  starting transfers between devices  16.7 us (25%)
  blocking collectives  10.7 us (16%)
  waiting for transfers between devices  9.19 us (14%)
  local copies, waits for them, and re-layouts  2.77 us (4%)
  other arithmetic  1.52 us (2%)
    all_to_all x1, blocking collectives, on_device(): lax.all_to_all(values, ('gx', 'gy'), split_axis=0, concat_axis=0, tiled=T...  10.7 us
    ppermute x8, starting transfers between devices, shifted(): lax.ppermute(x, axis, [(i, (i + step) % devices) for i in range(devices)])  8.51 us
    pallas_call x1, Pallas kernels, samples(): pl.pallas_call(sample_kernel, out_shape=jax.ShapeDtypeStruct((groups, ROW...  6.11 us
    all_to_all x1, starting transfers between devices, on_device(): lax.all_to_all(sent, ('gx', 'gy'), split_axis=0, concat_axis=0, tiled=True)  6.02 us
    ppermute x8, waiting for transfers between devices, shifted(): lax.ppermute(x, axis, [(i, (i + step) % devices) for i in range(devices)])  5.63 us
    pallas_call x2, Pallas kernels, along_z(): pl.pallas_call(z_kernel, out_shape=jax.ShapeDtypeStruct((9, z, x, y), F32...  5.51 us
    pallas_call x2, Pallas kernels, along_x_last(): pl.pallas_call(kernel, out_shape=(jax.ShapeDtypeStruct((count, z * x, y),...  4.19 us
    unnamed x10, local copies, waits for them, and re-layouts  2.77 us
  transfers between devices with their start and end apart: 11, of which 5 were waited for; matrix products, arithmetic and copies ran while one was open for 2% of the time, Pallas kernels for 24%

profile of v7, /device:TPU:0, one launch (start us, length us, event | category | flops | bytes accessed | tf_op | source)
XLA Modules:
  0.0 66.0 jit_solution(8387958210355026576)
XLA Ops:
  0.0 5.0 %collective-permute-start.5 = (f32[3,16,16,128]{3,2,1,0:T(8,128)}, f32[3,16,16,128]{3,2,1,0:T(8,128)S(1)}, u32[]{:S(2)}, u32[]{:S(2)}) collective-permute-start(f32[3,16,16,128]{3,2,1,0:T(8,128)} %own.1), channel_id=1, source_target_pairs={{0,24},{8,0},{16,8},{24,16},{1,25},{9,1},{17,9},{25,17},{2,26},{10... | collective-permute-start | bytes 1179656 | tf_op jit(solution)/shard_map/ppermute | solution.py:29
  5.8 0.8 %convert_select_fusion.refs_0_ = f32[8,1024]{1,0:T(8,128)S(1)} fusion(f32[3,1024]{1,0:T(4,128)} %param.13, s32[1024]{0:T(1024)} %bitcast.3, s32[1024]{0:T(1024)S(1)} %multiply_add_fusion, pred[8]{0:T(512)(128)(4,1)S(1)} %get-tuple-element.31, pred[8]{0:T(512)(128)(4,1)S(1)} %get-tuple-element.32), kind=kLoop, calls=%fused_computation | loop fusion | flops 24576 | bytes 53264 | tf_op jit(solution)/shard_map/jit(_where)/select_n | solution.py:434
  7.3 2.1 %shard_map.83 = (f32[8,4,512]{2,1,0:T(4,128)}, bf16[512,1024]{1,0:T(8,128)(2,1)S(1)}, s32[1,1024]{1,0:T(1,128)S(1)}) custom-call(f32[8,1024]{1,0:T(8,128)S(1)} %convert_select_fusion.refs_0_), custom_call_target="tpu_custom_call" | custom-call | flops 83886080 | bytes 163840 | tf_op jit(solution)/shard_map/pallas_call | solution.py:356
  9.4 6.0 %all-to-all-start = ((f32[8,4,512]{2,1,0:T(4,128)}), f32[8,4,512]{2,1,0:T(4,128)S(1)}, u32[]{:S(2)}, u32[]{:S(2)}) async-start(f32[8,4,512]{2,1,0:T(4,128)} %get-tuple-element.19), calls=%async_computation | async-start | bytes 131072 | tf_op jit(solution)/shard_map/all_to_all | solution.py:441
  15.4 1.2 %collective-permute-start.7 = (f32[3,16,16,128]{3,2,1,0:T(8,128)S(1)}, f32[3,16,16,128]{3,2,1,0:T(8,128)}, u32[]{:S(2)}, u32[]{:S(2)}) collective-permute-start(f32[3,16,16,128]{3,2,1,0:T(8,128)S(1)} %collective-permute-done.5.own), channel_id=1, source_target_pairs={{0,3},{1,0},{2,1},{3,2},{4,7},{5,4},{6,5},{7,6},{8,11},{9,8},{10,9... | collective-permute-start | bytes 1179656 | tf_op jit(solution)/shard_map/ppermute | solution.py:29
  16.7 1.5 %collective-permute-done.1.before = f32[3,16,16,128]{3,2,1,0:T(8,128)S(1)} collective-permute-done((f32[3,16,16,128]{3,2,1,0:T(8,128)}, f32[3,16,16,128]{3,2,1,0:T(8,128)S(1)}, u32[]{:S(2)}, u32[]{:S(2)}) %collective-permute-start.1) | collective-permute-done | bytes 393248 | tf_op jit(solution)/shard_map/ppermute | solution.py:29
  18.3 0.8 %copy-done.1 = f32[3,16,16,128]{3,2,1,0:T(8,128)} copy-done((f32[3,16,16,128]{3,2,1,0:T(8,128)}, f32[3,16,16,128]{3,2,1,0:T(8,128)S(1)}, u32[]{:S(2)}) %copy-start.1) | copy-done | bytes 393240
  19.0 1.0 %copy-done = f32[3,16,16,128]{3,2,1,0:T(8,128)S(1)} copy-done((f32[3,16,16,128]{3,2,1,0:T(8,128)S(1)}, f32[3,16,16,128]{3,2,1,0:T(8,128)}, u32[]{:S(2)}) %copy-start) | copy-done | bytes 393240
  20.0 1.0 %copy-done.2 = f32[3,16,16,128]{3,2,1,0:T(8,128)S(1)} copy-done((f32[3,16,16,128]{3,2,1,0:T(8,128)S(1)}, f32[3,16,16,128]{3,2,1,0:T(8,128)}, u32[]{:S(2)}) %copy-start.2) | copy-done | bytes 393240
  21.0 2.2 %shard_map.82.own = f32[9,16,16,128]{3,2,1,0:T(8,128)S(1)} custom-call(f32[3,16,16,128]{3,2,1,0:T(8,128)S(1)} %copy-done.2, f32[3,16,16,128]{3,2,1,0:T(8,128)S(1)} %copy-done, f32[3,16,16,128]{3,2,1,0:T(8,128)S(1)} %collective-permute-done.2.after), custom_call_target="tpu_custom_call" | custom-call | flops 19464192 | bytes 2752512 | tf_op jit(solution)/shard_map/pallas_call | solution.py:103
  23.2 1.7 %all-to-all-done.refs_0_ = f32[8,4,512]{2,1,0:T(4,128)S(1)} async-done(((f32[8,4,512]{2,1,0:T(4,128)}), f32[8,4,512]{2,1,0:T(4,128)S(1)}, u32[]{:S(2)}, u32[]{:S(2)}) %all-to-all-start) | async-done | bytes 65568 | tf_op jit(solution)/shard_map/all_to_all | solution.py:441
  24.9 1.5 %collective-permute-start.4 = (f32[3,16,16,128]{3,2,1,0:T(8,128)S(1)}, f32[3,16,16,128]{3,2,1,0:T(8,128)S(1)}, u32[]{:S(2)}, u32[]{:S(2)}) collective-permute-start(f32[3,16,16,128]{3,2,1,0:T(8,128)S(1)} %collective-permute-done.2.after), channel_id=1, source_target_pairs={{0,8},{8,16},{16,24},{24,0},{1,9},{9,17},{17,25},{25,1},{2,10},{10... | collective-permute-start | bytes 1179656 | tf_op jit(solution)/shard_map/ppermute | solution.py:29
  26.5 1.5 %shard_map.86 = (bf16[256,4096]{1,0:T(8,128)(2,1)S(1)}, bf16[256,4096]{1,0:T(8,128)(2,1)S(1)}, f32[128,4096]{1,0:T(8,128)S(1)}) custom-call(f32[8,4,512]{2,1,0:T(4,128)S(1)} %all-to-all-done.refs_0_), custom_call_target="tpu_custom_call" | custom-call | flops 8192000 | bytes 6553600 | tf_op jit(solution)/shard_map/pallas_call | solution.py:235
  28.0 3.3 %shard_map.84.right = f32[9,16,16,128]{3,2,1,0:T(8,128)S(1)} custom-call(f32[3,16,16,128]{3,2,1,0:T(8,128)} %collective-permute-done.6.before, f32[3,16,16,128]{3,2,1,0:T(8,128)S(1)} %collective-permute-done.5.own, f32[3,16,16,128]{3,2,1,0:T(8,128)} %collective-permute-done.7.after), custom_call_target="tpu_custom_call" | custom-call | flops 19464192 | bytes 2752512 | tf_op jit(solution)/shard_map/pallas_call | solution.py:103
  31.3 2.1 %shard_map.85.refs_3_ = f32[9,256,128]{2,1,0:T(8,128)S(1)} custom-call(f32[9,16,16,128]{3,2,1,0:T(8,128)S(1)} %shard_map.82.own, f32[9,16,16,128]{3,2,1,0:T(8,128)S(1)} %shard_map.84.right), custom_call_target="tpu_custom_call" | custom-call | flops 19464192 | bytes 3932160 | tf_op jit(solution)/shard_map/pallas_call | solution.py:136
  33.4 4.0 %collective-permute-done.4.refs_2_ = f32[3,16,16,128]{3,2,1,0:T(8,128)S(1)} collective-permute-done((f32[3,16,16,128]{3,2,1,0:T(8,128)S(1)}, f32[3,16,16,128]{3,2,1,0:T(8,128)S(1)}, u32[]{:S(2)}, u32[]{:S(2)}) %collective-permute-start.4) | collective-permute-done | bytes 393248 | tf_op jit(solution)/shard_map/ppermute | solution.py:29
  37.4 2.3 %shard_map.87 = (f32[5,256,128]{2,1,0:T(8,128)S(1)}, f32[5,32,256]{2,1,0:T(8,128)S(1)}) custom-call(f32[3,16,16,128]{3,2,1,0:T(8,128)S(1)} %collective-permute-done.3.refs_0_, f32[3,16,16,128]{3,2,1,0:T(8,128)S(1)} %collective-permute-done.refs_1_, f32[3,16,16,128]{3,2,1,0:T(8,128)S(1)} %collective-permute-done.4.refs_2_, f32[9,256,128]{2,1,0:T(8,128)S(1)} %shard_map.85.refs_3_), custom_call_target="tpu_custom_call" | custom-call | flops 16384000 | bytes 5242880 | tf_op jit(solution)/shard_map/pallas_call | solution.py:187
  39.7 1.5 %collective-permute-start.8 = (f32[5,32,256]{2,1,0:T(8,128)S(1)}, f32[5,32,256]{2,1,0:T(8,128)S(1)}, u32[]{:S(2)}, u32[]{:S(2)}) collective-permute-start(f32[5,32,256]{2,1,0:T(8,128)S(1)} %get-tuple-element.27), channel_id=1, source_target_pairs={{0,4},{4,0},{1,5},{5,1},{2,6},{6,2},{3,7},{7,3},{8,12},{12,8},{9,1... | collective-permute-start | bytes 491528 | tf_op jit(solution)/shard_map/ppermute | solution.py:411
  41.2 1.9 %shard_map.88 = (f32[4,256,128]{2,1,0:T(8,128)S(1)}, f32[4,32,256]{2,1,0:T(8,128)S(1)}) custom-call(f32[3,16,16,128]{3,2,1,0:T(8,128)S(1)} %collective-permute-done.3.refs_0_, f32[3,16,16,128]{3,2,1,0:T(8,128)S(1)} %collective-permute-done.refs_1_, f32[3,16,16,128]{3,2,1,0:T(8,128)S(1)} %collective-permute-done.4.refs_2_, f32[9,256,128]{2,1,0:T(8,128)S(1)} %shard_map.85.refs_3_), custom_call_target="tpu_custom_call" | custom-call | flops 13107200 | bytes 5242880 | tf_op jit(solution)/shard_map/pallas_call | solution.py:187
  43.8 2.5 %shard_map.89.partial = f32[9,128,256]{2,1,0:T(8,128)S(1)} custom-call(f32[128,128]{1,0:T(8,128)S(1)} %copy-done.3, f32[5,256,128]{2,1,0:T(8,128)S(1)} %get-tuple-element.25.refs_0_, f32[4,256,128]{2,1,0:T(8,128)S(1)} %get-tuple-element.26.refs_1_), custom_call_target="tpu_custom_call" | custom-call | flops 452984832 | bytes 2359296 | tf_op jit(solution)/shard_map/pallas_call | solution.py:267
  46.3 1.8 %collective-permute-done.9.second = f32[4,32,256]{2,1,0:T(8,128)S(1)} collective-permute-done((f32[4,32,256]{2,1,0:T(8,128)S(1)}, f32[4,32,256]{2,1,0:T(8,128)S(1)}, u32[]{:S(2)}, u32[]{:S(2)}) %collective-permute-start.9) | collective-permute-done | bytes 131104 | tf_op jit(solution)/shard_map/ppermute | solution.py:411
  48.1 6.1 %shard_map.90 = f32[8,8,512]{2,1,0:T(8,128)S(1)} custom-call(f32[9,128,256]{2,1,0:T(8,128)S(1)} %shard_map.89.partial, f32[5,32,256]{2,1,0:T(8,128)S(1)} %collective-permute-done.8.first, f32[4,32,256]{2,1,0:T(8,128)S(1)} %collective-permute-done.9.second, f32[128,32]{1,0:T(8,128)S(1)} %copy-done.4, bf16[256,4096]{1,0:T(8,128)(2,1)S(1)} %get-tuple-element.21.w_high, ...), custom_call_target="tpu_custom_call" | custom-call | flops 4831838208 | bytes 8388608 | tf_op jit(solution)/shard_map/pallas_call | solution.py:314
  54.2 10.7 %all_to_all.10 = f32[8,8,512]{2,1,0:T(8,128)S(1)} all-to-all(f32[8,8,512]{2,1,0:T(8,128)S(1)} %shard_map.90), channel_id=1, replica_groups=mesh['gx'=4,'gy'=2,'gz'=4] {'gx','gy'}, dimensions={0} | all-to-all | bytes 262144 | tf_op jit(solution)/shard_map/all_to_all | solution.py:458
  64.9 1.1 %shard_map.91 = f32[6,1024]{1,0:T(8,128)} custom-call(f32[64,512]{1,0:T(8,128)S(1)} %bitcast.2, bf16[512,1024]{1,0:T(8,128)(2,1)S(1)} %get-tuple-element.29.refs_1_, s32[1,1024]{1,0:T(1,128)S(1)} %get-tuple-element.30.refs_2_), custom_call_target="tpu_custom_call" | custom-call | flops 201326592 | bytes 102400 | tf_op jit(solution)/shard_map/pallas_call | solution.py:388
  (22 shorter events, 2.2 us)
Async XLA Ops:
  0.0 15.4 %collective-permute-start.5 = (f32[3,16,16,128]{3,2,1,0:T(8,128)}, f32[3,16,16,128]{3,2,1,0:T(8,128)S(1)}, u32[]{:S(2)}, u32[]{:S(2)}) collective-permute-start(f32[3,16,16,128]{3,2,1,0:T(8,128)} %own.1), channel_id=1, source_target_pairs={{0,24},{8,0},{16,8},{24,16},{1,25},{9,1},{17,9},{25,17},{2,26},{10... | collective-permute-start | bytes 1179656 | tf_op jit(solution)/shard_map/ppermute | solution.py:29
  6.6 10.2 %collective-permute-start.2 = (f32[3,16,16,128]{3,2,1,0:T(8,128)}, f32[3,16,16,128]{3,2,1,0:T(8,128)S(1)}, u32[]{:S(2)}, u32[]{:S(2)}) collective-permute-start(f32[3,16,16,128]{3,2,1,0:T(8,128)} %own.1), channel_id=1, source_target_pairs={{0,3},{1,0},{2,1},{3,2},{4,7},{5,4},{6,5},{7,6},{8,11},{9,8},{10,9... | collective-permute-start | bytes 1179656 | tf_op jit(solution)/shard_map/ppermute | solution.py:29
  7.3 11.0 %collective-permute-start.1 = (f32[3,16,16,128]{3,2,1,0:T(8,128)}, f32[3,16,16,128]{3,2,1,0:T(8,128)S(1)}, u32[]{:S(2)}, u32[]{:S(2)}) collective-permute-start(f32[3,16,16,128]{3,2,1,0:T(8,128)} %own.1), channel_id=1, source_target_pairs={{0,1},{1,2},{2,3},{3,0},{4,5},{5,6},{6,7},{7,4},{8,9},{9,10},{10,1... | collective-permute-start | bytes 1179656 | tf_op jit(solution)/shard_map/ppermute | solution.py:29
  7.3 17.7 %collective-permute-start = (f32[3,16,16,128]{3,2,1,0:T(8,128)}, f32[3,16,16,128]{3,2,1,0:T(8,128)S(1)}, u32[]{:S(2)}, u32[]{:S(2)}) collective-permute-start(f32[3,16,16,128]{3,2,1,0:T(8,128)} %own.1), channel_id=1, source_target_pairs={{0,8},{8,16},{16,24},{24,0},{1,9},{9,17},{17,25},{25,1},{2,10},{10... | collective-permute-start | bytes 1179656 | tf_op jit(solution)/shard_map/ppermute | solution.py:29
  9.4 15.6 %all-to-all-start = ((f32[8,4,512]{2,1,0:T(4,128)}), f32[8,4,512]{2,1,0:T(4,128)S(1)}, u32[]{:S(2)}, u32[]{:S(2)}) async-start(f32[8,4,512]{2,1,0:T(4,128)} %get-tuple-element.19), calls=%async_computation | async-start | bytes 131072 | tf_op jit(solution)/shard_map/all_to_all | solution.py:441
  15.4 12.6 %collective-permute-start.7 = (f32[3,16,16,128]{3,2,1,0:T(8,128)S(1)}, f32[3,16,16,128]{3,2,1,0:T(8,128)}, u32[]{:S(2)}, u32[]{:S(2)}) collective-permute-start(f32[3,16,16,128]{3,2,1,0:T(8,128)S(1)} %collective-permute-done.5.own), channel_id=1, source_target_pairs={{0,3},{1,0},{2,1},{3,2},{4,7},{5,4},{6,5},{7,6},{8,11},{9,8},{10,9... | collective-permute-start | bytes 1179656 | tf_op jit(solution)/shard_map/ppermute | solution.py:29
  16.6 11.4 %collective-permute-start.6 = (f32[3,16,16,128]{3,2,1,0:T(8,128)S(1)}, f32[3,16,16,128]{3,2,1,0:T(8,128)}, u32[]{:S(2)}, u32[]{:S(2)}) collective-permute-start(f32[3,16,16,128]{3,2,1,0:T(8,128)S(1)} %collective-permute-done.5.own), channel_id=1, source_target_pairs={{0,1},{1,2},{2,3},{3,0},{4,5},{5,6},{6,7},{7,4},{8,9},{9,10},{10,1... | collective-permute-start | bytes 1179656 | tf_op jit(solution)/shard_map/ppermute | solution.py:29
  18.3 0.8 %copy-start.1 = (f32[3,16,16,128]{3,2,1,0:T(8,128)}, f32[3,16,16,128]{3,2,1,0:T(8,128)S(1)}, u32[]{:S(2)}) copy-start(f32[3,16,16,128]{3,2,1,0:T(8,128)S(1)} %collective-permute-done.1.before) | copy-start | bytes 1179652
  19.0 1.0 %copy-start = (f32[3,16,16,128]{3,2,1,0:T(8,128)S(1)}, f32[3,16,16,128]{3,2,1,0:T(8,128)}, u32[]{:S(2)}) copy-start(f32[3,16,16,128]{3,2,1,0:T(8,128)} %own.1) | copy-start | bytes 1179652
  20.0 1.0 %copy-start.2 = (f32[3,16,16,128]{3,2,1,0:T(8,128)S(1)}, f32[3,16,16,128]{3,2,1,0:T(8,128)}, u32[]{:S(2)}) copy-start(f32[3,16,16,128]{3,2,1,0:T(8,128)} %copy-done.1) | copy-start | bytes 1179652
  24.9 12.4 %collective-permute-start.4 = (f32[3,16,16,128]{3,2,1,0:T(8,128)S(1)}, f32[3,16,16,128]{3,2,1,0:T(8,128)S(1)}, u32[]{:S(2)}, u32[]{:S(2)}) collective-permute-start(f32[3,16,16,128]{3,2,1,0:T(8,128)S(1)} %collective-permute-done.2.after), channel_id=1, source_target_pairs={{0,8},{8,16},{16,24},{24,0},{1,9},{9,17},{17,25},{25,1},{2,10},{10... | collective-permute-start | bytes 1179656 | tf_op jit(solution)/shard_map/ppermute | solution.py:29
  26.5 10.9 %collective-permute-start.3 = (f32[3,16,16,128]{3,2,1,0:T(8,128)S(1)}, f32[3,16,16,128]{3,2,1,0:T(8,128)S(1)}, u32[]{:S(2)}, u32[]{:S(2)}) collective-permute-start(f32[3,16,16,128]{3,2,1,0:T(8,128)S(1)} %collective-permute-done.refs_1_), channel_id=1, source_target_pairs={{0,1},{1,2},{2,3},{3,0},{4,5},{5,6},{6,7},{7,4},{8,9},{9,10},{10,1... | collective-permute-start | bytes 1179656 | tf_op jit(solution)/shard_map/ppermute | solution.py:29
  39.7 4.1 %copy-start.3 = (f32[128,128]{1,0:T(8,128)S(1)}, f32[128,128]{1,0:T(8,128)}, u32[]{:S(2)}) copy-start(f32[128,128]{1,0:T(8,128)} %constant.13.clone.band) | copy-start | bytes 196612
  39.7 8.4 %collective-permute-start.8 = (f32[5,32,256]{2,1,0:T(8,128)S(1)}, f32[5,32,256]{2,1,0:T(8,128)S(1)}, u32[]{:S(2)}, u32[]{:S(2)}) collective-permute-start(f32[5,32,256]{2,1,0:T(8,128)S(1)} %get-tuple-element.27), channel_id=1, source_target_pairs={{0,4},{4,0},{1,5},{5,1},{2,6},{6,2},{3,7},{7,3},{8,12},{12,8},{9,1... | collective-permute-start | bytes 491528 | tf_op jit(solution)/shard_map/ppermute | solution.py:411
  43.1 5.0 %collective-permute-start.9 = (f32[4,32,256]{2,1,0:T(8,128)S(1)}, f32[4,32,256]{2,1,0:T(8,128)S(1)}, u32[]{:S(2)}, u32[]{:S(2)}) collective-permute-start(f32[4,32,256]{2,1,0:T(8,128)S(1)} %get-tuple-element.28), channel_id=1, source_target_pairs={{0,4},{4,0},{1,5},{5,1},{2,6},{6,2},{3,7},{7,3},{8,12},{12,8},{9,1... | collective-permute-start | bytes 393224 | tf_op jit(solution)/shard_map/ppermute | solution.py:411
  43.8 4.4 %copy-start.4 = (f32[128,32]{1,0:T(8,128)S(1)}, f32[128,32]{1,0:T(8,128)}, u32[]{:S(2)}) copy-start(f32[128,32]{1,0:T(8,128)} %constant.14.clone.band) | copy-start | bytes 49156

commit v8 on v7

--- a/solution.py
+++ b/solution.py
@@ -246,42 +246,46 @@
     )(asked)
 
 
-def y_kernel(band, *refs):
-    *parts, out = refs
-    start = 0
-    for fields in parts:
-
-        def filtered(f, carry, fields=fields, start=start):
-            out[start + f] = lax.dot_general(
-                band[...], fields[f], (((1,), (1,)), ((), ())),
-                precision=lax.Precision.HIGHEST, preferred_element_type=F32,
+def y_kernel(band, fields, *refs):
+    out = refs[-1]
+
+    def filtered(f, carry):
+        total = lax.dot_general(
+            band[...], fields[f], (((1,), (1,)), ((), ())),
+            precision=lax.Precision.HIGHEST, preferred_element_type=F32,
+        )
+        if len(refs) > 1:
+            total = total + jnp.dot(
+                refs[0][...], refs[1][f], precision=lax.Precision.HIGHEST, preferred_element_type=F32
             )
-            return carry
-
-        lax.fori_loop(0, fields.shape[0], filtered, 0)
-        start = start + fields.shape[0]
-
-
-def along_y(band, parts):
-    _, cells, size_y = parts[0].shape
+        out[f] = total
+        return carry
+
+    lax.fori_loop(0, fields.shape[0], filtered, 0)
+
+
+def along_y(band, fields, *edges):
+    count, cells, size_y = fields.shape
     return pl.pallas_call(
         y_kernel,
-        out_shape=jax.ShapeDtypeStruct((9, size_y, cells), F32),
-        in_specs=[WHOLE] * (1 + len(parts)),
+        out_shape=jax.ShapeDtypeStruct((count, size_y, cells), F32),
+        in_specs=[WHOLE] * (2 + len(edges)),
         out_specs=WHOLE,
         compiler_params=PARAMS,
-        cost_estimate=pl.CostEstimate(flops=9 * 12 * size_y * size_y * cells, bytes_accessed=18 * cells * size_y * 4, transcendentals=0),
-    )(band, *parts)
-
-
-def sample_kernel(partial, first, second, band, w_high, w_low, w_y, out, field_high, field_low):
+        cost_estimate=pl.CostEstimate(flops=count * 12 * size_y * size_y * cells, bytes_accessed=2 * count * cells * size_y * 4, transcendentals=0),
+    )(band, fields, *edges)
+
+
+def sample_kernel(first, partial, strips, band, w_high, w_low, w_y, out, field_high, field_low):
     size_y = partial.shape[1]
     blocks = out.shape[2] // BLOCK
 
     def smooth(f):
-        strips = first[f] if f < first.shape[0] else second[f - first.shape[0]]
-        return partial[f] + jnp.dot(
-            band[...], strips, precision=lax.Precision.HIGHEST, preferred_element_type=F32
+        done = first.shape[0]
+        if f < done:
+            return first[f]
+        return partial[f - done] + jnp.dot(
+            band[...], strips[f - done], precision=lax.Precision.HIGHEST, preferred_element_type=F32
         )
 
     mean = [smooth(k) for k in range(3)]
@@ -308,7 +312,7 @@
     lax.fori_loop(0, out.shape[0] * blocks, sample, 0, unroll=16)
 
 
-def samples(partial, first, second, band, w_high, w_low, w_y, groups):
+def samples(first, partial, strips, band, w_high, w_low, w_y, groups):
     _, size_y, cells = partial.shape
     count = w_y.shape[1]
     return pl.pallas_call(
@@ -319,7 +323,7 @@
         scratch_shapes=[pltpu.VMEM((6 * size_y, cells), BF16), pltpu.VMEM((6 * size_y, cells), BF16)],
         compiler_params=PARAMS,
         cost_estimate=pl.CostEstimate(flops=6 * size_y * cells * count * 6, bytes_accessed=8 * 1024 * 1024, transcendentals=0),
-    )(partial, first, second, band, w_high, w_low, w_y)
+    )(first, partial, strips, band, w_high, w_low, w_y)
 
 
 def route_kernel(owners, capacity, record, out, slot_out, target_out):
@@ -451,8 +455,10 @@
     first_strips = y_strips(edges)
     second, edges = along_x_last(tuple(range(5, 9)), *left, partial)
     second_strips = y_strips(edges)
-    partial = along_y(jnp.asarray(band_own), (first, second))
-    values = samples(partial, first_strips, second_strips, jnp.asarray(band_strips), *weights, asked.shape[0])
+    band_own, band_strips = jnp.asarray(band_own), jnp.asarray(band_strips)
+    partial = along_y(band_own, second)
+    whole = along_y(band_own, after(first, partial), band_strips, first_strips)
+    values = samples(whole, partial, second_strips, band_strips, *weights, asked.shape[0])
     if folded:
         values = values.reshape(ROWS, owners, capacity).transpose(1, 0, 2)
     back = lax.all_to_all(values, ("gx", "gy"), split_axis=0, concat_axis=0, tiled=True)

time: 66.5 us -> 66.2 us (level)
    pallas_call x1 -> x2, Pallas kernels: 2.5 us -> 2.89 us  [along_y(): pl.pallas_call(y_kernel, out_shape=jax.ShapeDtypeStruct((count, size_y, c...]
  transfers between devices with their start and end apart: 11 -> 11, of which waited for: 5 -> 6; matrix products, arithmetic and copies ran while one was open for 2% -> 2% of each run, Pallas kernels for 24% -> 24%
where the time goes in v8:
time: 66.2 us; the launch traced here: 65.8 us
  Pallas kernels  24.8 us (37%)
  starting transfers between devices  16.7 us (25%)
  blocking collectives  11.1 us (17%)
  waiting for transfers between devices  8.77 us (13%)
  local copies, waits for them, and re-layouts  2.77 us (4%)
  other arithmetic  1.52 us (2%)
    all_to_all x1, blocking collectives, on_device(): lax.all_to_all(values, ('gx', 'gy'), split_axis=0, concat_axis=0, tiled=T...  11.1 us
    ppermute x8, starting transfers between devices, shifted(): lax.ppermute(x, axis, [(i, (i + step) % devices) for i in range(devices)])  8.51 us
    all_to_all x1, starting transfers between devices, on_device(): lax.all_to_all(sent, ('gx', 'gy'), split_axis=0, concat_axis=0, tiled=True)  6.02 us
    ppermute x8, waiting for transfers between devices, shifted(): lax.ppermute(x, axis, [(i, (i + step) % devices) for i in range(devices)])  5.62 us
    pallas_call x2, Pallas kernels, along_z(): pl.pallas_call(z_kernel, out_shape=jax.ShapeDtypeStruct((9, z, x, y), F32...  5.51 us
    pallas_call x1, Pallas kernels, samples(): pl.pallas_call(sample_kernel, out_shape=jax.ShapeDtypeStruct((groups, ROW...  5.45 us
    pallas_call x2, Pallas kernels, along_x_last(): pl.pallas_call(kernel, out_shape=(jax.ShapeDtypeStruct((count, z * x, y),...  4.19 us
    pallas_call x2, Pallas kernels, along_y(): pl.pallas_call(y_kernel, out_shape=jax.ShapeDtypeStruct((count, size_y, c...  2.89 us
  transfers between devices with their start and end apart: 11, of which 6 were waited for; matrix products, arithmetic and copies ran while one was open for 2% of the time, Pallas kernels for 24%

profile of v8, /device:TPU:0, one launch (start us, length us, event | category | flops | bytes accessed | tf_op | source)
XLA Modules:
  0.0 65.8 jit_solution(13895146202198003912)
XLA Ops:
  0.0 5.0 %collective-permute-start.5 = (f32[3,16,16,128]{3,2,1,0:T(8,128)}, f32[3,16,16,128]{3,2,1,0:T(8,128)S(1)}, u32[]{:S(2)}, u32[]{:S(2)}) collective-permute-start(f32[3,16,16,128]{3,2,1,0:T(8,128)} %own.1), channel_id=1, source_target_pairs={{0,24},{8,0},{16,8},{24,16},{1,25},{9,1},{17,9},{25,17},{2,26},{10... | collective-permute-start | bytes 1179656 | tf_op jit(solution)/shard_map/ppermute | solution.py:29
  5.8 0.8 %convert_select_fusion.refs_0_ = f32[8,1024]{1,0:T(8,128)S(1)} fusion(f32[3,1024]{1,0:T(4,128)} %param.13, s32[1024]{0:T(1024)} %bitcast.3, s32[1024]{0:T(1024)S(1)} %multiply_add_fusion, pred[8]{0:T(512)(128)(4,1)S(1)} %get-tuple-element.33, pred[8]{0:T(512)(128)(4,1)S(1)} %get-tuple-element.34), kind=kLoop, calls=%fused_computation | loop fusion | flops 24576 | bytes 53264 | tf_op jit(solution)/shard_map/jit(_where)/select_n | solution.py:438
  7.3 2.1 %shard_map.83 = (f32[8,4,512]{2,1,0:T(4,128)}, bf16[512,1024]{1,0:T(8,128)(2,1)S(1)}, s32[1,1024]{1,0:T(1,128)S(1)}) custom-call(f32[8,1024]{1,0:T(8,128)S(1)} %convert_select_fusion.refs_0_), custom_call_target="tpu_custom_call" | custom-call | flops 83886080 | bytes 163840 | tf_op jit(solution)/shard_map/pallas_call | solution.py:360
  9.4 6.0 %all-to-all-start = ((f32[8,4,512]{2,1,0:T(4,128)}), f32[8,4,512]{2,1,0:T(4,128)S(1)}, u32[]{:S(2)}, u32[]{:S(2)}) async-start(f32[8,4,512]{2,1,0:T(4,128)} %get-tuple-element.20), calls=%async_computation | async-start | bytes 131072 | tf_op jit(solution)/shard_map/all_to_all | solution.py:445
  15.4 1.2 %collective-permute-start.7 = (f32[3,16,16,128]{3,2,1,0:T(8,128)S(1)}, f32[3,16,16,128]{3,2,1,0:T(8,128)}, u32[]{:S(2)}, u32[]{:S(2)}) collective-permute-start(f32[3,16,16,128]{3,2,1,0:T(8,128)S(1)} %collective-permute-done.5.own), channel_id=1, source_target_pairs={{0,3},{1,0},{2,1},{3,2},{4,7},{5,4},{6,5},{7,6},{8,11},{9,8},{10,9... | collective-permute-start | bytes 1179656 | tf_op jit(solution)/shard_map/ppermute | solution.py:29
  16.7 1.5 %collective-permute-done.1.before = f32[3,16,16,128]{3,2,1,0:T(8,128)S(1)} collective-permute-done((f32[3,16,16,128]{3,2,1,0:T(8,128)}, f32[3,16,16,128]{3,2,1,0:T(8,128)S(1)}, u32[]{:S(2)}, u32[]{:S(2)}) %collective-permute-start.1) | collective-permute-done | bytes 393248 | tf_op jit(solution)/shard_map/ppermute | solution.py:29
  19.0 1.0 %copy-done = f32[3,16,16,128]{3,2,1,0:T(8,128)S(1)} copy-done((f32[3,16,16,128]{3,2,1,0:T(8,128)S(1)}, f32[3,16,16,128]{3,2,1,0:T(8,128)}, u32[]{:S(2)}) %copy-start) | copy-done | bytes 393240
  20.0 1.0 %copy-done.2 = f32[3,16,16,128]{3,2,1,0:T(8,128)S(1)} copy-done((f32[3,16,16,128]{3,2,1,0:T(8,128)S(1)}, f32[3,16,16,128]{3,2,1,0:T(8,128)}, u32[]{:S(2)}) %copy-start.2) | copy-done | bytes 393240
  21.0 2.2 %shard_map.82.own = f32[9,16,16,128]{3,2,1,0:T(8,128)S(1)} custom-call(f32[3,16,16,128]{3,2,1,0:T(8,128)S(1)} %copy-done.2, f32[3,16,16,128]{3,2,1,0:T(8,128)S(1)} %copy-done, f32[3,16,16,128]{3,2,1,0:T(8,128)S(1)} %collective-permute-done.2.after), custom_call_target="tpu_custom_call" | custom-call | flops 19464192 | bytes 2752512 | tf_op jit(solution)/shard_map/pallas_call | solution.py:103
  23.2 1.7 %all-to-all-done.refs_0_ = f32[8,4,512]{2,1,0:T(4,128)S(1)} async-done(((f32[8,4,512]{2,1,0:T(4,128)}), f32[8,4,512]{2,1,0:T(4,128)S(1)}, u32[]{:S(2)}, u32[]{:S(2)}) %all-to-all-start) | async-done | bytes 65568 | tf_op jit(solution)/shard_map/all_to_all | solution.py:445
  24.9 1.5 %collective-permute-start.4 = (f32[3,16,16,128]{3,2,1,0:T(8,128)S(1)}, f32[3,16,16,128]{3,2,1,0:T(8,128)S(1)}, u32[]{:S(2)}, u32[]{:S(2)}) collective-permute-start(f32[3,16,16,128]{3,2,1,0:T(8,128)S(1)} %collective-permute-done.2.after), channel_id=1, source_target_pairs={{0,8},{8,16},{16,24},{24,0},{1,9},{9,17},{17,25},{25,1},{2,10},{10... | collective-permute-start | bytes 1179656 | tf_op jit(solution)/shard_map/ppermute | solution.py:29
  26.5 1.5 %shard_map.86 = (bf16[256,4096]{1,0:T(8,128)(2,1)S(1)}, bf16[256,4096]{1,0:T(8,128)(2,1)S(1)}, f32[128,4096]{1,0:T(8,128)S(1)}) custom-call(f32[8,4,512]{2,1,0:T(4,128)S(1)} %all-to-all-done.refs_0_), custom_call_target="tpu_custom_call" | custom-call | flops 8192000 | bytes 6553600 | tf_op jit(solution)/shard_map/pallas_call | solution.py:235
  28.0 3.3 %shard_map.84.right = f32[9,16,16,128]{3,2,1,0:T(8,128)S(1)} custom-call(f32[3,16,16,128]{3,2,1,0:T(8,128)} %collective-permute-done.6.before, f32[3,16,16,128]{3,2,1,0:T(8,128)S(1)} %collective-permute-done.5.own, f32[3,16,16,128]{3,2,1,0:T(8,128)} %collective-permute-done.7.after), custom_call_target="tpu_custom_call" | custom-call | flops 19464192 | bytes 2752512 | tf_op jit(solution)/shard_map/pallas_call | solution.py:103
  31.3 2.1 %shard_map.85.refs_3_ = f32[9,256,128]{2,1,0:T(8,128)S(1)} custom-call(f32[9,16,16,128]{3,2,1,0:T(8,128)S(1)} %shard_map.82.own, f32[9,16,16,128]{3,2,1,0:T(8,128)S(1)} %shard_map.84.right), custom_call_target="tpu_custom_call" | custom-call | flops 19464192 | bytes 3932160 | tf_op jit(solution)/shard_map/pallas_call | solution.py:136
  33.4 4.0 %collective-permute-done.4.refs_2_ = f32[3,16,16,128]{3,2,1,0:T(8,128)S(1)} collective-permute-done((f32[3,16,16,128]{3,2,1,0:T(8,128)S(1)}, f32[3,16,16,128]{3,2,1,0:T(8,128)S(1)}, u32[]{:S(2)}, u32[]{:S(2)}) %collective-permute-start.4) | collective-permute-done | bytes 393248 | tf_op jit(solution)/shard_map/ppermute | solution.py:29
  37.4 2.3 %shard_map.87 = (f32[5,256,128]{2,1,0:T(8,128)S(1)}, f32[5,32,256]{2,1,0:T(8,128)S(1)}) custom-call(f32[3,16,16,128]{3,2,1,0:T(8,128)S(1)} %collective-permute-done.3.refs_0_, f32[3,16,16,128]{3,2,1,0:T(8,128)S(1)} %collective-permute-done.refs_1_, f32[3,16,16,128]{3,2,1,0:T(8,128)S(1)} %collective-permute-done.4.refs_2_, f32[9,256,128]{2,1,0:T(8,128)S(1)} %shard_map.85.refs_3_), custom_call_target="tpu_custom_call" | custom-call | flops 16384000 | bytes 5242880 | tf_op jit(solution)/shard_map/pallas_call | solution.py:187
  39.7 1.5 %collective-permute-start.8 = (f32[5,32,256]{2,1,0:T(8,128)S(1)}, f32[5,32,256]{2,1,0:T(8,128)S(1)}, u32[]{:S(2)}, u32[]{:S(2)}) collective-permute-start(f32[5,32,256]{2,1,0:T(8,128)S(1)} %get-tuple-element.29), channel_id=1, source_target_pairs={{0,4},{4,0},{1,5},{5,1},{2,6},{6,2},{3,7},{7,3},{8,12},{12,8},{9,1... | collective-permute-start | bytes 491528 | tf_op jit(solution)/shard_map/ppermute | solution.py:415
  41.2 1.9 %shard_map.88 = (f32[4,256,128]{2,1,0:T(8,128)S(1)}, f32[4,32,256]{2,1,0:T(8,128)S(1)}) custom-call(f32[3,16,16,128]{3,2,1,0:T(8,128)S(1)} %collective-permute-done.3.refs_0_, f32[3,16,16,128]{3,2,1,0:T(8,128)S(1)} %collective-permute-done.refs_1_, f32[3,16,16,128]{3,2,1,0:T(8,128)S(1)} %collective-permute-done.4.refs_2_, f32[9,256,128]{2,1,0:T(8,128)S(1)} %shard_map.85.refs_3_), custom_call_target="tpu_custom_call" | custom-call | flops 13107200 | bytes 5242880 | tf_op jit(solution)/shard_map/pallas_call | solution.py:187
  43.8 1.1 %shard_map.89.partial = f32[4,128,256]{2,1,0:T(8,128)S(1)} custom-call(f32[128,128]{1,0:T(8,128)S(1)} %copy-done.3, f32[4,256,128]{2,1,0:T(8,128)S(1)} %get-tuple-element.27.fields), custom_call_target="tpu_custom_call" | custom-call | flops 201326592 | bytes 1048576 | tf_op jit(solution)/shard_map/pallas_call | solution.py:269
  45.5 1.8 %shard_map.90.first = f32[5,128,256]{2,1,0:T(8,128)S(1)} custom-call(f32[128,128]{1,0:T(8,128)S(1)} %copy-done.3, f32[5,256,128]{2,1,0:T(8,128)S(1)} %get-tuple-element.28.fields, f32[128,32]{1,0:T(8,128)S(1)} %copy-done.4, f32[5,32,256]{2,1,0:T(8,128)S(1)} %collective-permute-done.8.refs_1_), custom_call_target="tpu_custom_call" | custom-call | flops 251658240 | bytes 1310720 | tf_op jit(solution)/shard_map/pallas_call | solution.py:269
  47.3 0.8 %collective-permute-done.9.strips = f32[4,32,256]{2,1,0:T(8,128)S(1)} collective-permute-done((f32[4,32,256]{2,1,0:T(8,128)S(1)}, f32[4,32,256]{2,1,0:T(8,128)S(1)}, u32[]{:S(2)}, u32[]{:S(2)}) %collective-permute-start.9) | collective-permute-done | bytes 131104 | tf_op jit(solution)/shard_map/ppermute | solution.py:415
  48.1 5.5 %shard_map.91 = f32[8,8,512]{2,1,0:T(8,128)S(1)} custom-call(f32[5,128,256]{2,1,0:T(8,128)S(1)} %shard_map.90.first, f32[4,128,256]{2,1,0:T(8,128)S(1)} %shard_map.89.partial, f32[4,32,256]{2,1,0:T(8,128)S(1)} %collective-permute-done.9.strips, f32[128,32]{1,0:T(8,128)S(1)} %copy-done.4, bf16[256,4096]{1,0:T(8,128)(2,1)S(1)} %get-tuple-element.22.w_high, ...), custom_call_target="tpu_custom_call" | custom-call | flops 4831838208 | bytes 8388608 | tf_op jit(solution)/shard_map/pallas_call | solution.py:318
  53.6 11.1 %all_to_all.10 = f32[8,8,512]{2,1,0:T(8,128)S(1)} all-to-all(f32[8,8,512]{2,1,0:T(8,128)S(1)} %shard_map.91), channel_id=1, replica_groups=mesh['gx'=4,'gy'=2,'gz'=4] {'gx','gy'}, dimensions={0} | all-to-all | bytes 262144 | tf_op jit(solution)/shard_map/all_to_all | solution.py:464
  64.7 1.1 %shard_map.92 = f32[6,1024]{1,0:T(8,128)} custom-call(f32[64,512]{1,0:T(8,128)S(1)} %bitcast.2, bf16[512,1024]{1,0:T(8,128)(2,1)S(1)} %get-tuple-element.31.refs_1_, s32[1,1024]{1,0:T(1,128)S(1)} %get-tuple-element.32.refs_2_), custom_call_target="tpu_custom_call" | custom-call | flops 201326592 | bytes 102400 | tf_op jit(solution)/shard_map/pallas_call | solution.py:392
  (23 shorter events, 3.6 us)
Async XLA Ops:
  0.0 15.4 %collective-permute-start.5 = (f32[3,16,16,128]{3,2,1,0:T(8,128)}, f32[3,16,16,128]{3,2,1,0:T(8,128)S(1)}, u32[]{:S(2)}, u32[]{:S(2)}) collective-permute-start(f32[3,16,16,128]{3,2,1,0:T(8,128)} %own.1), channel_id=1, source_target_pairs={{0,24},{8,0},{16,8},{24,16},{1,25},{9,1},{17,9},{25,17},{2,26},{10... | collective-permute-start | bytes 1179656 | tf_op jit(solution)/shard_map/ppermute | solution.py:29
  6.6 10.2 %collective-permute-start.2 = (f32[3,16,16,128]{3,2,1,0:T(8,128)}, f32[3,16,16,128]{3,2,1,0:T(8,128)S(1)}, u32[]{:S(2)}, u32[]{:S(2)}) collective-permute-start(f32[3,16,16,128]{3,2,1,0:T(8,128)} %own.1), channel_id=1, source_target_pairs={{0,3},{1,0},{2,1},{3,2},{4,7},{5,4},{6,5},{7,6},{8,11},{9,8},{10,9... | collective-permute-start | bytes 1179656 | tf_op jit(solution)/shard_map/ppermute | solution.py:29
  7.3 11.0 %collective-permute-start.1 = (f32[3,16,16,128]{3,2,1,0:T(8,128)}, f32[3,16,16,128]{3,2,1,0:T(8,128)S(1)}, u32[]{:S(2)}, u32[]{:S(2)}) collective-permute-start(f32[3,16,16,128]{3,2,1,0:T(8,128)} %own.1), channel_id=1, source_target_pairs={{0,1},{1,2},{2,3},{3,0},{4,5},{5,6},{6,7},{7,4},{8,9},{9,10},{10,1... | collective-permute-start | bytes 1179656 | tf_op jit(solution)/shard_map/ppermute | solution.py:29
  7.3 17.7 %collective-permute-start = (f32[3,16,16,128]{3,2,1,0:T(8,128)}, f32[3,16,16,128]{3,2,1,0:T(8,128)S(1)}, u32[]{:S(2)}, u32[]{:S(2)}) collective-permute-start(f32[3,16,16,128]{3,2,1,0:T(8,128)} %own.1), channel_id=1, source_target_pairs={{0,8},{8,16},{16,24},{24,0},{1,9},{9,17},{17,25},{25,1},{2,10},{10... | collective-permute-start | bytes 1179656 | tf_op jit(solution)/shard_map/ppermute | solution.py:29
  9.4 15.6 %all-to-all-start = ((f32[8,4,512]{2,1,0:T(4,128)}), f32[8,4,512]{2,1,0:T(4,128)S(1)}, u32[]{:S(2)}, u32[]{:S(2)}) async-start(f32[8,4,512]{2,1,0:T(4,128)} %get-tuple-element.20), calls=%async_computation | async-start | bytes 131072 | tf_op jit(solution)/shard_map/all_to_all | solution.py:445
  15.4 12.6 %collective-permute-start.7 = (f32[3,16,16,128]{3,2,1,0:T(8,128)S(1)}, f32[3,16,16,128]{3,2,1,0:T(8,128)}, u32[]{:S(2)}, u32[]{:S(2)}) collective-permute-start(f32[3,16,16,128]{3,2,1,0:T(8,128)S(1)} %collective-permute-done.5.own), channel_id=1, source_target_pairs={{0,3},{1,0},{2,1},{3,2},{4,7},{5,4},{6,5},{7,6},{8,11},{9,8},{10,9... | collective-permute-start | bytes 1179656 | tf_op jit(solution)/shard_map/ppermute | solution.py:29
  16.6 11.4 %collective-permute-start.6 = (f32[3,16,16,128]{3,2,1,0:T(8,128)S(1)}, f32[3,16,16,128]{3,2,1,0:T(8,128)}, u32[]{:S(2)}, u32[]{:S(2)}) collective-permute-start(f32[3,16,16,128]{3,2,1,0:T(8,128)S(1)} %collective-permute-done.5.own), channel_id=1, source_target_pairs={{0,1},{1,2},{2,3},{3,0},{4,5},{5,6},{6,7},{7,4},{8,9},{9,10},{10,1... | collective-permute-start | bytes 1179656 | tf_op jit(solution)/shard_map/ppermute | solution.py:29
  18.3 0.8 %copy-start.1 = (f32[3,16,16,128]{3,2,1,0:T(8,128)}, f32[3,16,16,128]{3,2,1,0:T(8,128)S(1)}, u32[]{:S(2)}) copy-start(f32[3,16,16,128]{3,2,1,0:T(8,128)S(1)} %collective-permute-done.1.before) | copy-start | bytes 1179652
  19.0 1.0 %copy-start = (f32[3,16,16,128]{3,2,1,0:T(8,128)S(1)}, f32[3,16,16,128]{3,2,1,0:T(8,128)}, u32[]{:S(2)}) copy-start(f32[3,16,16,128]{3,2,1,0:T(8,128)} %own.1) | copy-start | bytes 1179652
  20.0 1.0 %copy-start.2 = (f32[3,16,16,128]{3,2,1,0:T(8,128)S(1)}, f32[3,16,16,128]{3,2,1,0:T(8,128)}, u32[]{:S(2)}) copy-start(f32[3,16,16,128]{3,2,1,0:T(8,128)} %copy-done.1) | copy-start | bytes 1179652
  24.9 12.4 %collective-permute-start.4 = (f32[3,16,16,128]{3,2,1,0:T(8,128)S(1)}, f32[3,16,16,128]{3,2,1,0:T(8,128)S(1)}, u32[]{:S(2)}, u32[]{:S(2)}) collective-permute-start(f32[3,16,16,128]{3,2,1,0:T(8,128)S(1)} %collective-permute-done.2.after), channel_id=1, source_target_pairs={{0,8},{8,16},{16,24},{24,0},{1,9},{9,17},{17,25},{25,1},{2,10},{10... | collective-permute-start | bytes 1179656 | tf_op jit(solution)/shard_map/ppermute | solution.py:29
  26.5 10.9 %collective-permute-start.3 = (f32[3,16,16,128]{3,2,1,0:T(8,128)S(1)}, f32[3,16,16,128]{3,2,1,0:T(8,128)S(1)}, u32[]{:S(2)}, u32[]{:S(2)}) collective-permute-start(f32[3,16,16,128]{3,2,1,0:T(8,128)S(1)} %collective-permute-done.refs_1_), channel_id=1, source_target_pairs={{0,1},{1,2},{2,3},{3,0},{4,5},{5,6},{6,7},{7,4},{8,9},{9,10},{10,1... | collective-permute-start | bytes 1179656 | tf_op jit(solution)/shard_map/ppermute | solution.py:29
  33.4 10.3 %copy-start.3 = (f32[128,128]{1,0:T(8,128)S(1)}, f32[128,128]{1,0:T(8,128)}, u32[]{:S(2)}) copy-start(f32[128,128]{1,0:T(8,128)} %constant.13.clone.band) | copy-start | bytes 196612
  39.7 5.8 %copy-start.4 = (f32[128,32]{1,0:T(8,128)S(1)}, f32[128,32]{1,0:T(8,128)}, u32[]{:S(2)}) copy-start(f32[128,32]{1,0:T(8,128)} %constant.14.clone.refs_0_.band) | copy-start | bytes 49156
  39.7 5.8 %collective-permute-start.8 = (f32[5,32,256]{2,1,0:T(8,128)S(1)}, f32[5,32,256]{2,1,0:T(8,128)S(1)}, u32[]{:S(2)}, u32[]{:S(2)}) collective-permute-start(f32[5,32,256]{2,1,0:T(8,128)S(1)} %get-tuple-element.29), channel_id=1, source_target_pairs={{0,4},{4,0},{1,5},{5,1},{2,6},{6,2},{3,7},{7,3},{8,12},{12,8},{9,1... | collective-permute-start | bytes 491528 | tf_op jit(solution)/shard_map/ppermute | solution.py:415
  43.1 5.0 %collective-permute-start.9 = (f32[4,32,256]{2,1,0:T(8,128)S(1)}, f32[4,32,256]{2,1,0:T(8,128)S(1)}, u32[]{:S(2)}, u32[]{:S(2)}) collective-permute-start(f32[4,32,256]{2,1,0:T(8,128)S(1)} %get-tuple-element.30), channel_id=1, source_target_pairs={{0,4},{4,0},{1,5},{5,1},{2,6},{6,2},{3,7},{7,3},{8,12},{12,8},{9,1... | collective-permute-start | bytes 393224 | tf_op jit(solution)/shard_map/ppermute | solution.py:415

commit v9 on v8

--- a/solution.py
+++ b/solution.py
@@ -451,9 +451,9 @@
     weights = hats(asked, sizes)
     partial = after(partial, weights)
     band_own, band_strips = y_band(size_y)
-    first, edges = along_x_last(tuple(range(5)), *left, partial)
+    first, edges = along_x_last(tuple(range(4)), *left, partial)
     first_strips = y_strips(edges)
-    second, edges = along_x_last(tuple(range(5, 9)), *left, partial)
+    second, edges = along_x_last(tuple(range(4, 9)), *left, partial)
     second_strips = y_strips(edges)
     band_own, band_strips = jnp.asarray(band_own), jnp.asarray(band_strips)
     partial = along_y(band_own, second)

time: 66.2 us -> 67.5 us (1.020)
  waiting for transfers between devices: 8.77 us -> 10.3 us
    ppermute x2, waiting for transfers between devices: 1.45 us -> 2.96 us  [y_strips(): return lax.ppermute(edges, 'gy', [(0, 1), (1, 0)])]
  transfers between devices with their start and end apart: 11 -> 11, of which waited for: 6 -> 5; matrix products, arithmetic and copies ran while one was open for 2% -> 2% of each run, Pallas kernels for 24% -> 24%
where the time goes in v9:
time: 67.5 us; the launch traced here: 67.1 us
  Pallas kernels  25 us (37%)
  starting transfers between devices  16.7 us (25%)
  blocking collectives  10.7 us (16%)
  waiting for transfers between devices  10.3 us (15%)
  local copies, waits for them, and re-layouts  2.77 us (4%)
  other arithmetic  1.52 us (2%)
    all_to_all x1, blocking collectives, on_device(): lax.all_to_all(values, ('gx', 'gy'), split_axis=0, concat_axis=0, tiled=T...  10.7 us
    ppermute x8, starting transfers between devices, shifted(): lax.ppermute(x, axis, [(i, (i + step) % devices) for i in range(devices)])  8.51 us
    all_to_all x1, starting transfers between devices, on_device(): lax.all_to_all(sent, ('gx', 'gy'), split_axis=0, concat_axis=0, tiled=True)  6.02 us
    pallas_call x1, Pallas kernels, samples(): pl.pallas_call(sample_kernel, out_shape=jax.ShapeDtypeStruct((groups, ROW...  5.7 us
    ppermute x8, waiting for transfers between devices, shifted(): lax.ppermute(x, axis, [(i, (i + step) % devices) for i in range(devices)])  5.62 us
    pallas_call x2, Pallas kernels, along_z(): pl.pallas_call(z_kernel, out_shape=jax.ShapeDtypeStruct((9, z, x, y), F32...  5.51 us
    pallas_call x2, Pallas kernels, along_x_last(): pl.pallas_call(kernel, out_shape=(jax.ShapeDtypeStruct((count, z * x, y),...  4.19 us
    ppermute x2, waiting for transfers between devices, y_strips(): return lax.ppermute(edges, 'gy', [(0, 1), (1, 0)])  2.96 us
  transfers between devices with their start and end apart: 11, of which 5 were waited for; matrix products, arithmetic and copies ran while one was open for 2% of the time, Pallas kernels for 24%

profile of v9, /device:TPU:0, one launch (start us, length us, event | category | flops | bytes accessed | tf_op | source)
XLA Modules:
  0.0 67.1 jit_solution(1088616833676933728)
XLA Ops:
  0.0 5.0 %collective-permute-start.5 = (f32[3,16,16,128]{3,2,1,0:T(8,128)}, f32[3,16,16,128]{3,2,1,0:T(8,128)S(1)}, u32[]{:S(2)}, u32[]{:S(2)}) collective-permute-start(f32[3,16,16,128]{3,2,1,0:T(8,128)} %own.1), channel_id=1, source_target_pairs={{0,24},{8,0},{16,8},{24,16},{1,25},{9,1},{17,9},{25,17},{2,26},{10... | collective-permute-start | bytes 1179656 | tf_op jit(solution)/shard_map/ppermute | solution.py:29
  5.8 0.8 %convert_select_fusion.refs_0_ = f32[8,1024]{1,0:T(8,128)S(1)} fusion(f32[3,1024]{1,0:T(4,128)} %param.13, s32[1024]{0:T(1024)} %bitcast.3, s32[1024]{0:T(1024)S(1)} %multiply_add_fusion, pred[8]{0:T(512)(128)(4,1)S(1)} %get-tuple-element.33, pred[8]{0:T(512)(128)(4,1)S(1)} %get-tuple-element.34), kind=kLoop, calls=%fused_computation | loop fusion | flops 24576 | bytes 53264 | tf_op jit(solution)/shard_map/jit(_where)/select_n | solution.py:438
  7.3 2.1 %shard_map.83 = (f32[8,4,512]{2,1,0:T(4,128)}, bf16[512,1024]{1,0:T(8,128)(2,1)S(1)}, s32[1,1024]{1,0:T(1,128)S(1)}) custom-call(f32[8,1024]{1,0:T(8,128)S(1)} %convert_select_fusion.refs_0_), custom_call_target="tpu_custom_call" | custom-call | flops 83886080 | bytes 163840 | tf_op jit(solution)/shard_map/pallas_call | solution.py:360
  9.4 6.0 %all-to-all-start = ((f32[8,4,512]{2,1,0:T(4,128)}), f32[8,4,512]{2,1,0:T(4,128)S(1)}, u32[]{:S(2)}, u32[]{:S(2)}) async-start(f32[8,4,512]{2,1,0:T(4,128)} %get-tuple-element.20), calls=%async_computation | async-start | bytes 131072 | tf_op jit(solution)/shard_map/all_to_all | solution.py:445
  15.4 1.2 %collective-permute-start.7 = (f32[3,16,16,128]{3,2,1,0:T(8,128)S(1)}, f32[3,16,16,128]{3,2,1,0:T(8,128)}, u32[]{:S(2)}, u32[]{:S(2)}) collective-permute-start(f32[3,16,16,128]{3,2,1,0:T(8,128)S(1)} %collective-permute-done.5.own), channel_id=1, source_target_pairs={{0,3},{1,0},{2,1},{3,2},{4,7},{5,4},{6,5},{7,6},{8,11},{9,8},{10,9... | collective-permute-start | bytes 1179656 | tf_op jit(solution)/shard_map/ppermute | solution.py:29
  16.7 1.5 %collective-permute-done.1.before = f32[3,16,16,128]{3,2,1,0:T(8,128)S(1)} collective-permute-done((f32[3,16,16,128]{3,2,1,0:T(8,128)}, f32[3,16,16,128]{3,2,1,0:T(8,128)S(1)}, u32[]{:S(2)}, u32[]{:S(2)}) %collective-permute-start.1) | collective-permute-done | bytes 393248 | tf_op jit(solution)/shard_map/ppermute | solution.py:29
  19.0 1.0 %copy-done = f32[3,16,16,128]{3,2,1,0:T(8,128)S(1)} copy-done((f32[3,16,16,128]{3,2,1,0:T(8,128)S(1)}, f32[3,16,16,128]{3,2,1,0:T(8,128)}, u32[]{:S(2)}) %copy-start) | copy-done | bytes 393240
  20.0 1.0 %copy-done.2 = f32[3,16,16,128]{3,2,1,0:T(8,128)S(1)} copy-done((f32[3,16,16,128]{3,2,1,0:T(8,128)S(1)}, f32[3,16,16,128]{3,2,1,0:T(8,128)}, u32[]{:S(2)}) %copy-start.2) | copy-done | bytes 393240
  21.0 2.2 %shard_map.82.own = f32[9,16,16,128]{3,2,1,0:T(8,128)S(1)} custom-call(f32[3,16,16,128]{3,2,1,0:T(8,128)S(1)} %copy-done.2, f32[3,16,16,128]{3,2,1,0:T(8,128)S(1)} %copy-done, f32[3,16,16,128]{3,2,1,0:T(8,128)S(1)} %collective-permute-done.2.after), custom_call_target="tpu_custom_call" | custom-call | flops 19464192 | bytes 2752512 | tf_op jit(solution)/shard_map/pallas_call | solution.py:103
  23.2 1.7 %all-to-all-done.refs_0_ = f32[8,4,512]{2,1,0:T(4,128)S(1)} async-done(((f32[8,4,512]{2,1,0:T(4,128)}), f32[8,4,512]{2,1,0:T(4,128)S(1)}, u32[]{:S(2)}, u32[]{:S(2)}) %all-to-all-start) | async-done | bytes 65568 | tf_op jit(solution)/shard_map/all_to_all | solution.py:445
  24.9 1.5 %collective-permute-start.4 = (f32[3,16,16,128]{3,2,1,0:T(8,128)S(1)}, f32[3,16,16,128]{3,2,1,0:T(8,128)S(1)}, u32[]{:S(2)}, u32[]{:S(2)}) collective-permute-start(f32[3,16,16,128]{3,2,1,0:T(8,128)S(1)} %collective-permute-done.2.after), channel_id=1, source_target_pairs={{0,8},{8,16},{16,24},{24,0},{1,9},{9,17},{17,25},{25,1},{2,10},{10... | collective-permute-start | bytes 1179656 | tf_op jit(solution)/shard_map/ppermute | solution.py:29
  26.5 1.5 %shard_map.86 = (bf16[256,4096]{1,0:T(8,128)(2,1)S(1)}, bf16[256,4096]{1,0:T(8,128)(2,1)S(1)}, f32[128,4096]{1,0:T(8,128)S(1)}) custom-call(f32[8,4,512]{2,1,0:T(4,128)S(1)} %all-to-all-done.refs_0_), custom_call_target="tpu_custom_call" | custom-call | flops 8192000 | bytes 6553600 | tf_op jit(solution)/shard_map/pallas_call | solution.py:235
  28.0 3.3 %shard_map.84.right = f32[9,16,16,128]{3,2,1,0:T(8,128)S(1)} custom-call(f32[3,16,16,128]{3,2,1,0:T(8,128)} %collective-permute-done.6.before, f32[3,16,16,128]{3,2,1,0:T(8,128)S(1)} %collective-permute-done.5.own, f32[3,16,16,128]{3,2,1,0:T(8,128)} %collective-permute-done.7.after), custom_call_target="tpu_custom_call" | custom-call | flops 19464192 | bytes 2752512 | tf_op jit(solution)/shard_map/pallas_call | solution.py:103
  31.3 2.1 %shard_map.85.refs_3_ = f32[9,256,128]{2,1,0:T(8,128)S(1)} custom-call(f32[9,16,16,128]{3,2,1,0:T(8,128)S(1)} %shard_map.82.own, f32[9,16,16,128]{3,2,1,0:T(8,128)S(1)} %shard_map.84.right), custom_call_target="tpu_custom_call" | custom-call | flops 19464192 | bytes 3932160 | tf_op jit(solution)/shard_map/pallas_call | solution.py:136
  33.4 4.0 %collective-permute-done.4.refs_2_ = f32[3,16,16,128]{3,2,1,0:T(8,128)S(1)} collective-permute-done((f32[3,16,16,128]{3,2,1,0:T(8,128)S(1)}, f32[3,16,16,128]{3,2,1,0:T(8,128)S(1)}, u32[]{:S(2)}, u32[]{:S(2)}) %collective-permute-start.4) | collective-permute-done | bytes 393248 | tf_op jit(solution)/shard_map/ppermute | solution.py:29
  37.4 2.3 %shard_map.88 = (f32[5,256,128]{2,1,0:T(8,128)S(1)}, f32[5,32,256]{2,1,0:T(8,128)S(1)}) custom-call(f32[3,16,16,128]{3,2,1,0:T(8,128)S(1)} %collective-permute-done.3.refs_0_, f32[3,16,16,128]{3,2,1,0:T(8,128)S(1)} %collective-permute-done.refs_1_, f32[3,16,16,128]{3,2,1,0:T(8,128)S(1)} %collective-permute-done.4.refs_2_, f32[9,256,128]{2,1,0:T(8,128)S(1)} %shard_map.85.refs_3_), custom_call_target="tpu_custom_call" | custom-call | flops 16384000 | bytes 5242880 | tf_op jit(solution)/shard_map/pallas_call | solution.py:187
  39.7 1.5 %collective-permute-start.9 = (f32[5,32,256]{2,1,0:T(8,128)S(1)}, f32[5,32,256]{2,1,0:T(8,128)S(1)}, u32[]{:S(2)}, u32[]{:S(2)}) collective-permute-start(f32[5,32,256]{2,1,0:T(8,128)S(1)} %get-tuple-element.30), channel_id=1, source_target_pairs={{0,4},{4,0},{1,5},{5,1},{2,6},{6,2},{3,7},{7,3},{8,12},{12,8},{9,1... | collective-permute-start | bytes 491528 | tf_op jit(solution)/shard_map/ppermute | solution.py:415
  41.2 1.9 %shard_map.87 = (f32[4,256,128]{2,1,0:T(8,128)S(1)}, f32[4,32,256]{2,1,0:T(8,128)S(1)}) custom-call(f32[3,16,16,128]{3,2,1,0:T(8,128)S(1)} %collective-permute-done.3.refs_0_, f32[3,16,16,128]{3,2,1,0:T(8,128)S(1)} %collective-permute-done.refs_1_, f32[3,16,16,128]{3,2,1,0:T(8,128)S(1)} %collective-permute-done.4.refs_2_, f32[9,256,128]{2,1,0:T(8,128)S(1)} %shard_map.85.refs_3_), custom_call_target="tpu_custom_call" | custom-call | flops 13107200 | bytes 5242880 | tf_op jit(solution)/shard_map/pallas_call | solution.py:187
  43.8 1.4 %shard_map.89.partial = f32[5,128,256]{2,1,0:T(8,128)S(1)} custom-call(f32[128,128]{1,0:T(8,128)S(1)} %copy-done.3, f32[5,256,128]{2,1,0:T(8,128)S(1)} %get-tuple-element.27.fields), custom_call_target="tpu_custom_call" | custom-call | flops 251658240 | bytes 1310720 | tf_op jit(solution)/shard_map/pallas_call | solution.py:269
  45.2 3.0 %collective-permute-done.8.refs_1_ = f32[4,32,256]{2,1,0:T(8,128)S(1)} collective-permute-done((f32[4,32,256]{2,1,0:T(8,128)S(1)}, f32[4,32,256]{2,1,0:T(8,128)S(1)}, u32[]{:S(2)}, u32[]{:S(2)}) %collective-permute-start.8) | collective-permute-done | bytes 131104 | tf_op jit(solution)/shard_map/ppermute | solution.py:415
  48.1 1.4 %shard_map.90.first = f32[4,128,256]{2,1,0:T(8,128)S(1)} custom-call(f32[128,128]{1,0:T(8,128)S(1)} %copy-done.3, f32[4,256,128]{2,1,0:T(8,128)S(1)} %get-tuple-element.28.fields, f32[128,32]{1,0:T(8,128)S(1)} %copy-done.4, f32[4,32,256]{2,1,0:T(8,128)S(1)} %collective-permute-done.8.refs_1_), custom_call_target="tpu_custom_call" | custom-call | flops 201326592 | bytes 1048576 | tf_op jit(solution)/shard_map/pallas_call | solution.py:269
  49.6 5.7 %shard_map.91 = f32[8,8,512]{2,1,0:T(8,128)S(1)} custom-call(f32[4,128,256]{2,1,0:T(8,128)S(1)} %shard_map.90.first, f32[5,128,256]{2,1,0:T(8,128)S(1)} %shard_map.89.partial, f32[5,32,256]{2,1,0:T(8,128)S(1)} %collective-permute-done.9.strips, f32[128,32]{1,0:T(8,128)S(1)} %copy-done.4, bf16[256,4096]{1,0:T(8,128)(2,1)S(1)} %get-tuple-element.22.w_high, ...), custom_call_target="tpu_custom_call" | custom-call | flops 4831838208 | bytes 8388608 | tf_op jit(solution)/shard_map/pallas_call | solution.py:318
  55.3 10.7 %all_to_all.10 = f32[8,8,512]{2,1,0:T(8,128)S(1)} all-to-all(f32[8,8,512]{2,1,0:T(8,128)S(1)} %shard_map.91), channel_id=1, replica_groups=mesh['gx'=4,'gy'=2,'gz'=4] {'gx','gy'}, dimensions={0} | all-to-all | bytes 262144 | tf_op jit(solution)/shard_map/all_to_all | solution.py:464
  66.0 1.1 %shard_map.92 = f32[6,1024]{1,0:T(8,128)} custom-call(f32[64,512]{1,0:T(8,128)S(1)} %bitcast.2, bf16[512,1024]{1,0:T(8,128)(2,1)S(1)} %get-tuple-element.31.refs_1_, s32[1,1024]{1,0:T(1,128)S(1)} %get-tuple-element.32.refs_2_), custom_call_target="tpu_custom_call" | custom-call | flops 201326592 | bytes 102400 | tf_op jit(solution)/shard_map/pallas_call | solution.py:392
  (23 shorter events, 3.0 us)
Async XLA Ops:
  0.0 15.4 %collective-permute-start.5 = (f32[3,16,16,128]{3,2,1,0:T(8,128)}, f32[3,16,16,128]{3,2,1,0:T(8,128)S(1)}, u32[]{:S(2)}, u32[]{:S(2)}) collective-permute-start(f32[3,16,16,128]{3,2,1,0:T(8,128)} %own.1), channel_id=1, source_target_pairs={{0,24},{8,0},{16,8},{24,16},{1,25},{9,1},{17,9},{25,17},{2,26},{10... | collective-permute-start | bytes 1179656 | tf_op jit(solution)/shard_map/ppermute | solution.py:29
  6.6 10.2 %collective-permute-start.2 = (f32[3,16,16,128]{3,2,1,0:T(8,128)}, f32[3,16,16,128]{3,2,1,0:T(8,128)S(1)}, u32[]{:S(2)}, u32[]{:S(2)}) collective-permute-start(f32[3,16,16,128]{3,2,1,0:T(8,128)} %own.1), channel_id=1, source_target_pairs={{0,3},{1,0},{2,1},{3,2},{4,7},{5,4},{6,5},{7,6},{8,11},{9,8},{10,9... | collective-permute-start | bytes 1179656 | tf_op jit(solution)/shard_map/ppermute | solution.py:29
  7.3 11.0 %collective-permute-start.1 = (f32[3,16,16,128]{3,2,1,0:T(8,128)}, f32[3,16,16,128]{3,2,1,0:T(8,128)S(1)}, u32[]{:S(2)}, u32[]{:S(2)}) collective-permute-start(f32[3,16,16,128]{3,2,1,0:T(8,128)} %own.1), channel_id=1, source_target_pairs={{0,1},{1,2},{2,3},{3,0},{4,5},{5,6},{6,7},{7,4},{8,9},{9,10},{10,1... | collective-permute-start | bytes 1179656 | tf_op jit(solution)/shard_map/ppermute | solution.py:29
  7.3 17.7 %collective-permute-start = (f32[3,16,16,128]{3,2,1,0:T(8,128)}, f32[3,16,16,128]{3,2,1,0:T(8,128)S(1)}, u32[]{:S(2)}, u32[]{:S(2)}) collective-permute-start(f32[3,16,16,128]{3,2,1,0:T(8,128)} %own.1), channel_id=1, source_target_pairs={{0,8},{8,16},{16,24},{24,0},{1,9},{9,17},{17,25},{25,1},{2,10},{10... | collective-permute-start | bytes 1179656 | tf_op jit(solution)/shard_map/ppermute | solution.py:29
  9.4 15.6 %all-to-all-start = ((f32[8,4,512]{2,1,0:T(4,128)}), f32[8,4,512]{2,1,0:T(4,128)S(1)}, u32[]{:S(2)}, u32[]{:S(2)}) async-start(f32[8,4,512]{2,1,0:T(4,128)} %get-tuple-element.20), calls=%async_computation | async-start | bytes 131072 | tf_op jit(solution)/shard_map/all_to_all | solution.py:445
  15.4 12.6 %collective-permute-start.7 = (f32[3,16,16,128]{3,2,1,0:T(8,128)S(1)}, f32[3,16,16,128]{3,2,1,0:T(8,128)}, u32[]{:S(2)}, u32[]{:S(2)}) collective-permute-start(f32[3,16,16,128]{3,2,1,0:T(8,128)S(1)} %collective-permute-done.5.own), channel_id=1, source_target_pairs={{0,3},{1,0},{2,1},{3,2},{4,7},{5,4},{6,5},{7,6},{8,11},{9,8},{10,9... | collective-permute-start | bytes 1179656 | tf_op jit(solution)/shard_map/ppermute | solution.py:29
  16.6 11.4 %collective-permute-start.6 = (f32[3,16,16,128]{3,2,1,0:T(8,128)S(1)}, f32[3,16,16,128]{3,2,1,0:T(8,128)}, u32[]{:S(2)}, u32[]{:S(2)}) collective-permute-start(f32[3,16,16,128]{3,2,1,0:T(8,128)S(1)} %collective-permute-done.5.own), channel_id=1, source_target_pairs={{0,1},{1,2},{2,3},{3,0},{4,5},{5,6},{6,7},{7,4},{8,9},{9,10},{10,1... | collective-permute-start | bytes 1179656 | tf_op jit(solution)/shard_map/ppermute | solution.py:29
  18.3 0.8 %copy-start.1 = (f32[3,16,16,128]{3,2,1,0:T(8,128)}, f32[3,16,16,128]{3,2,1,0:T(8,128)S(1)}, u32[]{:S(2)}) copy-start(f32[3,16,16,128]{3,2,1,0:T(8,128)S(1)} %collective-permute-done.1.before) | copy-start | bytes 1179652
  19.0 1.0 %copy-start = (f32[3,16,16,128]{3,2,1,0:T(8,128)S(1)}, f32[3,16,16,128]{3,2,1,0:T(8,128)}, u32[]{:S(2)}) copy-start(f32[3,16,16,128]{3,2,1,0:T(8,128)} %own.1) | copy-start | bytes 1179652
  20.0 1.0 %copy-start.2 = (f32[3,16,16,128]{3,2,1,0:T(8,128)S(1)}, f32[3,16,16,128]{3,2,1,0:T(8,128)}, u32[]{:S(2)}) copy-start(f32[3,16,16,128]{3,2,1,0:T(8,128)} %copy-done.1) | copy-start | bytes 1179652
  24.9 12.4 %collective-permute-start.4 = (f32[3,16,16,128]{3,2,1,0:T(8,128)S(1)}, f32[3,16,16,128]{3,2,1,0:T(8,128)S(1)}, u32[]{:S(2)}, u32[]{:S(2)}) collective-permute-start(f32[3,16,16,128]{3,2,1,0:T(8,128)S(1)} %collective-permute-done.2.after), channel_id=1, source_target_pairs={{0,8},{8,16},{16,24},{24,0},{1,9},{9,17},{17,25},{25,1},{2,10},{10... | collective-permute-start | bytes 1179656 | tf_op jit(solution)/shard_map/ppermute | solution.py:29
  26.5 10.9 %collective-permute-start.3 = (f32[3,16,16,128]{3,2,1,0:T(8,128)S(1)}, f32[3,16,16,128]{3,2,1,0:T(8,128)S(1)}, u32[]{:S(2)}, u32[]{:S(2)}) collective-permute-start(f32[3,16,16,128]{3,2,1,0:T(8,128)S(1)} %collective-permute-done.refs_1_), channel_id=1, source_target_pairs={{0,1},{1,2},{2,3},{3,0},{4,5},{5,6},{6,7},{7,4},{8,9},{9,10},{10,1... | collective-permute-start | bytes 1179656 | tf_op jit(solution)/shard_map/ppermute | solution.py:29
  33.4 10.3 %copy-start.3 = (f32[128,128]{1,0:T(8,128)S(1)}, f32[128,128]{1,0:T(8,128)}, u32[]{:S(2)}) copy-start(f32[128,128]{1,0:T(8,128)} %constant.13.clone.band) | copy-start | bytes 196612
  39.7 8.4 %copy-start.4 = (f32[128,32]{1,0:T(8,128)S(1)}, f32[128,32]{1,0:T(8,128)}, u32[]{:S(2)}) copy-start(f32[128,32]{1,0:T(8,128)} %constant.14.clone.refs_0_.band) | copy-start | bytes 49156
  39.7 9.8 %collective-permute-start.9 = (f32[5,32,256]{2,1,0:T(8,128)S(1)}, f32[5,32,256]{2,1,0:T(8,128)S(1)}, u32[]{:S(2)}, u32[]{:S(2)}) collective-permute-start(f32[5,32,256]{2,1,0:T(8,128)S(1)} %get-tuple-element.30), channel_id=1, source_target_pairs={{0,4},{4,0},{1,5},{5,1},{2,6},{6,2},{3,7},{7,3},{8,12},{12,8},{9,1... | collective-permute-start | bytes 491528 | tf_op jit(solution)/shard_map/ppermute | solution.py:415
  43.1 5.0 %collective-permute-start.8 = (f32[4,32,256]{2,1,0:T(8,128)S(1)}, f32[4,32,256]{2,1,0:T(8,128)S(1)}, u32[]{:S(2)}, u32[]{:S(2)}) collective-permute-start(f32[4,32,256]{2,1,0:T(8,128)S(1)} %get-tuple-element.29), channel_id=1, source_target_pairs={{0,4},{4,0},{1,5},{5,1},{2,6},{6,2},{3,7},{7,3},{8,12},{12,8},{9,1... | collective-permute-start | bytes 393224 | tf_op jit(solution)/shard_map/ppermute | solution.py:415
